TPU v7x, 32 devices: a whole 2x2x4 slice. The times are simulated.
32 devices in a mesh: dp: 4 (over z), seq: 4 (over x, core), expert: 2 (over y).
Axes of the slice: x: 2, y: 2, z: 4, core: 2. Of those that a mesh axis runs over, the one named last changes fastest.
Arguments:
- layer_input: bfloat16 [2, 4, 2, 256, 768], P(None, 'dp', 'expert', 'seq'), may hold values from -6 to 6
- memory: bfloat16 [2, 4, 2, 256, 768], P(None, 'dp', 'expert', 'seq'), may hold values from -6 to 6
- cotangent: bfloat16 [2, 4, 2, 256, 768], P(None, 'dp', 'expert', 'seq'), may hold values from -6 to 6
- routes: int32 [2, 4, 2, 256, 1], P(None, 'dp', 'expert', 'seq'), may hold values from 0 to 1
- doc_lengths: int32 [2, 4, 2, 3], P(None, 'dp', 'expert'), may hold values from 1 to 254, as said below
- rel_buckets: int32 [256], replicated, may hold values from 0 to 31, as said below
- gains: float32 [3, 768], replicated, may hold values from 0.5 to 1.5
- bias_table: float32 [32, 12], replicated, may hold values from -3 to 3
- router: bfloat16 [768, 2], replicated, may hold values from -0.15625 to 0.15625
- attn_in: bfloat16 [4608, 768], P(('dp', 'seq', 'expert')), may hold values from -0.21875 to 0.21875
- attn_out: bfloat16 [1536, 768], P(('dp', 'seq', 'expert')), may hold values from -0.875 to 0.875
- expert_in: bfloat16 [2, 768, 3072], P('expert', ('dp', 'seq')), may hold values from -0.21875 to 0.21875
- expert_out: bfloat16 [2, 3072, 768], P('expert', ('dp', 'seq')), may hold values from -0.375 to 0.375
Outputs:
- layer_output: bfloat16 [2, 4, 2, 256, 768], P(None, 'dp', 'expert', 'seq')
- grad_input: float32 [2, 4, 2, 256, 768], P(None, 'dp', 'expert', 'seq')
- grad_memory: float32 [2, 4, 2, 256, 768], P(None, 'dp', 'expert', 'seq')
- grad_gains: float32 [3, 768], replicated
- grad_bias: float32 [32, 12], replicated
- grad_router: float32 [768, 2], replicated
- grad_attn_in: float32 [4608, 768], P(('dp', 'seq', 'expert'))
- grad_attn_out: float32 [1536, 768], P(('dp', 'seq', 'expert'))
- grad_expert_in: float32 [2, 768, 3072], P('expert', ('dp', 'seq'))
- grad_expert_out: float32 [2, 3072, 768], P('expert', ('dp', 'seq'))
Inputs may be any that keep to these rules, and one draw needn't show every extreme that they name: `doc_lengths`: each pack holds 3 documents laid end to end, their lengths summing to 256; one of them, at a place drawn from the seed, is longer than 192, the others are shorter than 32. `rel_buckets`: the bucket never falls as the distance grows; distance 0 has bucket 0 and distance 256 - 1 has bucket 32 - 1.
All inputs are finite; a program needn't handle non-finite values.
Results may differ from a plain program's by a relative error of at most 0.022.
Values may be sent and summed in bfloat16 or wider, within the bound.
A program may use at most 256 MiB of HBM per device.

v0:
```python
import jax
import jax.numpy as jnp
from jax import lax
from jax.sharding import PartitionSpec as P

HEADS = 12
HEAD = 64


EPS = 1e-06
NEG = -1e30
HIGHEST = lax.Precision.HIGHEST


def norm_apply(value, gain):
    return value * lax.rsqrt(jnp.mean(value * value, axis=-1, keepdims=True) + EPS) * gain


def norm_back(value, gain, grad):
    _, pull = jax.vjp(norm_apply, value, gain)
    return pull(grad)


def gelu_tanh(value):
    return jax.nn.gelu(value, approximate=True)


def times(left, right):
    return jnp.dot(left, right, preferred_element_type=jnp.float32)


def times_right(left, right):
    return jnp.einsum("te,de->td", left, right, preferred_element_type=jnp.float32)


def times_left(left, right):
    return jnp.einsum("td,te->de", left, right, preferred_element_type=jnp.float32)


def exact_right(left, right):
    return jnp.einsum(
        "te,de->td", left, right, precision=HIGHEST, preferred_element_type=jnp.float32
    )


def exact_left(left, right):
    return jnp.einsum(
        "td,te->de",
        left.astype(jnp.float32),
        right,
        precision=HIGHEST,
        preferred_element_type=jnp.float32,
    )


def attend_forward(query, keys, values, allowed, bias):
    count = query.shape[0]
    scale = HEAD ** (-0.5)
    query3 = query.reshape(count, HEADS, HEAD)
    scores = (
        jnp.einsum(
            "qhd,khd->hqk",
            query3,
            keys.reshape(-1, HEADS, HEAD),
            preferred_element_type=jnp.float32,
        )
        * scale
        + bias
    )
    masked = jnp.where(allowed[None], scores, NEG)
    summit = jnp.max(masked, axis=2, keepdims=True)
    raised = jnp.exp(masked - summit)
    total = jnp.sum(raised, axis=2, keepdims=True)
    weights = (raised / total).astype(jnp.bfloat16)
    mixed = jnp.einsum(
        "hqk,khd->qhd", weights, values.reshape(-1, HEADS, HEAD), preferred_element_type=jnp.float32
    )
    return (mixed.reshape(count, HEADS * HEAD).astype(jnp.bfloat16), summit + jnp.log(total))


def attend_query_side(query, keys, values, allowed, bias, log_total, grad_mixed):
    count = query.shape[0]
    scale = HEAD ** (-0.5)
    query3 = query.reshape(count, HEADS, HEAD)
    keys3 = keys.reshape(-1, HEADS, HEAD)
    values3 = values.reshape(-1, HEADS, HEAD)
    grad3 = grad_mixed.reshape(count, HEADS, HEAD)
    scores = (
        jnp.einsum("qhd,khd->hqk", query3, keys3, preferred_element_type=jnp.float32) * scale + bias
    )
    chances = jnp.exp(jnp.where(allowed[None], scores, NEG) - log_total)
    weights = chances.astype(jnp.bfloat16)
    grad_chances = jnp.einsum("qhd,khd->hqk", grad3, values3, preferred_element_type=jnp.float32)
    spread = jnp.sum(chances * grad_chances, axis=2, keepdims=True)
    grad_scores = (chances * (grad_chances - spread)).astype(jnp.bfloat16)
    grad_query = (
        (jnp.einsum("hqk,khd->qhd", grad_scores, keys3, preferred_element_type=jnp.float32) * scale)
        .reshape(count, HEADS * HEAD)
        .astype(jnp.bfloat16)
    )
    return (grad_query, grad_scores, weights, spread)


def key_terms(query, grad_mixed, weights, grad_scores):
    count = query.shape[0]
    scale = HEAD ** (-0.5)
    query3 = query.reshape(count, HEADS, HEAD)
    grad3 = grad_mixed.reshape(count, HEADS, HEAD)
    grad_values = jnp.einsum(
        "hqk,qhd->khd", weights, grad3, preferred_element_type=jnp.float32
    ).reshape(-1, HEADS * HEAD)
    grad_keys = (
        jnp.einsum("hqk,qhd->khd", grad_scores, query3, preferred_element_type=jnp.float32) * scale
    ).reshape(-1, HEADS * HEAD)
    return (grad_keys, grad_values)


def per_device(
    layer_input,
    memory,
    cotangent,
    routes,
    doc_lengths,
    rel_buckets,
    gains,
    bias_table,
    router,
    attn_in,
    attn_out,
    expert_in,
    expert_out,
):
    micro = layer_input.shape[0]
    rows = layer_input.shape[3]
    width = layer_input.shape[4]
    group = rows * lax.axis_size("seq")
    experts = router.shape[1]
    capacity = (5 * rows + 4 * experts - 1) // (4 * experts)
    buckets = bias_table.shape[0]
    query_pos = lax.axis_index("seq") * rows + jnp.arange(rows, dtype=jnp.int32)
    key_pos = jnp.arange(group, dtype=jnp.int32)
    distance = jnp.maximum(query_pos[:, None] - key_pos[None, :], 0)
    bucket_hot = (rel_buckets[:, None] == jnp.arange(buckets, dtype=jnp.int32)).astype(jnp.float32)
    distance_bias = jnp.dot(bucket_hot, bias_table, precision=HIGHEST)
    bias = jnp.transpose(jnp.take(distance_bias, distance, axis=0), (2, 0, 1))
    slot_ids = jnp.arange(experts * capacity, dtype=jnp.int32)
    expert_ids = jnp.arange(experts, dtype=jnp.int32)
    router_wide = router.astype(jnp.float32)
    out_list = []
    grad_x_list = []
    grad_memory_list = []
    small_total = None
    shards = None
    for index in range(micro):
        dense_in = lax.all_gather(attn_in, ("dp", "seq", "expert"), axis=0, tiled=True)
        dense_out = lax.all_gather(attn_out, ("dp", "seq", "expert"), axis=0, tiled=True)
        fetch_full_in = lax.all_gather(expert_in, ("dp", "seq"), axis=1, tiled=True)
        fetch_full_out = lax.all_gather(expert_out, ("dp", "seq"), axis=1, tiled=True)
        w_in = dense_in.reshape(6, width, width)
        w_out = dense_out.reshape(2, width, width)
        x_rows = layer_input[index, 0, 0].astype(jnp.float32)
        mem_rows = memory[index, 0, 0]
        route = routes[index, 0, 0, :, 0]
        ends = jnp.cumsum(doc_lengths[index, 0, 0])
        query_doc = jnp.sum((query_pos[:, None] >= ends[None, :]).astype(jnp.int32), axis=1)
        key_doc = jnp.sum((key_pos[:, None] >= ends[None, :]).astype(jnp.int32), axis=1)
        same = query_doc[:, None] == key_doc[None, :]
        causal = same & (key_pos[None, :] <= query_pos[:, None])
        normed1 = norm_apply(x_rows, gains[0]).astype(jnp.bfloat16)
        query = times(normed1, w_in[0]).astype(jnp.bfloat16)
        keys = times(normed1, w_in[1]).astype(jnp.bfloat16)
        values = times(normed1, w_in[2]).astype(jnp.bfloat16)
        mem_keys = times(mem_rows, w_in[4]).astype(jnp.bfloat16)
        mem_values = times(mem_rows, w_in[5]).astype(jnp.bfloat16)
        all_keys = lax.all_gather(keys, "seq", axis=0, tiled=True)
        all_values = lax.all_gather(values, "seq", axis=0, tiled=True)
        all_mem_keys = lax.all_gather(mem_keys, "seq", axis=0, tiled=True)
        all_mem_values = lax.all_gather(mem_values, "seq", axis=0, tiled=True)
        mixed, log_self = attend_forward(query, all_keys, all_values, causal, bias)
        hidden1 = x_rows + times(mixed, w_out[0])
        normed2 = norm_apply(hidden1, gains[1]).astype(jnp.bfloat16)
        cross_query = times(normed2, w_in[3]).astype(jnp.bfloat16)
        cross_mixed, log_cross = attend_forward(
            cross_query, all_mem_keys, all_mem_values, same, 0.0
        )
        hidden2 = hidden1 + times(cross_mixed, w_out[1])
        normed3 = norm_apply(hidden2, gains[2]).astype(jnp.bfloat16)
        routing = jax.nn.softmax(times(normed3, router), axis=1)
        route_hot = (route[:, None] == expert_ids[None, :]).astype(jnp.float32)
        gate = jnp.sum(routing * route_hot, axis=1)
        hot_count = route_hot.astype(jnp.int32)
        slot = jnp.sum((jnp.cumsum(hot_count, axis=0) - hot_count) * hot_count, axis=1)
        target = jnp.where(slot < capacity, route * capacity + slot, -1)
        dispatch = (target[:, None] == slot_ids[None, :]).astype(jnp.bfloat16)
        send = jnp.einsum(
            "tc,td->cd", dispatch, normed3, preferred_element_type=jnp.float32
        ).astype(jnp.bfloat16)
        received = lax.all_to_all(
            send.reshape(experts, capacity, width),
            "expert",
            split_axis=0,
            concat_axis=1,
            tiled=True,
        )
        inner = jnp.einsum(
            "esd,edf->esf", received, fetch_full_in, preferred_element_type=jnp.float32
        )
        hidden = gelu_tanh(inner).astype(jnp.bfloat16)
        result = jnp.einsum(
            "esf,efd->esd", hidden, fetch_full_out, preferred_element_type=jnp.float32
        ).astype(jnp.bfloat16)
        back = lax.all_to_all(result, "expert", split_axis=1, concat_axis=0, tiled=True).reshape(
            experts * capacity, width
        )
        combined = times(dispatch, back)
        out_rows = (hidden2 + gate[:, None] * combined).astype(jnp.bfloat16)
        grad_top = cotangent[index, 0, 0].astype(jnp.float32)
        grad_gate = jnp.sum(grad_top * combined, axis=1)
        grad_comb = gate[:, None] * grad_top
        grad_back = jnp.einsum(
            "tc,td->cd",
            dispatch.astype(jnp.float32),
            grad_comb,
            precision=HIGHEST,
            preferred_element_type=jnp.float32,
        )
        grad_result = lax.all_to_all(
            grad_back.astype(jnp.bfloat16).reshape(experts, capacity, width),
            "expert",
            split_axis=0,
            concat_axis=1,
            tiled=True,
        )
        grad_hidden = jnp.einsum(
            "esd,efd->esf", grad_result, fetch_full_out, preferred_element_type=jnp.float32
        )
        grad_full_out = jnp.einsum(
            "esf,esd->efd", hidden, grad_result, preferred_element_type=jnp.float32
        )
        grad_inner = jax.vjp(gelu_tanh, inner)[1](grad_hidden)[0].astype(jnp.bfloat16)
        grad_full_in = jnp.einsum(
            "esd,esf->edf", received, grad_inner, preferred_element_type=jnp.float32
        )
        grad_received = jnp.einsum(
            "esf,edf->esd", grad_inner, fetch_full_in, preferred_element_type=jnp.float32
        ).astype(jnp.bfloat16)
        grad_send = lax.all_to_all(
            grad_received, "expert", split_axis=1, concat_axis=0, tiled=True
        ).reshape(experts * capacity, width)
        grad_logits = grad_gate[:, None] * routing * (route_hot - gate[:, None])
        layer_grad_router = exact_left(normed3, grad_logits)
        grad_normed3 = times(dispatch, grad_send) + exact_right(grad_logits, router_wide)
        grad_h2_norm, grad_gain3 = norm_back(hidden2, gains[2], grad_normed3)
        grad_h2 = grad_top + grad_h2_norm
        grad_h2_low = grad_h2.astype(jnp.bfloat16)
        grad_wco = times_left(cross_mixed, grad_h2_low)
        grad_cross_mixed = times_right(grad_h2_low, w_out[1]).astype(jnp.bfloat16)
        grad_cq, cross_scores, cross_weights, cross_spread = attend_query_side(
            cross_query, all_mem_keys, all_mem_values, same, 0.0, log_cross, grad_cross_mixed
        )
        grad_ck, grad_cv = key_terms(cross_query, grad_cross_mixed, cross_weights, cross_scores)
        cross_key_sum = lax.psum_scatter(
            grad_ck.astype(jnp.bfloat16), "seq", scatter_dimension=0, tiled=True
        )
        cross_value_sum = lax.psum_scatter(
            grad_cv.astype(jnp.bfloat16), "seq", scatter_dimension=0, tiled=True
        )
        grad_wcq = times_left(normed2, grad_cq)
        grad_normed2 = times_right(grad_cq, w_in[3])
        grad_h1_norm, grad_gain2 = norm_back(hidden1, gains[1], grad_normed2)
        grad_h1 = grad_h2 + grad_h1_norm
        grad_h1_low = grad_h1.astype(jnp.bfloat16)
        grad_wso = times_left(mixed, grad_h1_low)
        grad_mixed = times_right(grad_h1_low, w_out[0]).astype(jnp.bfloat16)
        grad_q, grad_scores, self_weights, self_spread = attend_query_side(
            query, all_keys, all_values, causal, bias, log_self, grad_mixed
        )
        per_distance = jax.ops.segment_sum(
            jnp.transpose(grad_scores.astype(jnp.float32), (1, 2, 0)).reshape(-1, HEADS),
            distance.reshape(-1),
            num_segments=group,
        )
        grad_table = exact_left(bucket_hot, per_distance)
        grad_k, grad_v = key_terms(query, grad_mixed, self_weights, grad_scores)
        self_key_sum = lax.psum_scatter(
            grad_k.astype(jnp.bfloat16), "seq", scatter_dimension=0, tiled=True
        )
        self_value_sum = lax.psum_scatter(
            grad_v.astype(jnp.bfloat16), "seq", scatter_dimension=0, tiled=True
        )
        grad_memory_rows = times_right(cross_key_sum, w_in[4]) + times_right(
            cross_value_sum, w_in[5]
        )
        grad_normed1 = (
            times_right(grad_q, w_in[0])
            + times_right(self_key_sum, w_in[1])
            + times_right(self_value_sum, w_in[2])
        )
        grad_x_norm, grad_gain1 = norm_back(x_rows, gains[0], grad_normed1)
        grad_x_rows = grad_h1 + grad_x_norm
        grad_dense_in = jnp.stack(
            [
                times_left(normed1, grad_q),
                times_left(normed1, self_key_sum),
                times_left(normed1, self_value_sum),
                grad_wcq,
                times_left(mem_rows, cross_key_sum),
                times_left(mem_rows, cross_value_sum),
            ]
        )
        grad_dense_out = jnp.stack([grad_wso, grad_wco])
        large = (grad_dense_in, grad_dense_out, grad_full_in, grad_full_out)
        small = (jnp.stack([grad_gain1, grad_gain2, grad_gain3]), grad_table, layer_grad_router)
        out_rows, grad_x_rows, grad_memory_rows, large, small = (
            out_rows,
            grad_x_rows,
            grad_memory_rows,
            large,
            small,
        )
        out_list.append(out_rows)
        grad_x_list.append(grad_x_rows)
        grad_memory_list.append(grad_memory_rows)
        grad_in, grad_out, grad_ein, grad_eout = large
        part_in = lax.psum_scatter(
            grad_in.reshape(6 * width, width),
            ("dp", "seq", "expert"),
            scatter_dimension=0,
            tiled=True,
        )
        part_out = lax.psum_scatter(
            grad_out.reshape(2 * width, width),
            ("dp", "seq", "expert"),
            scatter_dimension=0,
            tiled=True,
        )
        part_ein = lax.psum_scatter(
            grad_ein.astype(jnp.bfloat16), ("dp", "seq"), scatter_dimension=1, tiled=True
        ).astype(jnp.float32)
        part_eout = lax.psum_scatter(
            grad_eout.astype(jnp.bfloat16), ("dp", "seq"), scatter_dimension=1, tiled=True
        ).astype(jnp.float32)
        settled = (part_in, part_out, part_ein, part_eout)
        shards = settled if shards is None else jax.tree.map(jnp.add, shards, settled)
        small_total = small if small_total is None else jax.tree.map(jnp.add, small_total, small)
    grad_gains, grad_bias, grad_router = lax.psum(small_total, ("dp", "seq", "expert"))
    layer_output = jnp.stack(out_list)[:, None, None]
    grad_input = jnp.stack(grad_x_list)[:, None, None]
    grad_memory = jnp.stack(grad_memory_list)[:, None, None]
    return (
        layer_output,
        grad_input,
        grad_memory,
        grad_gains,
        grad_bias,
        grad_router,
        shards[0],
        shards[1],
        shards[2],
        shards[3],
    )


def solution(mesh):
    return jax.shard_map(
        per_device,
        mesh=mesh,
        in_specs=(
            P(None, "dp", "expert", "seq", None),
            P(None, "dp", "expert", "seq", None),
            P(None, "dp", "expert", "seq", None),
            P(None, "dp", "expert", "seq", None),
            P(None, "dp", "expert", None),
            P(),
            P(),
            P(),
            P(),
            P(("dp", "seq", "expert"), None),
            P(("dp", "seq", "expert"), None),
            P("expert", ("dp", "seq"), None),
            P("expert", ("dp", "seq"), None),
        ),
        out_specs=(
            P(None, "dp", "expert", "seq", None),
            P(None, "dp", "expert", "seq", None),
            P(None, "dp", "expert", "seq", None),
            P(),
            P(),
            P(),
            P(("dp", "seq", "expert"), None),
            P(("dp", "seq", "expert"), None),
            P("expert", ("dp", "seq"), None),
            P("expert", ("dp", "seq"), None),
        ),
        check_vma=False,
    )
```

profile of v0, /device:TPU:12, one launch (start us, length us, event | category | flops | bytes accessed | tf_op | source)
XLA Modules:
  0.0 1156.2 jit_solution(692246090297762944)
XLA Ops:
  16.2 54.5 %gather_fusion = f32[16384,12]{1,0:T(8,128)} fusion(f32[256,12]{1,0:T(8,128)S(1)} %fusion.179, s32[16384]{0:T(1024)S(1)} %broadcast_clamp_fusion), kind=kCustom, calls=%fused_computation | custom fusion | bytes 1638400 | tf_op jit(solution)/shard_map/jit(_take)/gather | solution.py:145
  70.7 5.5 copy.217
  78.4 6.3 all-gather.5.cloned.1.call-done
  90.1 6.5 all_gather.44
  99.1 6.6 all_gather.45
  108.2 7.8 all_gather.51
  118.5 6.6 all_gather.50
  127.7 8.9 all_gather.41
  138.6 6.6 all_gather.49
  147.1 6.6 all_gather.48
  156.3 6.8 all_gather.42
  187.3 4.8 all-to-all-start.2
  203.4 3.4 all-to-all-start.6
  206.9 4.4 fusion.12
  211.3 4.1 all-to-all-start
  215.4 38.7 %all-gather.11.cloned.1.call-done = bf16[1,3072,768]{2,1,0:T(8,128)(2,1)} async-done(((bf16[1,192,768]{2,1,0:T(8,128)(2,1)}), bf16[1,3072,768]{2,1,0:T(8,128)(2,1)}) %all-gather.11.cloned.1.call-update) | async-done | bytes 4718608 | tf_op jit(solution)/shard_map/all_gather | solution.py:158
  254.1 4.4 fusion.71
  260.3 4.9 all-to-all-start.4
  265.2 3.5 fusion.14
  269.7 4.0 fusion.49
  273.7 2.2 fusion.52
  277.4 2.9 reduce.6
  281.8 4.0 all-to-all-start.3
  285.9 4.4 fusion.64
  290.3 2.2 fusion.55
  293.5 2.3 reduce.8
  298.2 2.3 reduce.9
  302.9 2.3 reduce.7
  305.9 3.4 all-to-all-start.1
  313.4 4.3 all-to-all-start.7
  319.4 2.7 fusion.176
  324.3 4.0 all-to-all-start.5
  337.9 2.3 convert_add_fusion.3
  353.4 2.4 multiply_reduce_fusion.7
  367.3 2.3 convolution_convert_fusion.7
  388.0 2.3 convolution_convert_fusion.6
  398.6 4.6 fusion.18
  403.5 3.7 fusion.19
  407.3 4.5 fusion.16
  411.9 3.5 fusion.17
  417.9 2.8 maximum_add_fusion
  426.3 2.8 bitcast_dynamic-update-slice_fusion.10
  429.2 2.8 bitcast_dynamic-update-slice_fusion.9
  432.0 2.0 bitcast_dynamic-update-slice_fusion.8
  434.1 2.8 bitcast_dynamic-update-slice_fusion.3
  436.9 19.8 %reduce-scatter.53.cloned.1.call-done = bf16[64,768]{1,0:T(8,128)(2,1)} async-done(((bf16[256,768]{1,0:T(8,128)(2,1)}), bf16[64,768]{1,0:T(8,128)(2,1)}) %reduce-scatter.53.cloned.1.call-update) | async-done | bytes 98320
  456.7 2.8 bitcast_dynamic-update-slice_fusion.2
  459.5 21.1 %reduce-scatter.47.cloned.1.call-done = bf16[64,768]{1,0:T(8,128)(2,1)} async-done(((bf16[256,768]{1,0:T(8,128)(2,1)}), bf16[64,768]{1,0:T(8,128)(2,1)}) %reduce-scatter.47.cloned.1.call-update) | async-done | bytes 98320
  480.6 2.9 bitcast_dynamic-update-slice_fusion.6
  483.5 20.9 %reduce-scatter.49.cloned.1.call-done = bf16[64,768]{1,0:T(8,128)(2,1)} async-done(((bf16[256,768]{1,0:T(8,128)(2,1)}), bf16[64,768]{1,0:T(8,128)(2,1)}) %reduce-scatter.49.cloned.1.call-update) | async-done | bytes 98320
  504.4 2.9 bitcast_dynamic-update-slice_fusion.5
  509.3 18.4 %reduce-scatter.55.cloned.1.call-done = bf16[64,768]{1,0:T(8,128)(2,1)} async-done(((bf16[256,768]{1,0:T(8,128)(2,1)}), bf16[64,768]{1,0:T(8,128)(2,1)}) %reduce-scatter.55.cloned.1.call-update) | async-done | bytes 98320
  527.7 2.9 bitcast_dynamic-update-slice_fusion.1
  530.6 20.9 %reduce-scatter.57.cloned.1.call-done = bf16[64,768]{1,0:T(8,128)(2,1)} async-done(((bf16[256,768]{1,0:T(8,128)(2,1)}), bf16[64,768]{1,0:T(8,128)(2,1)}) %reduce-scatter.57.cloned.1.call-update) | async-done | bytes 98320
  551.5 2.8 bitcast_dynamic-update-slice_fusion
  554.3 16.1 %add.346 = f32[6,768,768]{2,1,0:T(8,128)} add(f32[6,768,768]{2,1,0:T(8,128)} %bitcast_dynamic-update-slice_fusion.2, f32[6,768,768]{2,1,0:T(8,128)} %bitcast_dynamic-update-slice_fusion) | non-fusion elementwise | flops 3538944 | bytes 42467328 | tf_op jit(solution)/shard_map/add | solution.py:344
  572.2 3.2 fusion.141
  575.4 6.1 copy.219
  581.6 4.8 copy.218
  586.5 109.6 %scatter_custom_fusion.1 = f32[256,12]{1,0:T(8,128)S(1)} fusion(s32[16384]{0:T(1024)S(1)} %bitcast.601, f32[16384,12]{1,0:T(8,128)} %bitcast.524, f32[]{:T(128)} %constant.63.clone.1), kind=kCustom, calls=%fused_computation.336 | custom fusion | flops 196608 | bytes 12800 | tf_op jit(solution)/shard_map/scatter-add | solution.py:278
  696.1 109.8 %scatter_custom_fusion = f32[256,12]{1,0:T(8,128)S(1)} fusion(s32[16384]{0:T(1024)S(1)} %bitcast.602, f32[16384,12]{1,0:T(8,128)} %bitcast.523, f32[]{:T(128)} %constant.63.clone.1), kind=kCustom, calls=%fused_computation.338 | custom fusion | flops 196608 | bytes 12800 | tf_op jit(solution)/shard_map/scatter-add | solution.py:278
  819.0 42.4 %all-reduce = (f32[3,768]{1,0:T(4,128)}, f32[32,12]{0,1:T(8,128)}, f32[768,2]{0,1:T(2,128)}) all-reduce(f32[3,768]{1,0:T(4,128)S(1)} %maximum_add_fusion.1, f32[32,12]{0,1:T(8,128)S(1)} %convolution_add_fusion.10, f32[768,2]{0,1:T(2,128)S(1)} %convolution_add_fusion.11), channel_id=1, replica_groups=mesh['dp'=4,'seq'=4,'expert'=2] {'dp','seq','expert'}, use_global_device_ids=true, to_apply=%region_56.57 | all-reduce | flops 4224 | bytes 33792 | tf_op jit(solution)/shard_map/psum | solution.py:346
  874.2 105.9 %reduce-scatter.41.cloned.1.call-done = f32[48,768]{1,0:T(8,128)} async-done(((f32[1536,768]{1,0:T(8,128)}), f32[48,768]{1,0:T(8,128)}) %reduce-scatter.41.cloned.1.call-update) | async-done | bytes 147472 | tf_op jit(solution)/shard_map/reduce_scatter | solution.py:331
  980.1 168.8 %reduce-scatter.39.cloned.1.call-done = f32[144,768]{1,0:T(8,128)} async-done(((f32[4608,768]{1,0:T(8,128)}), f32[144,768]{1,0:T(8,128)}) %reduce-scatter.39.cloned.1.call-update) | async-done | bytes 442384 | tf_op jit(solution)/shard_map/reduce_scatter | solution.py:325
  (561 shorter events, 186.2 us)
Async XLA Ops:
  7.2 77.5 %all-gather.5.cloned.1.call-start = ((), (), s32[]{:S(2)}) async-start(), calls=%async_computation.22 | async-start | bytes 7299072 | tf_op jit(solution)/shard_map/all_gather | solution.py:155
  7.9 158.6 %all-gather.7.cloned.1.call-start = ((), (), s32[]{:S(2)}) async-start(), calls=%async_computation.23 | async-start | bytes 2433024 | tf_op jit(solution)/shard_map/all_gather | solution.py:156
  8.7 198.2 %all-gather.9.cloned.1.call-start = ((), (), s32[]{:S(2)}) async-start(), calls=%async_computation.24 | async-start | bytes 5013504 | tf_op jit(solution)/shard_map/all_gather | solution.py:157
  9.4 244.7 %all-gather.11.cloned.1.call-start = ((), (), s32[]{:S(2)}) async-start(), calls=%async_computation.25 | async-start | bytes 5013504 | tf_op jit(solution)/shard_map/all_gather | solution.py:158
  10.0 67.7 %copy-start.116 = (s32[64]{0:T(128)}, s32[64]{0:T(128)S(1)}, u32[]{:S(2)}) copy-start(s32[64]{0:T(128)S(1)} %iota_add_fusion) | copy-start | bytes 772
  12.1 58.6 %copy-start.120 = (s32[64]{0:T(128)}, s32[64]{0:T(128)S(1)}, u32[]{:S(2)}) copy-start(s32[64]{0:T(128)S(1)} %get-tuple-element.119) | copy-start | bytes 772
  12.1 58.6 %copy-start.122 = (s32[64]{0:T(128)}, s32[64]{0:T(128)S(1)}, u32[]{:S(2)}) copy-start(s32[64]{0:T(128)S(1)} %get-tuple-element.118) | copy-start | bytes 772
  13.2 57.5 %copy-start.149 = (f32[64]{0:T(128)}, f32[64]{0:T(128)S(1)}, u32[]{:S(2)}) copy-start(f32[64]{0:T(128)S(1)} %get-tuple-element.77) | copy-start | bytes 772
  13.7 140.9 %copy-start.131 = (f32[64]{0:T(128)}, f32[64]{0:T(128)S(1)}, u32[]{:S(2)}) copy-start(f32[64]{0:T(128)S(1)} %fusion.259) | copy-start | bytes 772
  13.7 131.6 %copy-start.133 = (f32[64]{0:T(128)}, f32[64]{0:T(128)S(1)}, u32[]{:S(2)}) copy-start(f32[64]{0:T(128)S(1)} %fusion.262) | copy-start | bytes 772
  14.6 171.2 %copy-start.104 = (f32[768]{0:T(1024)}, f32[768]{0:T(1024)S(1)}, u32[]{:S(2)}) copy-start(f32[768]{0:T(1024)S(1)} %get-tuple-element.78) | copy-start | bytes 9220
  76.2 87.4 %copy-start.13 = (f32[64,256,12]{1,0,2:T(8,128)}, f32[64,256,12]{1,0,2:T(8,128)S(1)}, u32[]{:S(2)}) copy-start(f32[64,256,12]{1,0,2:T(8,128)S(1)} %copy.217) | copy-start | bytes 2359300
  86.5 77.1 %copy-start.50 = (bf16[64,768]{0,1:T(8,128)(2,1)}, bf16[64,768]{0,1:T(8,128)(2,1)S(1)}, u32[]{:S(2)}) copy-start(bf16[64,768]{0,1:T(8,128)(2,1)S(1)} %copy.240) | copy-start | bytes 294916
  88.4 74.8 %copy-start.57 = (bf16[64,768]{0,1:T(8,128)(2,1)}, bf16[64,768]{0,1:T(8,128)(2,1)S(1)}, u32[]{:S(2)}) copy-start(bf16[64,768]{0,1:T(8,128)(2,1)S(1)} %copy.242) | copy-start | bytes 294916
  186.4 67.7 %copy-start.66 = (bf16[64,768]{1,0:T(8,128)(2,1)}, bf16[64,768]{1,0:T(8,128)(2,1)S(1)}, u32[]{:S(2)}) copy-start(bf16[64,768]{1,0:T(8,128)(2,1)S(1)} %get-tuple-element.111) | copy-start | bytes 294916
  186.4 67.7 %copy-start.68 = (bf16[64,768]{1,0:T(8,128)(2,1)}, bf16[64,768]{1,0:T(8,128)(2,1)S(1)}, u32[]{:S(2)}) copy-start(bf16[64,768]{1,0:T(8,128)(2,1)S(1)} %get-tuple-element.110) | copy-start | bytes 294916
  187.3 16.1 %all-to-all-start.2 = ((bf16[2,40,768]{2,1,0:T(8,128)(2,1)}), bf16[2,40,768]{2,1,0:T(8,128)(2,1)S(1)}, u32[]{:S(2)}, u32[]{:S(2)}) async-start(bf16[2,40,768]{2,1,0:T(8,128)(2,1)} %bitcast.592), calls=%async_computation.2 | async-start | bytes 245760 | tf_op jit(solution)/shard_map/all_to_all | solution.py:198
  203.4 146.4 %copy-start.97 = (f32[12,64]{1,0:T(8,128)}, f32[12,64]{1,0:T(8,128)S(1)}, u32[]{:S(2)}) copy-start(f32[12,64]{1,0:T(8,128)S(1)} %log_add_fusion.3) | copy-start | bytes 9220
  203.4 7.9 all-to-all-start.6
  211.3 49.0 %all-to-all-start = ((bf16[2,40,768]{2,1,0:T(8,128)(2,1)}), bf16[2,40,768]{2,1,0:T(8,128)(2,1)}, u32[]{:S(2)}, u32[]{:S(2)}) async-start(bf16[2,40,768]{2,1,0:T(8,128)(2,1)} %bitcast.15), calls=%async_computation | async-start | bytes 245760 | tf_op jit(solution)/shard_map/all_to_all | solution.py:198
  260.3 21.6 %all-to-all-start.4 = ((bf16[2,40,768]{2,1,0:T(8,128)(2,1)}), bf16[2,40,768]{2,1,0:T(8,128)(2,1)}, u32[]{:S(2)}, u32[]{:S(2)}) async-start(bf16[2,40,768]{2,1,0:T(8,128)(2,1)} %bitcast.591), calls=%async_computation.4 | async-start | bytes 245760 | tf_op jit(solution)/shard_map/all_to_all | solution.py:227
  281.8 24.0 %all-to-all-start.3 = ((bf16[2,2,15360]{2,1,0:T(2,128)(2,1)}), bf16[2,2,15360]{2,1,0:T(2,128)(2,1)}, u32[]{:S(2)}, u32[]{:S(2)}) async-start(bf16[2,2,15360]{2,1,0:T(2,128)(2,1)} %reshape.951), calls=%async_computation.3 | async-start | bytes 245760 | tf_op jit(solution)/shard_map/all_to_all | solution.py:212
  305.9 6.9 all-to-all-start.1
  313.4 10.8 all-to-all-start.7
  324.3 8.6 all-to-all-start.5
  328.3 98.1 %reduce-scatter.43.cloned.1.call-start = ((), (), s32[]{:S(2)}) async-start(), calls=%async_computation.32 | async-start | bytes 491520
  367.3 61.9 %reduce-scatter.45.cloned.1.call-start = ((), (), s32[]{:S(2)}) async-start(), calls=%async_computation.33 | async-start | bytes 491520
  371.6 62.5 %reduce-scatter.51.cloned.1.call-start = ((), (), s32[]{:S(2)}) async-start(), calls=%async_computation.36 | async-start | bytes 491520
  375.5 81.2 %reduce-scatter.53.cloned.1.call-start = ((), (), s32[]{:S(2)}) async-start(), calls=%async_computation.37 | async-start | bytes 491520
  379.8 100.8 %reduce-scatter.47.cloned.1.call-start = ((), (), s32[]{:S(2)}) async-start(), calls=%async_computation.34 | async-start | bytes 491520
  387.9 116.4 %reduce-scatter.49.cloned.1.call-start = ((), (), s32[]{:S(2)}) async-start(), calls=%async_computation.35 | async-start | bytes 491520
  392.3 135.5 %reduce-scatter.55.cloned.1.call-start = ((), (), s32[]{:S(2)}) async-start(), calls=%async_computation.38 | async-start | bytes 491520
  396.2 155.3 %reduce-scatter.57.cloned.1.call-start = ((), (), s32[]{:S(2)}) async-start(), calls=%async_computation.39 | async-start | bytes 491520
  398.5 471.9 %reduce-scatter.35.cloned.1.call-start = ((), (), s32[]{:S(2)}) async-start(), calls=%async_computation.28 | async-start | bytes 5013504 | tf_op jit(solution)/shard_map/reduce_scatter | solution.py:340
  403.2 467.1 %reduce-scatter.37.cloned.1.call-start = ((), (), s32[]{:S(2)}) async-start(), calls=%async_computation.29 | async-start | bytes 5013504 | tf_op jit(solution)/shard_map/reduce_scatter | solution.py:340
  407.3 465.0 %reduce-scatter.31.cloned.1.call-start = ((), (), s32[]{:S(2)}) async-start(), calls=%async_computation.26 | async-start | bytes 5013504 | tf_op jit(solution)/shard_map/reduce_scatter | solution.py:337
  411.9 460.4 %reduce-scatter.33.cloned.1.call-start = ((), (), s32[]{:S(2)}) async-start(), calls=%async_computation.27 | async-start | bytes 5013504 | tf_op jit(solution)/shard_map/reduce_scatter | solution.py:337
  415.5 564.6 %reduce-scatter.41.cloned.1.call-start = ((), (), s32[]{:S(2)}) async-start(), calls=%async_computation.31 | async-start | bytes 4866048 | tf_op jit(solution)/shard_map/reduce_scatter | solution.py:331
  420.7 728.2 %reduce-scatter.39.cloned.1.call-start = ((), (), s32[]{:S(2)}) async-start(), calls=%async_computation.30 | async-start | bytes 14598144 | tf_op jit(solution)/shard_map/reduce_scatter | solution.py:325
  434.1 73.2 %copy-start.52 = (bf16[12,64,64]{2,1,0:T(8,128)(2,1)S(1)}, bf16[12,64,64]{2,1,0:T(8,128)(2,1)}, u32[]{:S(2)}) copy-start(bf16[12,64,64]{2,1,0:T(8,128)(2,1)} %copy-done.51) | copy-start | bytes 294916
  434.1 73.2 %copy-start.137 = (f32[64]{0:T(128)S(1)}, f32[64]{0:T(128)}, u32[]{:S(2)}) copy-start(f32[64]{0:T(128)} %copy-done.135) | copy-start | bytes 772
  581.5 224.4 %copy-start.95 = (bf16[1,64,768]{2,1,0:T(8,128)(2,1)S(1)}, bf16[1,64,768]{2,1,0:T(8,128)(2,1)}, u32[]{:S(2)}) copy-start(bf16[1,64,768]{2,1,0:T(8,128)(2,1)} %get-tuple-element.102) | copy-start | bytes 294916
  581.5 224.4 %copy-start.96 = (bf16[1,64,768]{2,1,0:T(8,128)(2,1)S(1)}, bf16[1,64,768]{2,1,0:T(8,128)(2,1)}, u32[]{:S(2)}) copy-start(bf16[1,64,768]{2,1,0:T(8,128)(2,1)} %get-tuple-element.103) | copy-start | bytes 294916
  581.5 225.1 %copy-start.69 = (bf16[64,768]{1,0:T(8,128)(2,1)S(1)}, bf16[64,768]{1,0:T(8,128)(2,1)}, u32[]{:S(2)}) copy-start(bf16[64,768]{1,0:T(8,128)(2,1)} %copy-done.68) | copy-start | bytes 294916
  581.5 225.1 %copy-start.123 = (s32[64]{0:T(128)S(1)}, s32[64]{0:T(128)}, u32[]{:S(2)}) copy-start(s32[64]{0:T(128)} %copy-done.122) | copy-start | bytes 772
  581.5 225.1 %copy-start.125 = (f32[64]{0:T(128)S(1)}, f32[64]{0:T(128)}, u32[]{:S(2)}) copy-start(f32[64]{0:T(128)} %copy-done.124) | copy-start | bytes 772
  581.5 225.1 %copy-start.130 = (f32[64,2]{0,1:T(2,128)S(1)}, f32[64,2]{0,1:T(2,128)}, u32[]{:S(2)}) copy-start(f32[64,2]{0,1:T(2,128)} %get-tuple-element.87) | copy-start | bytes 1540
  581.5 225.1 %copy-start.143 = (f32[64]{0:T(128)S(1)}, f32[64]{0:T(128)}, u32[]{:S(2)}) copy-start(f32[64]{0:T(128)} %get-tuple-element.74) | copy-start | bytes 772
  581.6 225.2 %copy-start.67 = (bf16[64,768]{1,0:T(8,128)(2,1)S(1)}, bf16[64,768]{1,0:T(8,128)(2,1)}, u32[]{:S(2)}) copy-start(bf16[64,768]{1,0:T(8,128)(2,1)} %copy-done.66) | copy-start | bytes 294916
  581.6 225.2 %copy-start.121 = (s32[64]{0:T(128)S(1)}, s32[64]{0:T(128)}, u32[]{:S(2)}) copy-start(s32[64]{0:T(128)} %copy-done.120) | copy-start | bytes 772
  581.6 225.2 %copy-start.127 = (f32[64]{0:T(128)S(1)}, f32[64]{0:T(128)}, u32[]{:S(2)}) copy-start(f32[64]{0:T(128)} %copy-done.126) | copy-start | bytes 772
  581.6 225.2 %copy-start.129 = (f32[64,2]{0,1:T(2,128)S(1)}, f32[64,2]{0,1:T(2,128)}, u32[]{:S(2)}) copy-start(f32[64,2]{0,1:T(2,128)} %get-tuple-element.91) | copy-start | bytes 1540
  581.6 225.2 %copy-start.142 = (f32[64]{0:T(128)S(1)}, f32[64]{0:T(128)}, u32[]{:S(2)}) copy-start(f32[64]{0:T(128)} %copy-done.141) | copy-start | bytes 772
  581.6 225.4 %copy-start.128 = (s32[256]{0:T(256)S(1)}, s32[256]{0:T(256)}, u32[]{:S(2)}) copy-start(s32[256]{0:T(256)} %param.18) | copy-start | bytes 3076
  581.6 226.0 %copy-start.90 = (bf16[64,768]{1,0:T(8,128)(2,1)S(1)}, bf16[64,768]{1,0:T(8,128)(2,1)}, u32[]{:S(2)}) copy-start(bf16[64,768]{1,0:T(8,128)(2,1)} %reduce-scatter.45.cloned.1.call-done) | copy-start | bytes 294916
  581.6 227.8 %copy-start.88 = (bf16[64,768]{1,0:T(8,128)(2,1)S(1)}, bf16[64,768]{1,0:T(8,128)(2,1)}, u32[]{:S(2)}) copy-start(bf16[64,768]{1,0:T(8,128)(2,1)} %reduce-scatter.43.cloned.1.call-done) | copy-start | bytes 294916
  581.6 229.7 %copy-start.94 = (bf16[64,768]{1,0:T(8,128)(2,1)S(1)}, bf16[64,768]{1,0:T(8,128)(2,1)}, u32[]{:S(2)}) copy-start(bf16[64,768]{1,0:T(8,128)(2,1)} %reduce-scatter.49.cloned.1.call-done) | copy-start | bytes 294916
  586.5 226.7 %copy-start.92 = (bf16[64,768]{1,0:T(8,128)(2,1)S(1)}, bf16[64,768]{1,0:T(8,128)(2,1)}, u32[]{:S(2)}) copy-start(bf16[64,768]{1,0:T(8,128)(2,1)} %reduce-scatter.47.cloned.1.call-done) | copy-start | bytes 294916
  586.5 228.6 %copy-start.59 = (bf16[12,64,64]{2,1,0:T(8,128)(2,1)S(1)}, bf16[12,64,64]{2,1,0:T(8,128)(2,1)}, u32[]{:S(2)}) copy-start(bf16[12,64,64]{2,1,0:T(8,128)(2,1)} %copy-done.58) | copy-start | bytes 294916
  586.5 230.4 %copy-start.73 = (bf16[12,64,64]{2,1,0:T(8,128)(2,1)S(1)}, bf16[12,64,64]{2,1,0:T(8,128)(2,1)}, u32[]{:S(2)}) copy-start(bf16[12,64,64]{2,1,0:T(8,128)(2,1)} %copy-done.72) | copy-start | bytes 294916
  816.9 52.5 %copy-start.148 = (f32[64]{0:T(128)S(1)}, f32[64]{0:T(128)}, u32[]{:S(2)}) copy-start(f32[64]{0:T(128)} %copy-done.147) | copy-start | bytes 772
  816.9 52.5 %copy-start.43 = (f32[64,768]{1,0:T(8,128)S(1)}, f32[64,768]{1,0:T(8,128)}, u32[]{:S(2)}) copy-start(f32[64,768]{1,0:T(8,128)} %copy-done.41) | copy-start | bytes 589828
  816.9 52.5 %copy-start.45 = (f32[64,768]{1,0:T(8,128)S(1)}, f32[64,768]{1,0:T(8,128)}, u32[]{:S(2)}) copy-start(f32[64,768]{1,0:T(8,128)} %get-tuple-element.105) | copy-start | bytes 589828
  861.4 287.5 %copy-start.1 = (f32[32,12]{0,1:T(8,128)S(1)}, f32[32,12]{0,1:T(8,128)}, u32[]{:S(2)}) copy-start(f32[32,12]{0,1:T(8,128)} %param.20) | copy-start | bytes 4612
  (123 other events, 1161.1 us)
Sparse Core Ops, SparseCore 0:
  10.9 73.7 all-gather.4
  87.6 56.0 all-gather.6
  146.1 53.9 all-gather.8
  202.2 51.8 all-gather.10
  367.4 19.3 reduce-scatter.42
  389.1 20.8 reduce-scatter.44
  412.5 20.7 reduce-scatter.50
  435.8 20.8 reduce-scatter.52
  459.8 20.7 reduce-scatter.46
  483.5 20.7 reduce-scatter.48
  506.9 20.7 reduce-scatter.54
  530.6 20.7 reduce-scatter.56
  555.3 75.0 reduce-scatter.34
  634.6 74.5 reduce-scatter.36
  712.9 74.5 reduce-scatter.30
  791.7 76.0 reduce-scatter.32
  873.7 106.3 reduce-scatter.40
  987.6 161.3 reduce-scatter.38
where the time goes:
time: 1170 us; the launch traced here: 1160 us
  waiting for transfers between devices  424 us (36%)
  other arithmetic  279 us (24%)
  matrix products  179 us (15%)
  local copies, waits for them, and re-layouts  125 us (11%)
  blocking collectives  98.7 us (8%)
  starting transfers between devices  33.9 us (3%)
  between operations  17 us (1%)
    scatter-add x2, other arithmetic, per_device(): jax.ops.segment_sum(jnp.transpose(grad_scores.astype(jnp.float32), (1, 2,...  219 us
    reduce_scatter x1, waiting for transfers between devices, per_device(): lax.psum_scatter(grad_in.reshape(6 * width, width), ('dp', 'seq', 'expert...  169 us
    reduce_scatter x1, waiting for transfers between devices, per_device(): lax.psum_scatter(grad_out.reshape(2 * width, width), ('dp', 'seq', 'exper...  106 us
    unnamed x26, waiting for transfers between devices  104 us
    gather x2, local copies, waits for them, and re-layouts, per_device(): bias = jnp.transpose(jnp.take(distance_bias, distance, axis=0), (2, 0, 1))  60 us
    psum x1, blocking collectives, per_device(): lax.psum(small_total, ('dp', 'seq', 'expert'))  42.4 us
    all_gather x1, waiting for transfers between devices, per_device(): lax.all_gather(expert_out, ('dp', 'seq'), axis=1, tiled=True)  38.7 us
    unnamed x341, local copies, waits for them, and re-layouts  36.3 us
  transfers between devices with their start and end apart: 26, of which 9 were waited for; matrix products, arithmetic and copies ran while one was open for 47% of the time, Pallas kernels for 0%

commit v1 on v0

v1 whole, which is shorter than its diff:
```python
import functools

import jax
import jax.numpy as jnp
from jax import lax
from jax.experimental import pallas as pl
from jax.experimental.pallas import tpu as pltpu
from jax.sharding import PartitionSpec as P

HEADS = 12
HEAD = 64

EPS = 1e-06
NEG = -1e30
HIGHEST = lax.Precision.HIGHEST
MESH = pl.DeviceIdType.MESH
BF = jnp.bfloat16
F32 = jnp.float32


class Place:
    def __init__(self):
        self.nz, self.ns, self.ny = (lax.axis_size(a) for a in ("dp", "seq", "expert"))
        self.nx = self.ns // 2
        self.z, self.s, self.y = (lax.axis_index(a) for a in ("dp", "seq", "expert"))
        self.x, self.c = self.s // 2, lax.rem(self.s, 2)

    def device(self, z=None, x=None, c=None, y=None):
        z = self.z if z is None else z
        x = self.x if x is None else x
        c = self.c if c is None else c
        y = self.y if y is None else y
        return (z, x * 2 + c, y)

    def other_x(self):
        return [lax.rem(self.x + k, self.nx) for k in range(1, self.nx)]

    def other_y(self):
        return [lax.rem(self.y + k, self.ny) for k in range(1, self.ny)]

    def by_distance(self, k):
        order = [sorted(range(self.nz), key=lambda d: (abs(d - z), d)) for z in range(self.nz)]
        out = jnp.int32(0)
        for z in range(self.nz):
            out = jnp.where(self.z == z, jnp.int32(order[z][k]), out)
        return out

    def greet(self):
        barrier = pltpu.get_barrier_semaphore()
        for x in self.other_x():
            pl.semaphore_signal(barrier, inc=1, device_id=self.device(x=x), device_id_type=MESH)
        for y in self.other_y():
            pl.semaphore_signal(barrier, inc=1, device_id=self.device(y=y), device_id_type=MESH)
        pl.semaphore_signal(barrier, inc=1, device_id=self.device(c=1 - self.c), device_id_type=MESH)

        @pl.when(self.z > 0)
        def _():
            pl.semaphore_signal(barrier, inc=1, device_id=self.device(z=self.z - 1), device_id_type=MESH)

        @pl.when(self.z < self.nz - 1)
        def _():
            pl.semaphore_signal(barrier, inc=1, device_id=self.device(z=self.z + 1), device_id_type=MESH)

        beside = jnp.where(self.z > 0, 1, 0) + jnp.where(self.z < self.nz - 1, 1, 0)
        pl.semaphore_wait(barrier, self.nx - 1 + self.ny - 1 + 1 + beside)


def spread_kernel(x_ref, m_ref, ain, aout, ein, eout, xo, mo, aino, aouto, eino, eouto,
                  act_send, act_recv, line_send, side_send, core_send, ici_recv, core_recv, own_sem):
    at = Place()
    nz, nx, ny = at.nz, at.nx, at.ny
    tok = x_ref.shape[1]
    shards = (ain, aout, ein, eout)
    fulls = (aino, aouto, eino, eouto)
    acts = ((x_ref, xo), (m_ref, mo))
    dense, expert = (0, 1), (2, 3)

    def spot(a, z, x, c, y):
        s = x * 2 + c
        rows = shards[a].shape[0]
        index = (z * at.ns + s) * ny + y if a in dense else z * at.ns + s
        return fulls[a].at[pl.ds(pl.multiple_of(index * rows, 16), rows)]

    waits = []

    def send(src, dst, ssem, rsem, **where):
        copy = pltpu.make_async_remote_copy(
            src_ref=src, dst_ref=dst, send_sem=ssem, recv_sem=rsem,
            device_id=at.device(**where), device_id_type=MESH,
        )
        copy.start()
        waits.append(copy.wait_send)

    def arrive(ref, sem):
        pltpu.make_async_copy(ref, ref, sem).wait()

    at.greet()
    for i, (src, full) in enumerate(acts):
        dst = full.at[:, pl.ds(pl.multiple_of(at.s * tok, 16), tok)]
        for k, x in enumerate(at.other_x()):
            send(src, dst, act_send.at[i, k], act_recv.at[i, at.x, at.c], x=x)
        send(src, dst, act_send.at[i, nx - 1 + at.x], act_recv.at[i, at.x, at.c], c=1 - at.c)
        own = pltpu.make_async_copy(src, dst, own_sem.at[4 + i])
        own.start()
        waits.append(own.wait)

    def along_line(a, z, src):
        dst = spot(a, z, at.x, at.c, at.y)
        sem = ici_recv.at[a, z, at.x, at.y]

        def one(side, to):
            return pltpu.make_async_remote_copy(
                src_ref=src, dst_ref=dst, send_sem=line_send.at[a, z, side], recv_sem=sem,
                device_id=at.device(z=to), device_id_type=MESH,
            )

        left = (z >= at.z) & (at.z > 0)
        right = (z <= at.z) & (at.z < nz - 1)

        @pl.when(left)
        def _():
            one(0, at.z - 1).start()

        @pl.when(right)
        def _():
            one(1, at.z + 1).start()

        def wait():
            @pl.when(left)
            def _():
                one(0, at.z - 1).wait_send()

            @pl.when(right)
            def _():
                one(1, at.z + 1).wait_send()

        waits.append(wait)

    def to_sides(a, z, src):
        dst = spot(a, z, at.x, at.c, at.y)
        for k, x in enumerate(at.other_x()):
            send(src, dst, side_send.at[a, z, k], ici_recv.at[a, z, at.x, at.y], x=x)
        if a in dense:
            for k, y in enumerate(at.other_y()):
                send(src, dst, side_send.at[a, z, nx - 1 + k], ici_recv.at[a, z, at.x, at.y], y=y)

    def to_core(a, z, x, y, src):
        send(src, spot(a, z, x, at.c, y), core_send.at[a, z, x, y], core_recv.at[a, z, x, y], c=1 - at.c)

    zs = [at.by_distance(k) for k in range(nz)]
    for group in (dense, expert):
        for a in group:
            along_line(a, at.z, shards[a])
    for k in range(nz):
        for a in dense:
            here = spot(a, zs[k], at.x, at.c, at.y)
            if k:
                arrive(here, ici_recv.at[a, zs[k], at.x, at.y])
                along_line(a, zs[k], here)
            else:
                own = pltpu.make_async_copy(shards[a], here, own_sem.at[a])
                own.start()
                waits.append(own.wait)
            to_sides(a, zs[k], here if k else shards[a])
            to_core(a, zs[k], at.x, at.y, here if k else shards[a])
        if k == 0:
            for i, (src, full) in enumerate(acts):
                for j, x in enumerate(at.other_x()):
                    dst = full.at[:, pl.ds(pl.multiple_of((x * 2 + at.c) * tok, 16), tok)]
                    arrive(dst, act_recv.at[i, x, at.c])
                    send(dst, dst, act_send.at[i, nx - 1 + x], act_recv.at[i, x, at.c], c=1 - at.c)
    for k in range(nz):
        for a in expert:
            here = spot(a, zs[k], at.x, at.c, at.y)
            if k:
                arrive(here, ici_recv.at[a, zs[k], at.x, at.y])
                along_line(a, zs[k], here)
            else:
                own = pltpu.make_async_copy(shards[a], here, own_sem.at[a])
                own.start()
                waits.append(own.wait)
            to_sides(a, zs[k], here if k else shards[a])
            to_core(a, zs[k], at.x, at.y, here if k else shards[a])
        for a in dense:
            for x in at.other_x():
                here = spot(a, zs[k], x, at.c, at.y)
                arrive(here, ici_recv.at[a, zs[k], x, at.y])
                for j, y in enumerate(at.other_y()):
                    send(here, here, side_send.at[a, zs[k], nx - 1 + ny - 1 + j + (ny - 1) * x],
                         ici_recv.at[a, zs[k], x, at.y], y=y)
                to_core(a, zs[k], x, at.y, here)
    for k in range(nz):
        for a in dense:
            for y in at.other_y():
                for x in range(nx):
                    here = spot(a, zs[k], x, at.c, y)
                    arrive(here, ici_recv.at[a, zs[k], x, y])
                    to_core(a, zs[k], x, y, here)
        for a in expert:
            for x in at.other_x():
                here = spot(a, zs[k], x, at.c, at.y)
                arrive(here, ici_recv.at[a, zs[k], x, at.y])
                to_core(a, zs[k], x, at.y, here)
    for a in range(4):
        for z in range(nz):
            for x in range(nx):
                for y in range(ny) if a in dense else [at.y]:
                    arrive(spot(a, z, x, 1 - at.c, y), core_recv.at[a, z, x, y])
    for i, (src, full) in enumerate(acts):
        for x in range(nx):
            dst = full.at[:, pl.ds(pl.multiple_of((x * 2 + 1 - at.c) * tok, 16), tok)]
            arrive(dst, act_recv.at[i, x, 1 - at.c])
    for wait in waits:
        wait()


def in_tiles(*arrays):
    return all(a.shape[-2] % 16 == 0 for a in arrays)


def spread(x, m, ain, aout, ein, eout):
    if not in_tiles(x, m, ain, aout, ein, eout):
        everywhere, peers = ("dp", "seq", "expert"), ("dp", "seq")
        return (
            *[lax.all_gather(a, "seq", axis=1, tiled=True) for a in (x, m)],
            *[lax.all_gather(a, everywhere, axis=0, tiled=True) for a in (ain, aout)],
            *[lax.all_gather(a, peers, axis=0, tiled=True) for a in (ein, eout)],
        )
    nz, ns, ny = (lax.axis_size(a) for a in ("dp", "seq", "expert"))
    nx = ns // 2
    tall = nz * ns
    any_ = pl.BlockSpec(memory_space=pl.ANY)
    dma = pltpu.SemaphoreType.DMA
    return pl.pallas_call(
        spread_kernel,
        out_shape=[
            jax.ShapeDtypeStruct((x.shape[0], ns * x.shape[1], x.shape[2]), BF),
            jax.ShapeDtypeStruct((x.shape[0], ns * x.shape[1], x.shape[2]), BF),
            jax.ShapeDtypeStruct((tall * ny * ain.shape[0], ain.shape[1]), BF),
            jax.ShapeDtypeStruct((tall * ny * aout.shape[0], aout.shape[1]), BF),
            jax.ShapeDtypeStruct((tall * ein.shape[0], ein.shape[1]), BF),
            jax.ShapeDtypeStruct((tall * eout.shape[0], eout.shape[1]), BF),
        ],
        in_specs=[any_] * 6,
        out_specs=[any_] * 6,
        scratch_shapes=[
            dma((2, 2 * nx)),
            dma((2, nx, 2)),
            dma((4, nz, 2)),
            dma((4, nz, nx - 1 + (ny - 1) * (1 + nx))),
            dma((4, nz, nx, ny)),
            dma((4, nz, nx, ny)),
            dma((4, nz, nx, ny)),
            dma((6,)),
        ],
        compiler_params=pltpu.CompilerParams(collective_id=0, has_side_effects=True),
        name="spread",
    )(x, m, ain, aout, ein, eout)


def add_into(total, other):
    lead = total.shape[:-2]
    count = 1
    for n in lead:
        count *= n
    rows = total.shape[-2]
    step = 48 if total.shape[-1] <= 1024 else 16

    def body(i, carry):
        index = []
        rest = i // (rows // step)
        for n in reversed(lead):
            index.insert(0, lax.rem(rest, n))
            rest = rest // n
        r = pl.ds(pl.multiple_of(lax.rem(i, rows // step) * step, 16), step)
        at = (*index, r)
        total[at] = (total[at].astype(F32) + other[at].astype(F32)).astype(total.dtype)
        return carry

    lax.fori_loop(0, count * (rows // step), body, 0)


def collect_kernel(g0, g1, g2, g3, o0, o1, o2, o3, c0, c1, c2, c3, y0, y1, x0, x1, x2, x3, z0, z1, z2, z3,
                   core_send, core_recv, y_send, y_recv, x_send, x_recv, z_send, z_recv):
    at = Place()
    nz, nx, ny = at.nz, at.nx, at.ny
    grads, outs = (g0, g1, g2, g3), (o0, o1, o2, o3)
    cores, ys, xs, zs_ = (c0, c1, c2, c3), (y0, y1), (x0, x1, x2, x3), (z0, z1, z2, z3)
    dense, expert = (0, 1), (2, 3)
    waits = []

    def copy(src, dst, ssem, rsem, **where):
        return pltpu.make_async_remote_copy(
            src_ref=src, dst_ref=dst, send_sem=ssem, recv_sem=rsem,
            device_id=at.device(**where), device_id_type=MESH,
        )

    def send(*args, **where):
        one = copy(*args, **where)
        one.start()
        waits.append(one.wait_send)

    def arrive(ref, sem):
        pltpu.make_async_copy(ref, ref, sem).wait()

    at.greet()
    order = [at.by_distance(nz - 1 - k) for k in range(nz)]

    def core_part(a, k, c):
        return grads[a].at[order[k], :, c]

    for k in range(nz):
        for a in range(4):
            send(core_part(a, k, 1 - at.c), cores[a].at[k], core_send.at[a, k], core_recv.at[a, k], c=1 - at.c)

    def stage_core(k):
        for a in expert + dense:
            arrive(cores[a].at[k], core_recv.at[a, k])
            add_into(cores[a].at[k], core_part(a, k, at.c))
            if a in expert:
                for j, x in enumerate(at.other_x()):
                    send(cores[a].at[k, x], xs[a].at[k, nx - 2 - j], x_send.at[a, k, j], x_recv.at[a, k, nx - 2 - j], x=x)
            else:
                for j, y in enumerate(at.other_y()):
                    send(cores[a].at[k, :, y], ys[a].at[k, ny - 2 - j], y_send.at[a, k, j], y_recv.at[a, k, ny - 2 - j], y=y)

    def stage_y(k):
        for a in dense:
            for j in range(ny - 1):
                arrive(ys[a].at[k, j], y_recv.at[a, k, j])
                add_into(ys[a].at[k, 0], ys[a].at[k, j] if j else cores[a].at[k, :, at.y])
            for j, x in enumerate(at.other_x()):
                send(ys[a].at[k, 0, x], xs[a].at[k, nx - 2 - j], x_send.at[a, k, j], x_recv.at[a, k, nx - 2 - j], x=x)

    def stage_x(k):
        for a in expert + dense:
            for j in range(nx - 1):
                arrive(xs[a].at[k, j], x_recv.at[a, k, j])
                own = cores[a].at[k, at.x] if a in expert else ys[a].at[k, 0, at.x]
                add_into(xs[a].at[k, 0], xs[a].at[k, j] if j else own)

    def stage_z(k):
        d = order[k]
        for a in expert + dense:
            total = xs[a].at[k, 0]
            for side, here in enumerate((at.z > 0, at.z < nz - 1)):
                feeds = here & ((d >= at.z) if side == 0 else (d <= at.z))

                @pl.when(feeds)
                def _(a=a, side=side, total=total):
                    arrive(zs_[a].at[side, d], z_recv.at[a, side, d])
                    add_into(total, zs_[a].at[side, d])

            if k == nz - 1:
                outs[a][...] = total[...].astype(F32)
                continue

            def hop(side, a=a, total=total):
                return copy(total, zs_[a].at[1 - side, d], z_send.at[a, d], z_recv.at[a, 1 - side, d],
                            z=at.z - 1 if side == 0 else at.z + 1)

            @pl.when(d < at.z)
            def _():
                hop(0).start()

            @pl.when(d > at.z)
            def _():
                hop(1).start()

            def wait(hop=hop):
                @pl.when(d < at.z)
                def _():
                    hop(0).wait_send()

                @pl.when(d > at.z)
                def _():
                    hop(1).wait_send()

            waits.append(wait)

    for t in range(nz + 2):
        if 0 <= t < nz:
            stage_core(t)
        if 0 <= t - 1 < nz:
            stage_y(t - 1)
        if 0 <= t - 2 < nz:
            stage_x(t - 2)
            stage_z(t - 2)
    for wait in waits:
        wait()


def collect(gin, gout, gein, geout):
    nz, ns, ny = (lax.axis_size(a) for a in ("dp", "seq", "expert"))
    nx = ns // 2
    width = gin.shape[-1]
    parts = (
        gin.reshape(nz, nx, 2, ny, -1, width),
        gout.reshape(nz, nx, 2, ny, -1, width),
        gein.reshape(nz, nx, 2, -1, gein.shape[-1]),
        geout.reshape(nz, nx, 2, -1, width),
    )
    ends = [p.shape[-2:] for p in parts]
    if not in_tiles(*parts):
        everywhere, peers = ("dp", "seq", "expert"), ("dp", "seq")
        return [
            lax.psum_scatter(a, over, scatter_dimension=0, tiled=True).astype(F32)
            for a, over in ((gin, everywhere), (gout, everywhere), (gein, peers), (geout, peers))
        ]
    vmem = pl.BlockSpec(memory_space=pltpu.VMEM)
    dma = pltpu.SemaphoreType.DMA
    return pl.pallas_call(
        collect_kernel,
        out_shape=[jax.ShapeDtypeStruct(e, F32) for e in ends],
        in_specs=[vmem] * 4,
        out_specs=[vmem] * 4,
        scratch_shapes=[
            *[pltpu.VMEM((nz, nx, ny, *e), BF) for e in ends[:2]],
            *[pltpu.VMEM((nz, nx, *e), BF) for e in ends[2:]],
            *[pltpu.VMEM((nz, ny - 1, nx, *e), BF) for e in ends[:2]],
            *[pltpu.VMEM((nz, nx - 1, *e), BF) for e in ends],
            *[pltpu.VMEM((2, nz, *e), BF) for e in ends],
            dma((4, nz)),
            dma((4, nz)),
            dma((2, nz, ny - 1)),
            dma((2, nz, ny - 1)),
            dma((4, nz, nx - 1)),
            dma((4, nz, nx - 1)),
            dma((4, nz)),
            dma((4, 2, nz)),
        ],
        compiler_params=pltpu.CompilerParams(
            collective_id=1, has_side_effects=True, vmem_limit_bytes=60 * 2**20
        ),
        name="collect",
    )(*parts)


def norm_apply(value, gain):
    return value * lax.rsqrt(jnp.mean(value * value, axis=-1, keepdims=True) + EPS) * gain


def norm_back(value, gain, grad):
    r = lax.rsqrt(jnp.mean(value * value, axis=-1, keepdims=True) + EPS)
    scaled = grad * gain
    back = r * scaled - value * (r * r * r) * jnp.mean(scaled * value, axis=-1, keepdims=True)
    return back, jnp.sum(grad * value * r, axis=0)


def gelu_tanh(value):
    return jax.nn.gelu(value, approximate=True)


def times(left, right):
    return jnp.dot(left, right, preferred_element_type=F32)


def times_right(left, right):
    return jnp.einsum("te,de->td", left, right, preferred_element_type=F32)


def times_left(left, right):
    return jnp.einsum("td,te->de", left, right, preferred_element_type=F32)


def split(a, packs):
    return a.reshape(packs, -1, HEADS, HEAD)


def attend(query, keys, values, allowed, bias, packs):
    scores = jnp.einsum("pqhd,pkhd->phqk", split(query, packs), split(keys, packs), preferred_element_type=F32)
    masked = jnp.where(allowed[:, None], scores * HEAD**-0.5 + bias, NEG)
    raised = jnp.exp(masked - jnp.max(masked, axis=3, keepdims=True))
    chances = raised / jnp.sum(raised, axis=3, keepdims=True)
    mixed = jnp.einsum("phqk,pkhd->pqhd", chances.astype(BF), split(values, packs), preferred_element_type=F32)
    return mixed.reshape(query.shape).astype(BF), chances


def attend_back(query, keys, values, chances, grad, packs):
    scale = HEAD**-0.5
    g4 = split(grad, packs)
    grad_chances = jnp.einsum("pqhd,pkhd->phqk", g4, split(values, packs), preferred_element_type=F32)
    spread_ = jnp.sum(chances * grad_chances, axis=3, keepdims=True)
    grad_scores = (chances * (grad_chances - spread_)).astype(BF)
    grad_query = jnp.einsum("phqk,pkhd->pqhd", grad_scores, split(keys, packs), preferred_element_type=F32) * scale
    grad_keys = jnp.einsum("phqk,pqhd->pkhd", grad_scores, split(query, packs), preferred_element_type=F32) * scale
    grad_values = jnp.einsum("phqk,pqhd->pkhd", chances.astype(BF), g4, preferred_element_type=F32)
    return (
        grad_query.reshape(query.shape).astype(BF),
        grad_keys.reshape(keys.shape).astype(BF),
        grad_values.reshape(keys.shape).astype(BF),
        grad_scores,
    )


def per_device(layer_input, memory, cotangent, routes, doc_lengths, rel_buckets, gains, bias_table, router,
               attn_in, attn_out, expert_in, expert_out):
    packs, rows, width = layer_input.shape[0], layer_input.shape[3], layer_input.shape[4]
    seqs = lax.axis_size("seq")
    group = rows * seqs
    experts = router.shape[1]
    capacity = (5 * rows + 4 * experts - 1) // (4 * experts)
    buckets = bias_table.shape[0]
    rank = lax.axis_index("seq")

    x_all, m_all, w_in, w_out, e_in, e_out = spread(
        layer_input[:, 0, 0], memory[:, 0, 0], attn_in, attn_out, expert_in[0], expert_out[0]
    )
    w_in = w_in.reshape(6, width, width)
    w_out = w_out.reshape(2, width, width)
    x_all = x_all.reshape(packs * group, width)
    m_all = m_all.reshape(packs * group, width)
    x_rows = layer_input.reshape(packs * rows, width).astype(F32)

    query_pos = rank * rows + jnp.arange(rows, dtype=jnp.int32)
    key_pos = jnp.arange(group, dtype=jnp.int32)
    ends = jnp.cumsum(doc_lengths[:, 0, 0], axis=1)
    query_doc = jnp.sum((query_pos[None, :, None] >= ends[:, None, :]).astype(jnp.int32), axis=2)
    key_doc = jnp.sum((key_pos[None, :, None] >= ends[:, None, :]).astype(jnp.int32), axis=2)
    same = query_doc[:, :, None] == key_doc[:, None, :]
    causal = same & (key_pos[None, None, :] <= query_pos[None, :, None])
    bucket_hot = (rel_buckets[:, None] == jnp.arange(buckets, dtype=jnp.int32)).astype(F32)
    line_at = jnp.arange(group + rows, dtype=jnp.int32) - (group - 1) + rank * rows
    line_hot = (jnp.take(rel_buckets, jnp.clip(line_at, 0, group - 1))[None, :] == jnp.arange(buckets)[:, None]).astype(F32)
    line = jnp.einsum("bh,bj->hj", bias_table, line_hot, precision=HIGHEST)
    line = line[:, ::-1]
    wide = group + rows
    tiled = jnp.broadcast_to(line[:, None, :], (HEADS, rows, wide)).reshape(HEADS, rows * wide)
    skew = tiled[:, rows : rows + rows * (wide - 1)].reshape(HEADS, rows, wide - 1)[:, :, :group]

    normed1_all = norm_apply(x_all.astype(F32), gains[0]).astype(BF)
    normed1 = norm_apply(x_rows, gains[0]).astype(BF)
    query = times(normed1, w_in[0]).astype(BF)
    keys = times(normed1_all, w_in[1]).astype(BF)
    values = times(normed1_all, w_in[2]).astype(BF)
    mem_keys = times(m_all, w_in[4]).astype(BF)
    mem_values = times(m_all, w_in[5]).astype(BF)
    mixed, chances_self = attend(query, keys, values, causal, skew[None], packs)
    hidden1 = x_rows + times(mixed, w_out[0])
    normed2 = norm_apply(hidden1, gains[1]).astype(BF)
    cross_query = times(normed2, w_in[3]).astype(BF)
    cross_mixed, chances_cross = attend(cross_query, mem_keys, mem_values, same, 0.0, packs)
    hidden2 = hidden1 + times(cross_mixed, w_out[1])
    normed3 = norm_apply(hidden2, gains[2]).astype(BF)

    routing = jax.nn.softmax(times(normed3, router), axis=1)
    route = routes[:, 0, 0, :, 0]
    route_hot = (route[:, :, None] == jnp.arange(experts, dtype=jnp.int32)).astype(jnp.int32)
    slot = jnp.sum((jnp.cumsum(route_hot, axis=1) - route_hot) * route_hot, axis=2)
    hot = route_hot.reshape(packs * rows, experts).astype(F32)
    gate = jnp.sum(routing * hot, axis=1)
    target = jnp.where(slot < capacity, (route * packs + jnp.arange(packs)[:, None]) * capacity + slot, -1).reshape(-1)
    dispatch = (target[:, None] == jnp.arange(experts * packs * capacity, dtype=jnp.int32)).astype(BF)

    def swap(a):
        shape = (experts, packs * capacity, width)
        return lax.all_to_all(a.reshape(shape), "expert", split_axis=0, concat_axis=0, tiled=True).reshape(-1, width)

    received = swap(times_left(dispatch, normed3).astype(BF))
    inner = times(received, e_in)
    hidden, pull = jax.vjp(gelu_tanh, inner)
    hidden = hidden.astype(BF)
    result = times(hidden, e_out).astype(BF)
    combined = times(dispatch, swap(result))
    out_rows = (hidden2 + gate[:, None] * combined).astype(BF)
    grad_top = cotangent.reshape(packs * rows, width).astype(F32)
    grad_gate = jnp.sum(grad_top * combined, axis=1)
    grad_result = swap(times_left(dispatch, (gate[:, None] * grad_top).astype(BF)).astype(BF))
    grad_hidden = times_right(grad_result, e_out)
    grad_eout = times_left(hidden, grad_result).astype(BF)
    grad_inner = pull(grad_hidden)[0].astype(BF)
    grad_ein = times_left(received, grad_inner).astype(BF)
    grad_send = swap(times_right(grad_inner, e_in).astype(BF))
    grad_logits = grad_gate[:, None] * routing * (hot - gate[:, None])
    grad_router = jnp.einsum("td,te->de", normed3.astype(F32), grad_logits, precision=HIGHEST)
    grad_normed3 = times(dispatch, grad_send) + jnp.einsum(
        "te,de->td", grad_logits, router.astype(F32), precision=HIGHEST
    )
    back3, gain3 = norm_back(hidden2, gains[2], grad_normed3)
    grad_h2 = grad_top + back3
    grad_h2_low = grad_h2.astype(BF)
    grad_wco = times_left(cross_mixed, grad_h2_low)
    grad_cross = times_right(grad_h2_low, w_out[1]).astype(BF)
    grad_cq, grad_ck, grad_cv, _ = attend_back(cross_query, mem_keys, mem_values, chances_cross, grad_cross, packs)
    back2, gain2 = norm_back(hidden1, gains[1], times_right(grad_cq, w_in[3]))
    grad_h1 = grad_h2 + back2
    grad_h1_low = grad_h1.astype(BF)
    grad_wso = times_left(mixed, grad_h1_low)
    grad_mixed = times_right(grad_h1_low, w_out[0]).astype(BF)
    grad_q, grad_k, grad_v, grad_scores = attend_back(query, keys, values, chances_self, grad_mixed, packs)

    total = jnp.sum(grad_scores.astype(F32), axis=0)[:, ::-1]
    padded = jnp.pad(total, ((0, 0), (0, 0), (0, wide - group))).reshape(HEADS, rows * wide)
    diagonal = padded[:, : rows * (wide - 1)].reshape(HEADS, rows, wide - 1).sum(axis=1)
    at = jnp.clip(rank * rows + (rows - 1) - jnp.arange(wide - 1, dtype=jnp.int32), 0, group - 1)
    diagonal_hot = (jnp.take(rel_buckets, at)[:, None] == jnp.arange(buckets)).astype(F32)
    grad_table = jnp.einsum("jb,hj->bh", diagonal_hot, diagonal, precision=HIGHEST)

    def to_owner(a):
        return lax.psum_scatter(a.reshape(packs, group, width), "seq", scatter_dimension=1, tiled=True)

    grad_memory = to_owner((times_right(grad_ck, w_in[4]) + times_right(grad_cv, w_in[5])).astype(BF))
    part1 = to_owner((times_right(grad_k, w_in[1]) + times_right(grad_v, w_in[2])).astype(BF))
    grad_normed1 = times_right(grad_q, w_in[0]) + part1.reshape(packs * rows, width).astype(F32)
    back1, gain1 = norm_back(x_rows, gains[0], grad_normed1)
    grad_x = grad_h1 + back1
    grad_in = jnp.concatenate(
        [
            times_left(normed1, grad_q),
            times_left(normed1_all, grad_k),
            times_left(normed1_all, grad_v),
            times_left(normed2, grad_cq),
            times_left(m_all, grad_ck),
            times_left(m_all, grad_cv),
        ]
    ).astype(BF)
    grad_out = jnp.concatenate([grad_wso, grad_wco]).astype(BF)
    shards = collect(grad_in, grad_out, grad_ein, grad_eout)
    small = lax.psum((jnp.stack([gain1, gain2, gain3]), grad_table, grad_router), ("dp", "seq", "expert"))
    shape = (packs, 1, 1, rows, width)
    return (
        out_rows.reshape(shape),
        grad_x.reshape(shape),
        grad_memory.astype(F32).reshape(shape),
        *small,
        shards[0],
        shards[1],
        shards[2][None],
        shards[3][None],
    )


def solution(mesh):
    tokens = P(None, "dp", "expert", "seq", None)
    dense = P(("dp", "seq", "expert"), None)
    expert = P("expert", ("dp", "seq"), None)
    return jax.shard_map(
        per_device,
        mesh=mesh,
        in_specs=(tokens, tokens, tokens, tokens, P(None, "dp", "expert", None), P(), P(), P(), P(),
                  dense, dense, expert, expert),
        out_specs=(tokens, tokens, tokens, P(), P(), P(), dense, dense, expert, expert),
        check_vma=False,
    )
```

time: 1170 us -> 488 us (0.42)
  waiting for transfers between devices: 424 us -> 1.16 us
  other arithmetic: 279 us -> 28.8 us
  Pallas kernels: 0 us -> 210 us
  matrix products: 179 us -> 109 us
  local copies, waits for them, and re-layouts: 125 us -> 55.3 us
  blocking collectives: 98.7 us -> 41 us
  starting transfers between devices: 33.9 us -> 18.1 us
    reduce_scatter x6 -> x2, waiting for transfers between devices: 275 us -> 0.01 us  [to_owner(): lax.psum_scatter(a.reshape(packs, group, width), 'seq', scatter_dimension...]
    scatter-add x2 -> x0, other arithmetic: 219 us -> none  [per_device(): jax.ops.segment_sum(jnp.transpose(grad_scores.astype(jnp.float32), (1, 2,...]
    pallas_call x0 -> x2, Pallas kernels: none -> 210 us  [the longest x1 118 us: collect(): pl.pallas_call(collect_kernel, out_shape=[jax.ShapeDtypeStruct(e, F32) fo...]
    unnamed x26 -> x2, waiting for transfers between devices: 104 us -> 0.03 us
    dot_general x101 -> x50, matrix products: 179 us -> 106 us  [the longest x12 29.2 us: times_left(): return jnp.einsum('td,te->de', left, right, preferred_element_type=F32)]
    all_gather x8 -> x0, blocking collectives: 56.3 us -> none  [the longest x2 15.5 us: per_device(): all_values = lax.all_gather(values, 'seq', axis=0, tiled=True)]
    gather x2, local copies, waits for them, and re-layouts: 60 us -> 6.36 us  [the longest x1 3.71 us: per_device(): jnp.take(rel_buckets, at)[:, None] == jnp.arange(buckets)]
    all_gather x4 -> x0, waiting for transfers between devices: 45.1 us -> none  [the longest x1 38.7 us: per_device(): lax.all_gather(expert_out, ('dp', 'seq'), axis=1, tiled=True)]
  transfers between devices with their start and end apart: 26 -> 6, of which waited for: 9 -> 1; matrix products, arithmetic and copies ran while one was open for 47% -> 13% of each run, Pallas kernels for 0% -> 25%
where the time goes in v1:
time: 488 us; the launch traced here: 479 us
  Pallas kernels  210 us (43%)
  matrix products  109 us (22%)
  local copies, waits for them, and re-layouts  55.3 us (11%)
  blocking collectives  41 us (8%)
  other arithmetic  28.8 us (6%)
  starting transfers between devices  18.1 us (4%)
  between operations  15.7 us (3%)
    pallas_call x1, Pallas kernels, collect(): pl.pallas_call(collect_kernel, out_shape=[jax.ShapeDtypeStruct(e, F32) fo...  118 us
    pallas_call x1, Pallas kernels, spread(): pl.pallas_call(spread_kernel, out_shape=[jax.ShapeDtypeStruct((x.shape[0]...  92.5 us
    psum x1, blocking collectives, per_device(): lax.psum((jnp.stack([gain1, gain2, gain3]), grad_table, grad_router), ('d...  41 us
    dot_general x12, matrix products, times_left(): return jnp.einsum('td,te->de', left, right, preferred_element_type=F32)  29.2 us
    dot_general x13, matrix products, times(): return jnp.dot(left, right, preferred_element_type=F32)  28.8 us
    dot_general x10, matrix products, times_right(): return jnp.einsum('te,de->td', left, right, preferred_element_type=F32)  25.3 us
    all_to_all x4, starting transfers between devices, swap(): lax.all_to_all(a.reshape(shape), 'expert', split_axis=0, concat_axis=0, t...  17.9 us
    reshape x12, local copies, waits for them, and re-layouts, split(): return a.reshape(packs, -1, HEADS, HEAD)  13.5 us
  transfers between devices with their start and end apart: 6, of which 1 were waited for; matrix products, arithmetic and copies ran while one was open for 13% of the time, Pallas kernels for 25%

profile of v1, /device:TPU:12, one launch (start us, length us, event | category | flops | bytes accessed | tf_op | source)
XLA Modules:
  0.0 479.4 jit_solution(16342660390559058621)
XLA Ops:
  8.4 1.4 slice_reduce_fusion
  10.9 92.5 %spread.1 = (bf16[2,256,768]{2,1,0:T(8,128)(2,1)}, bf16[2,256,768]{2,1,0:T(8,128)(2,1)}, bf16[4608,768]{1,0:T(8,128)(2,1)}, bf16[1536,768]{1,0:T(8,128)(2,1)}, b...) custom-call(bf16[2,64,768]{2,1,0:T(8,128)(2,1)} %bitcast.190, bf16[2,64,768]{2,1,0:T(8,128)(2,1)} %bitcast.222, ...), custom_call_target="tpu_custom_call" | custom-call | tf_op jit(solution)/shard_map/spread/pallas_call | solution.py:234
  106.7 2.1 convolution_convert_fusion.13
  108.8 3.0 convolution_convert_fusion.12
  111.8 3.0 convolution_convert_fusion.11
  114.8 2.9 convolution_convert_fusion.10
  119.9 1.6 convolution_convert_fusion.25
  123.0 2.6 gather_fusion
  131.1 1.6 add_select_fusion
  132.7 1.5 fusion.110
  134.4 2.8 fusion.27
  137.8 1.6 copy.84
  141.6 1.7 convolution_convert_fusion.24
  144.4 1.4 copy.105
  145.8 2.4 copy.86
  148.2 2.9 reshape.438
  151.2 2.9 fusion.111
  154.1 2.1 fusion.28
  163.4 2.0 convolution_convert_fusion.19
  165.4 5.0 %all-to-all-start.2 = ((bf16[2,80,768]{2,1,0:T(8,128)(2,1)}), bf16[2,80,768]{2,1,0:T(8,128)(2,1)}, u32[]{:S(2)}, u32[]{:S(2)}) async-start(bf16[2,80,768]{2,1,0:T(8,128)(2,1)} %bitcast.20), calls=%async_computation.2 | async-start | bytes 491520 | tf_op jit(solution)/shard_map/all_to_all | solution.py:557
  170.4 1.7 convolution_convert_fusion.21
  172.1 1.5 fusion.64
  173.5 3.7 gather_fusion.1
  178.5 1.9 multiply_convert_fusion.1
  180.9 3.5 all-to-all-start
  184.4 5.5 %fusion.115 = f32[160,3072]{1,0:T(8,128)} fusion(bf16[160,768]{1,0:T(8,128)(2,1)} %bitcast.21, bf16[3072,768]{1,0:T(8,128)(2,1)} %get-tuple-element.25), kind=kOutput, calls=%fused_computation.220 | convolution fusion | flops 754974720 | bytes 6930432 | tf_op jit(solution)/shard_map/te,de->td/dot_general | solution.py:459
  189.9 5.0 %fusion.8 = (bf16[160,3072]{1,0:T(8,128)(2,1)S(1)}, f32[160,3072]{1,0:T(8,128)S(1)}) fusion(f32[160,3072]{1,0:T(8,128)} %fusion.115, bf16[160,768]{1,0:T(8,128)(2,1)S(1)} %bitcast.201, bf16[768,3072]{1,0:T(8,128)(2,1)} %get-tuple-element.24), kind=kOutput, calls=%fused_computation.15 | convolution fusion | flops 764805120 | bytes 9879552 | tf_op jit(solution)/shard_map/dot_general | solution.py:455
  194.9 4.7 convolution_convert_fusion.20
  199.6 5.0 %convolution_convert_fusion = bf16[3072,768]{1,0:T(8,128)(2,1)} fusion(bf16[160,768]{1,0:T(8,128)(2,1)} %bitcast.21, f32[160,3072]{1,0:T(8,128)S(1)} %get-tuple-element.97), kind=kOutput, calls=%fused_computation.4 | convolution fusion | flops 761757696 | bytes 6930432 | tf_op jit(solution)/shard_map/td,te->de/dot_general | solution.py:463
  204.6 2.4 convolution_convert_fusion.18
  207.0 4.6 all-to-all-start.3
  211.6 4.8 convolution_convert_fusion.1
  216.4 4.9 %all-to-all-start.1 = ((bf16[2,80,768]{2,1,0:T(8,128)(2,1)}), bf16[2,80,768]{2,1,0:T(8,128)(2,1)}, u32[]{:S(2)}, u32[]{:S(2)}) async-start(bf16[2,80,768]{2,1,0:T(8,128)(2,1)} %bitcast.221), calls=%async_computation.1 | async-start | bytes 491520 | tf_op jit(solution)/shard_map/all_to_all | solution.py:557
  221.5 1.9 fusion.80
  225.9 2.1 multiply_reduce_fusion.3
  228.0 1.8 convert_add_fusion
  231.5 1.4 copy.107
  232.9 2.5 multiply_reduce_fusion.1
  238.3 1.9 convert_element_type.298
  240.2 2.7 multiply_reduce_fusion.4
  246.7 5.8 %fusion.21 = bf16[2,256,12,64]{1,3,2,0:T(8,128)(2,1)} fusion(bf16[2,64,12,64]{1,3,2,0:T(8,128)(2,1)} %copy.103, f32[2,12,64]{2,1,0:T(8,128)} %copy-done.54, f32[2,12,64,256]{3,2,1,0:T(8,128)} %copy-done.6), kind=kOutput, calls=%fused_computation.57 | convolution fusion | flops 51906304 | bytes 2562048 | tf_op jit(solution)/shard_map/phqk,pqhd->pkhd/dot_general | solution.py:487
  252.5 1.7 multiply_reduce_fusion
  254.2 1.4 convert_reduce_fusion
  259.8 1.5 convolution_convert_fusion.2
  262.3 2.4 fusion.43
  265.9 3.3 add_convert_fusion.1
  269.3 1.5 copy.100
  271.7 2.5 fusion.18
  274.3 1.8 fusion.17
  276.1 1.5 convolution_convert_fusion.3
  282.8 1.8 reshape.455
  284.5 2.2 reshape.456
  286.8 2.0 reduce_sum.234
  288.7 3.1 fusion.16
  291.9 1.7 fusion.15
  293.5 1.8 fusion.14
  295.4 2.2 fusion.33
  297.6 3.2 add_convert_fusion
  300.8 1.5 pad_maximum_fusion
  302.9 1.9 fusion.13
  304.8 117.9 %collect.1 = (f32[144,768]{1,0:T(8,128)}, f32[48,768]{1,0:T(8,128)}, f32[48,3072]{1,0:T(8,128)}, f32[192,768]{1,0:T(8,128)}) custom-call(bf16[4,2,2,2,144,768]{5,4,3,2,1,0:T(8,128)(2,1)} %bitcast.38.g0, bf16[4,2,2,2,48,768]{5,4,3,2,1,0:T(8,128)(2,1)} %bitcast.189, bf16[4,2,2,48,3072]{4,3,2,1,0:T(8,128)(2,1)} %bitcast.188, bf16[4,2,2,192,768]{4,3,2,1,0:T(8,128)(2,1)} %bitcast.195), custom_call_target="tpu_custom_call" | custom-call | tf_op jit(solution)/shard_map/collect/pallas_call | solution.py:412
  423.3 1.9 fusion.72
  425.3 41.0 %all-reduce.1 = (f32[3,768]{1,0:T(4,128)}, f32[32,12]{0,1:T(8,128)}, f32[768,2]{0,1:T(2,128)}) all-reduce(f32[3,768]{1,0:T(4,128)S(1)} %pad_maximum_fusion.1, f32[32,12]{0,1:T(8,128)S(1)} %fusion.79, f32[768,2]{0,1:T(2,128)S(1)} %fusion.107), channel_id=1, replica_groups=mesh['dp'=4,'seq'=4,'expert'=2] {'dp','seq','expert'}, use_global_device_ids=true, to_apply=%region_27.28 | all-reduce | flops 4224 | bytes 33792 | tf_op jit(solution)/shard_map/psum | solution.py:619
  467.3 1.8 bitcast_convert_fusion
  (301 shorter events, 56.1 us)
Async XLA Ops:
  7.2 118.5 %copy-start = (f32[32,12]{0,1:T(8,128)S(1)}, f32[32,12]{0,1:T(8,128)}, u32[]{:S(2)}) copy-start(f32[32,12]{0,1:T(8,128)} %param.20) | copy-start | bytes 4612
  108.8 3.0 copy-start.91
  119.1 3.2 copy-start.80
  119.9 3.1 copy-start.2
  122.3 8.8 %copy-start.17 = (bf16[2,64,12,64]{1,3,2,0:T(8,128)(2,1)}, bf16[2,64,12,64]{1,3,2,0:T(8,128)(2,1)S(1)}, u32[]{:S(2)}) copy-start(bf16[2,64,12,64]{1,3,2,0:T(8,128)(2,1)S(1)} %copy.101) | copy-start | bytes 589828
  134.2 3.0 copy-start.54
  137.8 2.7 copy-start.25
  137.8 2.7 copy-start.3
  140.9 15.9 %copy-start.10 = (f32[128,768]{1,0:T(8,128)}, f32[128,768]{1,0:T(8,128)S(1)}, u32[]{:S(2)}) copy-start(f32[128,768]{1,0:T(8,128)S(1)} %get-tuple-element.89) | copy-start | bytes 1179652
  145.8 5.4 %copy-start.31 = (bf16[2,64,12,64]{1,3,2,0:T(8,128)(2,1)}, bf16[2,64,12,64]{1,3,2,0:T(8,128)(2,1)S(1)}, u32[]{:S(2)}) copy-start(bf16[2,64,12,64]{1,3,2,0:T(8,128)(2,1)S(1)} %copy.105) | copy-start | bytes 589828
  145.8 5.4 %copy-start.59 = (pred[2,64,256]{2,1,0:T(8,128)(4,1)S(1)}, pred[2,64,256]{2,1,0:T(8,128)(4,1)}, u32[]{:S(2)}) copy-start(pred[2,64,256]{2,1,0:T(8,128)(4,1)} %get-tuple-element.78) | copy-start | bytes 98308
  156.6 5.1 %copy-start.56 = (f32[768]{0:T(1024)S(1)}, f32[768]{0:T(1024)}, u32[]{:S(2)}) copy-start(f32[768]{0:T(1024)} %get-tuple-element.66) | copy-start | bytes 9220
  156.9 4.8 %copy-start.27 = (bf16[128,768]{0,1:T(8,128)(2,1)}, bf16[128,768]{0,1:T(8,128)(2,1)S(1)}, u32[]{:S(2)}) copy-start(bf16[128,768]{0,1:T(8,128)(2,1)S(1)} %convert_element_type.278) | copy-start | bytes 589828
  157.3 8.0 %copy-start.8 = (f32[128,768]{1,0:T(8,128)}, f32[128,768]{1,0:T(8,128)S(1)}, u32[]{:S(2)}) copy-start(f32[128,768]{1,0:T(8,128)S(1)} %get-tuple-element.93) | copy-start | bytes 1179652
  157.9 7.5 %copy-start.78 = (f32[128]{0:T(128)}, f32[128]{0:T(128)S(1)}, u32[]{:S(2)}) copy-start(f32[128]{0:T(128)S(1)} %get-tuple-element.85) | copy-start | bytes 1540
  159.8 5.5 %copy-start.73 = (s32[128]{0:T(128)}, s32[128]{0:T(128)S(1)}, u32[]{:S(2)}) copy-start(s32[128]{0:T(128)S(1)} %eq.89) | copy-start | bytes 1540
  165.4 15.6 %all-to-all-start.2 = ((bf16[2,80,768]{2,1,0:T(8,128)(2,1)}), bf16[2,80,768]{2,1,0:T(8,128)(2,1)}, u32[]{:S(2)}, u32[]{:S(2)}) async-start(bf16[2,80,768]{2,1,0:T(8,128)(2,1)} %bitcast.20), calls=%async_computation.2 | async-start | bytes 491520 | tf_op jit(solution)/shard_map/all_to_all | solution.py:557
  170.4 8.2 %copy-start.4 = (bf16[2,256,768]{2,1,0:T(8,128)(2,1)S(1)}, bf16[2,256,768]{2,1,0:T(8,128)(2,1)}, u32[]{:S(2)}) copy-start(bf16[2,256,768]{2,1,0:T(8,128)(2,1)} %get-tuple-element.20) | copy-start | bytes 2359300
  177.2 3.2 copy-start.83
  180.9 8.9 %all-to-all-start = ((bf16[2,80,768]{2,1,0:T(8,128)(2,1)}), bf16[2,80,768]{2,1,0:T(8,128)(2,1)S(1)}, u32[]{:S(2)}, u32[]{:S(2)}) async-start(bf16[2,80,768]{2,1,0:T(8,128)(2,1)} %bitcast.203), calls=%async_computation | async-start | bytes 491520 | tf_op jit(solution)/shard_map/all_to_all | solution.py:557
  194.8 9.8 %copy-start.16 = (bf16[160,3072]{1,0:T(8,128)(2,1)}, bf16[160,3072]{1,0:T(8,128)(2,1)S(1)}, u32[]{:S(2)}) copy-start(bf16[160,3072]{1,0:T(8,128)(2,1)S(1)} %get-tuple-element.96) | copy-start | bytes 2949124
  194.8 9.7 %slice-start = ((s8[4718592]{0:T(1024)(128)(4,1)}), s8[4194304]{0:T(1024)(128)(4,1)S(1)}, s32[]{:S(2)}) async-start(s8[4718592]{0:T(1024)(128)(4,1)} %bitcast.193), calls=%async_computation.8 | async-start | bytes 8388608
  199.6 5.0 %slice-start.1 = ((s8[4718592]{0:T(1024)(128)(4,1)}), s8[524288]{0:T(1024)(128)(4,1)S(1)}, s32[]{:S(2)}) async-start(s8[4718592]{0:T(1024)(128)(4,1)} %bitcast.193), calls=%async_computation.9 | async-start | bytes 1048576
  207.0 9.4 %all-to-all-start.3 = ((bf16[2,80,768]{2,1,0:T(8,128)(2,1)}), bf16[2,80,768]{2,1,0:T(8,128)(2,1)}, u32[]{:S(2)}, u32[]{:S(2)}) async-start(bf16[2,80,768]{2,1,0:T(8,128)(2,1)} %bitcast.22), calls=%async_computation.3 | async-start | bytes 491520 | tf_op jit(solution)/shard_map/all_to_all | solution.py:557
  211.6 9.9 %copy-start.69 = (s32[128]{0:T(128)S(1)}, s32[128]{0:T(128)}, u32[]{:S(2)}) copy-start(s32[128]{0:T(128)} %copy-done.68) | copy-start | bytes 1540
  211.6 12.9 %copy-start.24 = (bf16[2,1,1,64,768]{4,3,2,1,0:T(8,128)(2,1)S(1)}, bf16[2,1,1,64,768]{4,3,2,1,0:T(8,128)(2,1)}, u32[]{:S(2)}) copy-start(bf16[2,1,1,64,768]{4,3,2,1,0:T(8,128)(2,1)} %param.15) | copy-start | bytes 589828
  216.4 9.5 %copy-start.9 = (f32[128,768]{1,0:T(8,128)S(1)}, f32[128,768]{1,0:T(8,128)}, u32[]{:S(2)}) copy-start(f32[128,768]{1,0:T(8,128)} %copy-done.8) | copy-start | bytes 1179652
  216.4 9.5 %copy-start.66 = (f32[128]{0:T(128)S(1)}, f32[128]{0:T(128)}, u32[]{:S(2)}) copy-start(f32[128]{0:T(128)} %copy-done.65) | copy-start | bytes 1540
  216.4 9.5 %copy-start.70 = (bf16[768,2]{0,1:T(2,128)(2,1)S(1)}, bf16[768,2]{0,1:T(2,128)(2,1)}, u32[]{:S(2)}) copy-start(bf16[768,2]{0,1:T(2,128)(2,1)} %param.21) | copy-start | bytes 9220
  216.4 9.5 %copy-start.71 = (f32[128,2]{0,1:T(2,128)S(1)}, f32[128,2]{0,1:T(2,128)}, u32[]{:S(2)}) copy-start(f32[128,2]{0,1:T(2,128)} %get-tuple-element.75) | copy-start | bytes 3076
  216.4 9.5 %copy-start.74 = (s32[128]{0:T(128)S(1)}, s32[128]{0:T(128)}, u32[]{:S(2)}) copy-start(s32[128]{0:T(128)} %copy-done.73) | copy-start | bytes 1540
  216.4 9.5 %copy-start.79 = (f32[128]{0:T(128)S(1)}, f32[128]{0:T(128)}, u32[]{:S(2)}) copy-start(f32[128]{0:T(128)} %copy-done.78) | copy-start | bytes 1540
  216.4 8.1 %all-to-all-start.1 = ((bf16[2,80,768]{2,1,0:T(8,128)(2,1)}), bf16[2,80,768]{2,1,0:T(8,128)(2,1)}, u32[]{:S(2)}, u32[]{:S(2)}) async-start(bf16[2,80,768]{2,1,0:T(8,128)(2,1)} %bitcast.221), calls=%async_computation.1 | async-start | bytes 491520 | tf_op jit(solution)/shard_map/all_to_all | solution.py:557
  221.3 202.0 %reduce-scatter.3.cloned.1.call-start = ((), (), s32[]{:S(2)}) async-start(), calls=%async_computation.6 | async-start | bytes 983040 | tf_op jit(solution)/shard_map/reduce_scatter | solution.py:600
  236.8 3.4 copy-start.11
  236.8 3.4 copy-start.87
  238.3 4.6 copy-start.89
  240.2 2.7 copy-start.12
  246.7 5.8 %copy-start.7 = (f32[2,12,64,256]{3,2,1,0:T(8,128)S(1)}, f32[2,12,64,256]{3,2,1,0:T(8,128)}, u32[]{:S(2)}) copy-start(f32[2,12,64,256]{3,2,1,0:T(8,128)} %get-tuple-element.87) | copy-start | bytes 4718596
  246.7 5.8 %copy-start.34 = (bf16[2,256,12,64]{1,0,3,2:T(2,128)(2,1)S(1)}, bf16[2,256,12,64]{1,0,3,2:T(2,128)(2,1)}, u32[]{:S(2)}) copy-start(bf16[2,256,12,64]{1,0,3,2:T(2,128)(2,1)} %reshape.430) | copy-start | bytes 2359300
  265.9 3.3 copy-start.37
  269.3 5.0 %copy-start.35 = (bf16[2,256,768]{2,1,0:T(8,128)(2,1)S(1)}, bf16[2,256,768]{2,1,0:T(8,128)(2,1)}, u32[]{:S(2)}) copy-start(bf16[2,256,768]{2,1,0:T(8,128)(2,1)} %multiply_convert_fusion.1) | copy-start | bytes 2359300
  269.3 5.0 %copy-start.45 = (bf16[96,8,2,256]{3,1,2,0:T(8,128)(2,1)S(1)}, bf16[96,8,2,256]{3,1,2,0:T(8,128)(2,1)}, u32[]{:S(2)}) copy-start(bf16[96,8,2,256]{3,1,2,0:T(8,128)(2,1)} %copy-done.44) | copy-start | bytes 2359300
  269.3 198.0 %reduce-scatter.5.cloned.1.call-start = ((), (), s32[]{:S(2)}) async-start(), calls=%async_computation.7 | async-start | bytes 983040 | tf_op jit(solution)/shard_map/reduce_scatter | solution.py:600
  288.7 3.1 copy-start.13
  288.7 3.1 copy-start.46
  288.7 3.1 copy-start.58
  288.7 3.1 copy-start.88
  297.6 3.2 copy-start.14
  297.6 3.2 copy-start.15
  304.8 118.0 %copy-start.60 = (f32[12,319]{1,0:T(8,128)S(1)}, f32[12,319]{1,0:T(8,128)}, u32[]{:S(2)}) copy-start(f32[12,319]{1,0:T(8,128)} %reduce_sum.234) | copy-start | bytes 45940
  304.8 118.0 %copy-start.85 = (s32[319]{0:T(512)S(1)}, s32[319]{0:T(512)}, u32[]{:S(2)}) copy-start(s32[319]{0:T(512)} %and_select_fusion) | copy-start | bytes 3832
  304.8 118.3 %copy-start.67 = (f32[128]{0:T(128)S(1)}, f32[128]{0:T(128)}, u32[]{:S(2)}) copy-start(f32[128]{0:T(128)} %copy-done.65) | copy-start | bytes 1540
  304.8 118.3 %copy-start.72 = (f32[128,2]{0,1:T(2,128)S(1)}, f32[128,2]{0,1:T(2,128)}, u32[]{:S(2)}) copy-start(f32[128,2]{0,1:T(2,128)} %get-tuple-element.75) | copy-start | bytes 3076
  304.8 118.3 %copy-start.75 = (s32[128]{0:T(128)S(1)}, s32[128]{0:T(128)}, u32[]{:S(2)}) copy-start(s32[128]{0:T(128)} %copy-done.73) | copy-start | bytes 1540
  304.8 118.3 %copy-start.77 = (f32[128]{0:T(128)S(1)}, f32[128]{0:T(128)}, u32[]{:S(2)}) copy-start(f32[128]{0:T(128)} %copy-done.76) | copy-start | bytes 1540
  304.8 118.5 %copy-start.52 = (bf16[128,768]{0,1:T(8,128)(2,1)S(1)}, bf16[128,768]{0,1:T(8,128)(2,1)}, u32[]{:S(2)}) copy-start(bf16[128,768]{0,1:T(8,128)(2,1)} %convert_element_type.304) | copy-start | bytes 589828
  304.8 118.5 %copy-start.84 = (f32[128]{0:T(128)S(1)}, f32[128]{0:T(128)}, u32[]{:S(2)}) copy-start(f32[128]{0:T(128)} %copy-done.82) | copy-start | bytes 1540
  422.7 43.6 %copy-start.90 = (f32[128]{0:T(128)S(1)}, f32[128]{0:T(128)}, u32[]{:S(2)}) copy-start(f32[128]{0:T(128)} %multiply_multiply_fusion.2) | copy-start | bytes 1540
  425.2 43.8 %copy-start.49 = (f32[144,768]{1,0:T(8,128)S(1)}, f32[144,768]{1,0:T(8,128)}, u32[]{:S(2)}) copy-start(f32[144,768]{1,0:T(8,128)} %get-tuple-element.125) | copy-start | bytes 1327108
  425.2 44.5 %copy-start.53 = (f32[48,768]{1,0:T(8,128)S(1)}, f32[48,768]{1,0:T(8,128)}, u32[]{:S(2)}) copy-start(f32[48,768]{1,0:T(8,128)} %get-tuple-element.126) | copy-start | bytes 442372
  466.3 4.1 copy-start.48
  467.3 4.0 copy-start.47
  469.0 3.1 copy-start.1
  (38 other events, 70.4 us)
Sparse Core Ops, SparseCore 0:
  269.4 27.1 reduce-scatter.2
  300.9 31.3 reduce-scatter.4

commit v2 on v1

--- a/solution.py
+++ b/solution.py
@@ -40,9 +40,12 @@
 
     def by_distance(self, k):
         order = [sorted(range(self.nz), key=lambda d: (abs(d - z), d)) for z in range(self.nz)]
-        out = jnp.int32(0)
-        for z in range(self.nz):
-            out = jnp.where(self.z == z, jnp.int32(order[z][k]), out)
+        return self.pick([row[k] for row in order])
+
+    def pick(self, values):
+        out = jnp.int32(values[0])
+        for z in range(1, self.nz):
+            out = jnp.where(self.z == z, jnp.int32(values[z]), out)
         return out
 
     def greet(self):
@@ -53,21 +56,119 @@
             pl.semaphore_signal(barrier, inc=1, device_id=self.device(y=y), device_id_type=MESH)
         pl.semaphore_signal(barrier, inc=1, device_id=self.device(c=1 - self.c), device_id_type=MESH)
 
-        @pl.when(self.z > 0)
-        def _():
-            pl.semaphore_signal(barrier, inc=1, device_id=self.device(z=self.z - 1), device_id_type=MESH)
-
-        @pl.when(self.z < self.nz - 1)
-        def _():
-            pl.semaphore_signal(barrier, inc=1, device_id=self.device(z=self.z + 1), device_id_type=MESH)
-
-        beside = jnp.where(self.z > 0, 1, 0) + jnp.where(self.z < self.nz - 1, 1, 0)
-        pl.semaphore_wait(barrier, self.nx - 1 + self.ny - 1 + 1 + beside)
-
-
-def spread_kernel(x_ref, m_ref, ain, aout, ein, eout, xo, mo, aino, aouto, eino, eouto,
-                  act_send, act_recv, line_send, side_send, core_send, ici_recv, core_recv, own_sem):
+        for k in range(1, self.nz):
+            z = lax.rem(self.z + k, self.nz)
+            pl.semaphore_signal(barrier, inc=1, device_id=self.device(z=z), device_id_type=MESH)
+        pl.semaphore_wait(barrier, self.nx - 1 + self.ny - 1 + 1 + self.nz - 1)
+
+
+def rms_rows(src, gain, dst, rows, step=64):
+    @pl.loop(0, rows // step)
+    def _(i):
+        at = pl.ds(pl.multiple_of(i * step, step), step)
+        value = src[at, :].astype(F32)
+        r = lax.rsqrt(jnp.mean(value * value, axis=-1, keepdims=True) + EPS)
+        dst[at, :] = (value * r * gain).astype(BF)
+
+
+def project(left, weight, base, dst):
+    width = dst.shape[-1]
+    step = 256 if width % 256 == 0 else width
+
+    @pl.loop(0, width // step)
+    def _(j):
+        at = pl.ds(pl.multiple_of(j * step, step), step)
+        out = jnp.dot(left[...], weight[pl.ds(base, width), at], preferred_element_type=F32)
+        dst[:, at] = out.astype(dst.dtype)
+
+
+def prepare_bias(rel, table, bias, rank, rows, group):
+    buckets, heads = table.shape
+    wide = group + 128
+    lane = lax.broadcasted_iota(jnp.int32, (group, wide), 1)
+    shift = jnp.where(lane < group, lane, lane - wide)
+    distance = jnp.clip(rank * rows - shift, 0, group - 1)
+    hot = (lax.broadcasted_iota(jnp.int32, (group, wide), 0) == distance).astype(F32).astype(BF)
+    which = jnp.dot(jnp.broadcast_to(rel[...].astype(F32), (8, group)).astype(BF), hot, preferred_element_type=F32)
+    picks = (lax.broadcasted_iota(jnp.int32, (buckets, wide), 0) == which[0:1].astype(jnp.int32)).astype(F32)
+    line = lax.dot_general(table[...], picks, (((0,), (0,)), ((), ())), precision=HIGHEST, preferred_element_type=F32)
+    for h in range(heads):
+        band = pltpu.roll(jnp.broadcast_to(line[h : h + 1], (rows, wide)), 0, 1, stride=1, stride_axis=0)
+        bias[h // 2, pl.ds((h % 2) * rows, rows), :] = band[:, :group]
+
+
+def prepare_masks(lengths, same, causal, rank, rows, group):
+    key = lax.broadcasted_iota(jnp.int32, (rows, group), 1)
+    query = rank * rows + lax.broadcasted_iota(jnp.int32, (rows, group), 0)
+    for p in range(same.shape[0]):
+        end = jnp.int32(0)
+        kd = jnp.zeros((rows, group), jnp.int32)
+        qd = jnp.zeros((rows, group), jnp.int32)
+        for n in range(lengths.shape[1]):
+            end = end + lengths[p, n]
+            kd = kd + jnp.where(key >= end, 1, 0)
+            qd = qd + jnp.where(query >= end, 1, 0)
+        same[p] = jnp.where(kd == qd, 0.0, NEG)
+        causal[p] = jnp.where((kd == qd) & (key <= query), 0.0, NEG)
+
+
+def two_heads(pair):
+    first = lax.broadcasted_iota(jnp.int32, pair.shape, 1) < HEAD
+    zero = jnp.zeros_like(pair)
+    return jnp.concatenate([jnp.where(first, pair, zero), jnp.where(first, zero, pair)], axis=0)
+
+
+def one_pair(stacked):
+    rows = stacked.shape[0] // 2
+    first = lax.broadcasted_iota(jnp.int32, (rows, stacked.shape[1]), 1) < HEAD
+    return jnp.where(first, stacked[:rows], stacked[rows:])
+
+
+def attend_pairs(query, keys, values, bias, mask, chances, mixed):
+    packs, pairs, double, group = chances.shape
+    rows = double // 2
+
+    def body(i, carry):
+        p, j = i // pairs, lax.rem(i, pairs)
+        mine = pl.ds(pl.multiple_of(p * rows, rows), rows)
+        theirs = pl.ds(pl.multiple_of(p * group, group), group)
+        lanes = pl.ds(pl.multiple_of(j * 128, 128), 128)
+        scores = lax.dot_general(
+            two_heads(query[mine, lanes]), keys[theirs, lanes], (((1,), (1,)), ((), ())), preferred_element_type=F32
+        )
+        scores = scores * HEAD**-0.5
+        if bias is not None:
+            scores = scores + bias[j]
+        scores = (scores.reshape(2, rows, group) + mask[p][None]).reshape(double, group)
+        raised = jnp.exp(scores - jnp.max(scores, axis=1, keepdims=True))
+        weights = (raised * (1.0 / jnp.sum(raised, axis=1, keepdims=True))).astype(BF)
+        chances[p, j] = weights
+        out = jnp.dot(weights, values[theirs, lanes], preferred_element_type=F32)
+        mixed[mine, lanes] = one_pair(out).astype(BF)
+        return carry
+
+    lax.fori_loop(0, packs * pairs, body, 0, unroll=2)
+
+
+def add_product(total, left, weight, base):
+    width = total.shape[-1]
+    step = 256 if width % 256 == 0 else width
+
+    @pl.loop(0, width // step)
+    def _(j):
+        at = pl.ds(pl.multiple_of(j * step, step), step)
+        total[:, at] += jnp.dot(left[...], weight[pl.ds(base, width), at], preferred_element_type=F32)
+
+
+def forward_kernel(lengths, rel, gains, table, x_ref, m_ref, ain, aout, ein, eout,
+                   ain_out, aout_out, eino, eouto, xo, mo, n1_all, q, k_, v, kc, vc, pr_self, pr_cross, mixed, n2,
+                   qc, cross_mixed, h1, h2, n3, n1,
+                   aino, aouto, bias, same, causal,
+                   act_send, act_recv, line_send, side_send, core_send, ici_recv, core_recv, own_sem):
     at = Place()
+    width = x_ref.shape[-1]
+    packs = x_ref.shape[0]
+    group = xo.shape[1]
     nz, nx, ny = at.nz, at.nx, at.ny
     tok = x_ref.shape[1]
     shards = (ain, aout, ein, eout)
@@ -81,7 +182,7 @@
         index = (z * at.ns + s) * ny + y if a in dense else z * at.ns + s
         return fulls[a].at[pl.ds(pl.multiple_of(index * rows, 16), rows)]
 
-    waits = []
+    waits, own_acts, own_dense = [], [], []
 
     def send(src, dst, ssem, rsem, **where):
         copy = pltpu.make_async_remote_copy(
@@ -102,7 +203,7 @@
         send(src, dst, act_send.at[i, nx - 1 + at.x], act_recv.at[i, at.x, at.c], c=1 - at.c)
         own = pltpu.make_async_copy(src, dst, own_sem.at[4 + i])
         own.start()
-        waits.append(own.wait)
+        own_acts.append(own.wait)
 
     def along_line(a, z, src):
         dst = spot(a, z, at.x, at.c, at.y)
@@ -148,8 +249,8 @@
         send(src, spot(a, z, x, at.c, y), core_send.at[a, z, x, y], core_recv.at[a, z, x, y], c=1 - at.c)
 
     zs = [at.by_distance(k) for k in range(nz)]
-    for group in (dense, expert):
-        for a in group:
+    for kind in (dense, expert):
+        for a in kind:
             along_line(a, at.z, shards[a])
     for k in range(nz):
         for a in dense:
@@ -160,7 +261,7 @@
             else:
                 own = pltpu.make_async_copy(shards[a], here, own_sem.at[a])
                 own.start()
-                waits.append(own.wait)
+                own_dense.append(own.wait)
             to_sides(a, zs[k], here if k else shards[a])
             to_core(a, zs[k], at.x, at.y, here if k else shards[a])
         if k == 0:
@@ -189,6 +290,18 @@
                     send(here, here, side_send.at[a, zs[k], nx - 1 + ny - 1 + j + (ny - 1) * x],
                          ici_recv.at[a, zs[k], x, at.y], y=y)
                 to_core(a, zs[k], x, at.y, here)
+    prepare_bias(rel, table, bias, at.s, tok, group)
+    prepare_masks(lengths, same, causal, at.s, tok, group)
+    for i, (src, full) in enumerate(acts):
+        for x in range(nx):
+            dst = full.at[:, pl.ds(pl.multiple_of((x * 2 + 1 - at.c) * tok, 16), tok)]
+            arrive(dst, act_recv.at[i, x, 1 - at.c])
+    own_acts[0]()
+    own_acts[1]()
+    for p in range(packs):
+        rms_rows(xo.at[p], gains[0:1], n1_all.at[pl.ds(p * group, group)], group)
+        h1[pl.ds(p * tok, tok), :] = x_ref[p].astype(F32)
+        n1[pl.ds(p * tok, tok), :] = n1_all[pl.ds(pl.multiple_of(p * group + at.s * tok, tok), tok), :]
     for k in range(nz):
         for a in dense:
             for y in at.other_y():
@@ -196,20 +309,44 @@
                     here = spot(a, zs[k], x, at.c, y)
                     arrive(here, ici_recv.at[a, zs[k], x, y])
                     to_core(a, zs[k], x, y, here)
+    for a in dense:
+        for z in range(nz):
+            for x in range(nx):
+                for y in range(ny):
+                    arrive(spot(a, z, x, 1 - at.c, y), core_recv.at[a, z, x, y])
+    for wait in own_dense:
+        wait()
+    keep = [pltpu.make_async_copy(aino, ain_out, own_sem.at[6]), pltpu.make_async_copy(aouto, aout_out, own_sem.at[7])]
+    for copy in keep:
+        copy.start()
+
+    project(n1, aino, 0, q)
+    project(n1_all, aino, width, k_)
+    project(n1_all, aino, 2 * width, v)
+    for p in range(packs):
+        project(mo.at[p], aino, 4 * width, kc.at[pl.ds(p * group, group)])
+        project(mo.at[p], aino, 5 * width, vc.at[pl.ds(p * group, group)])
+    attend_pairs(q, k_, v, bias, causal, pr_self, mixed)
+    add_product(h1, mixed, aouto, 0)
+    rms_rows(h1, gains[1:2], n2, packs * tok)
+    project(n2, aino, 3 * width, qc)
+    attend_pairs(qc, kc, vc, None, same, pr_cross, cross_mixed)
+    h2[...] = h1[...]
+    add_product(h2, cross_mixed, aouto, width)
+    rms_rows(h2, gains[2:3], n3, packs * tok)
+
+    for k in range(nz):
         for a in expert:
             for x in at.other_x():
                 here = spot(a, zs[k], x, at.c, at.y)
                 arrive(here, ici_recv.at[a, zs[k], x, at.y])
                 to_core(a, zs[k], x, at.y, here)
-    for a in range(4):
+    for a in expert:
         for z in range(nz):
             for x in range(nx):
-                for y in range(ny) if a in dense else [at.y]:
-                    arrive(spot(a, z, x, 1 - at.c, y), core_recv.at[a, z, x, y])
-    for i, (src, full) in enumerate(acts):
-        for x in range(nx):
-            dst = full.at[:, pl.ds(pl.multiple_of((x * 2 + 1 - at.c) * tok, 16), tok)]
-            arrive(dst, act_recv.at[i, x, 1 - at.c])
+                arrive(spot(a, z, x, 1 - at.c, at.y), core_recv.at[a, z, x, at.y])
+    for copy in keep:
+        copy.wait()
     for wait in waits:
         wait()
 
@@ -218,32 +355,41 @@
     return all(a.shape[-2] % 16 == 0 for a in arrays)
 
 
-def spread(x, m, ain, aout, ein, eout):
-    if not in_tiles(x, m, ain, aout, ein, eout):
-        everywhere, peers = ("dp", "seq", "expert"), ("dp", "seq")
-        return (
-            *[lax.all_gather(a, "seq", axis=1, tiled=True) for a in (x, m)],
-            *[lax.all_gather(a, everywhere, axis=0, tiled=True) for a in (ain, aout)],
-            *[lax.all_gather(a, peers, axis=0, tiled=True) for a in (ein, eout)],
-        )
+def forward(lengths, rel, gains, table, x, m, ain, aout, ein, eout):
     nz, ns, ny = (lax.axis_size(a) for a in ("dp", "seq", "expert"))
     nx = ns // 2
     tall = nz * ns
+    packs, tok, width = x.shape
+    group = ns * tok
+    pairs = width // 128
     any_ = pl.BlockSpec(memory_space=pl.ANY)
+    vmem = pl.BlockSpec(memory_space=pltpu.VMEM)
+    smem = pl.BlockSpec(memory_space=pltpu.SMEM)
     dma = pltpu.SemaphoreType.DMA
+    full = [(tall * ny * ain.shape[0], width), (tall * ny * aout.shape[0], width)]
+    low = lambda *shape: jax.ShapeDtypeStruct(shape, BF)
+    every, mine = low(packs * group, width), low(packs * tok, width)
+    chances = low(packs, pairs, 2 * tok, group)
+    wide = jax.ShapeDtypeStruct((packs * tok, width), F32)
     return pl.pallas_call(
-        spread_kernel,
+        forward_kernel,
         out_shape=[
-            jax.ShapeDtypeStruct((x.shape[0], ns * x.shape[1], x.shape[2]), BF),
-            jax.ShapeDtypeStruct((x.shape[0], ns * x.shape[1], x.shape[2]), BF),
-            jax.ShapeDtypeStruct((tall * ny * ain.shape[0], ain.shape[1]), BF),
-            jax.ShapeDtypeStruct((tall * ny * aout.shape[0], aout.shape[1]), BF),
-            jax.ShapeDtypeStruct((tall * ein.shape[0], ein.shape[1]), BF),
-            jax.ShapeDtypeStruct((tall * eout.shape[0], eout.shape[1]), BF),
+            low(*full[0]),
+            low(*full[1]),
+            low(tall * ein.shape[0], ein.shape[1]),
+            low(tall * eout.shape[0], width),
+            low(packs, group, width),
+            low(packs, group, width),
+            every, mine, every, every, every, every, chances, chances, mine, mine, mine, mine, wide, wide, mine, mine,
         ],
-        in_specs=[any_] * 6,
-        out_specs=[any_] * 6,
+        in_specs=[smem, *[vmem] * 5, *[any_] * 4],
+        out_specs=[*[any_] * 4, *[vmem] * 18],
         scratch_shapes=[
+            pltpu.VMEM(full[0], BF),
+            pltpu.VMEM(full[1], BF),
+            pltpu.VMEM((pairs, 2 * tok, group), F32),
+            pltpu.VMEM((packs, tok, group), F32),
+            pltpu.VMEM((packs, tok, group), F32),
             dma((2, 2 * nx)),
             dma((2, nx, 2)),
             dma((4, nz, 2)),
@@ -251,11 +397,13 @@
             dma((4, nz, nx, ny)),
             dma((4, nz, nx, ny)),
             dma((4, nz, nx, ny)),
-            dma((6,)),
+            dma((8,)),
         ],
-        compiler_params=pltpu.CompilerParams(collective_id=0, has_side_effects=True),
-        name="spread",
-    )(x, m, ain, aout, ein, eout)
+        compiler_params=pltpu.CompilerParams(
+            collective_id=0, has_side_effects=True, vmem_limit_bytes=60 * 2**20
+        ),
+        name="forward",
+    )(lengths, rel.reshape(1, -1), gains, table, x, m, ain, aout, ein, eout)
 
 
 def add_into(total, other):
@@ -264,7 +412,7 @@
     for n in lead:
         count *= n
     rows = total.shape[-2]
-    step = 48 if total.shape[-1] <= 1024 else 16
+    step = next(n for n in ((48, 32, 16) if total.shape[-1] <= 1024 else (16,)) if rows % n == 0)
 
     def body(i, carry):
         index = []
@@ -280,11 +428,121 @@
     lax.fori_loop(0, count * (rows // step), body, 0)
 
 
-def collect_kernel(g0, g1, g2, g3, o0, o1, o2, o3, c0, c1, c2, c3, y0, y1, x0, x1, x2, x3, z0, z1, z2, z3,
-                   core_send, core_recv, y_send, y_recv, x_send, x_recv, z_send, z_recv):
+def product_t(left, weight, base, dst, add=False):
+    width = weight.shape[-1]
+    step = 256 if width % 256 == 0 else width
+    shape = dst.shape[:-1]
+
+    @pl.loop(0, width // step)
+    def _(j):
+        at = pl.ds(pl.multiple_of(j * step, step), step)
+        rows = weight[pl.ds(pl.multiple_of(base + j * step, step), step), :]
+        out = lax.dot_general(left[...], rows, (((1,), (1,)), ((), ())), preferred_element_type=F32)
+        out = out.reshape(*shape, step)
+        where = (*[slice(None)] * len(shape), at)
+        if add:
+            out = out + dst[where].astype(F32)
+        dst[where] = out.astype(dst.dtype)
+
+
+def two_products_t(left1, base1, left2, base2, weight, dst):
+    width = weight.shape[-1]
+    step = 256 if width % 256 == 0 else width
+    shape = dst.shape[:-1]
+
+    @pl.loop(0, width // step)
+    def _(j):
+        at = pl.ds(pl.multiple_of(j * step, step), step)
+        out = 0.0
+        for left, base in ((left1, base1), (left2, base2)):
+            rows = weight[pl.ds(pl.multiple_of(base + j * step, step), step), :]
+            out = out + lax.dot_general(left[...], rows, (((1,), (1,)), ((), ())), preferred_element_type=F32)
+        dst[(*[slice(None)] * len(shape), at)] = out.reshape(*shape, step).astype(dst.dtype)
+
+
+def outer_product(left, right, dst, base):
+    width = dst.shape[-1]
+    step = 256 if width % 256 == 0 else width
+
+    @pl.loop(0, width // step)
+    def _(j):
+        at = pl.ds(pl.multiple_of(j * step, step), step)
+        out = lax.dot_general(left[:, at], right[...], (((0,), (0,)), ((), ())), preferred_element_type=F32)
+        dst[pl.ds(pl.multiple_of(base + j * step, step), step), :] = out.astype(dst.dtype)
+
+
+def norm_back_rows(value, gain, grad, total, gain_grad, step=64):
+    gain_grad[...] = jnp.zeros_like(gain_grad)
+
+    @pl.loop(0, value.shape[0] // step)
+    def _(i):
+        at = pl.ds(pl.multiple_of(i * step, step), step)
+        v, g = value[at, :].astype(F32), grad[at, :]
+        r = lax.rsqrt(jnp.mean(v * v, axis=-1, keepdims=True) + EPS)
+        scaled = g * gain
+        total[at, :] += r * scaled - v * (r * r * r) * jnp.mean(scaled * v, axis=-1, keepdims=True)
+        gain_grad[...] += jnp.sum(g * v * r, axis=0, keepdims=True)
+
+
+def attend_pairs_back(query, keys, values, chances, grad, grad_q, grad_k, grad_v, diagonal):
+    packs, pairs, double, group = chances.shape
+    rows = double // 2
+    scale = HEAD**-0.5
+
+    def body(i, carry):
+        p, j = i // pairs, lax.rem(i, pairs)
+        mine = pl.ds(pl.multiple_of(p * rows, rows), rows)
+        theirs = pl.ds(pl.multiple_of(p * group, group), group)
+        lanes = pl.ds(pl.multiple_of(j * 128, 128), 128)
+        ga = two_heads(grad[mine, lanes])
+        low = chances[p, j]
+        wide = low.astype(F32)
+        gp = lax.dot_general(ga, values[theirs, lanes], (((1,), (1,)), ((), ())), preferred_element_type=F32)
+        gs = (wide * (gp - jnp.sum(wide * gp, axis=1, keepdims=True))).astype(BF)
+        gq = jnp.dot(gs, keys[theirs, lanes], preferred_element_type=F32)
+        grad_q[mine, lanes] = (one_pair(gq) * scale).astype(BF)
+        gk = lax.dot_general(gs, two_heads(query[mine, lanes]), (((0,), (0,)), ((), ())), preferred_element_type=F32)
+        grad_k[theirs, lanes] = (gk * scale).astype(BF)
+        gv = lax.dot_general(low, ga, (((0,), (0,)), ((), ())), preferred_element_type=F32)
+        grad_v[theirs, lanes] = gv.astype(BF)
+        if diagonal is not None:
+            a = lax.broadcasted_iota(jnp.int32, (rows, rows), 0)
+            b = lax.broadcasted_iota(jnp.int32, (rows, rows), 1)
+            flip = (a + b == rows - 1).astype(F32).astype(BF)
+            for half in range(2):
+                turned = jnp.dot(flip, gs[half * rows : (half + 1) * rows], preferred_element_type=F32)
+                turned = jnp.concatenate([turned, jnp.zeros((rows, 128), F32)], axis=1)
+                band = pltpu.roll(turned, 0, 1, stride=1, stride_axis=0)
+                diagonal[pl.ds(2 * j + half, 1), :] += jnp.sum(band, axis=0, keepdims=True)
+        return carry
+
+    lax.fori_loop(0, packs * pairs, body, 0, unroll=2)
+
+
+def table_grad(rel, diagonal, rank, rows, group, buckets):
+    wide = group + 128
+    lane = lax.broadcasted_iota(jnp.int32, (group, wide), 1)
+    distance = jnp.clip(rank * rows + rows - 1 - lane, 0, group - 1)
+    hot = (lax.broadcasted_iota(jnp.int32, (group, wide), 0) == distance).astype(F32).astype(BF)
+    which = jnp.dot(jnp.broadcast_to(rel[...].astype(F32), (8, group)).astype(BF), hot, preferred_element_type=F32)
+    picks = (lax.broadcasted_iota(jnp.int32, (buckets, wide), 0) == which[0:1].astype(jnp.int32)).astype(F32)
+    return lax.dot_general(picks, diagonal[...], (((1,), (1,)), ((), ())), precision=HIGHEST, preferred_element_type=F32)
+
+
+def backward_kernel(rel, gains, x_rows, win_hbm, wout_hbm, gein_hbm, geout_hbm, m_all, n1_all, n1, q, k_, v, kc, vc,
+                    pr_self, pr_cross, mixed, n2, qc, cross_mixed, h1, gh2, gain3, grouter,
+                    o0, o1, o2, o3, grad_x, grad_mem, sum_wide, sum_table,
+                    win, wout, gin, gout, own2, own3, c0, c1, c2, c3, y0, y1, x0, x1, x2, x3, z0, z1, z2, z3,
+                    gb, ga, gq, gk, gv, gn, diagonal, gain_row, act_part, act_core, act_x, wide_sum, table_sum,
+                    wide_in, table_in,
+                    load_sem, core_send, core_recv, y_send, y_recv, x_send, x_recv, z_send, z_recv,
+                    act_send, act_recv, small_send, small_recv):
     at = Place()
     nz, nx, ny = at.nz, at.nx, at.ny
-    grads, outs = (g0, g1, g2, g3), (o0, o1, o2, o3)
+    packs, group = act_part.shape[1], m_all.shape[0] // act_part.shape[1]
+    tok, width = act_part.shape[4], m_all.shape[1]
+    buckets = table_sum.shape[1]
+    outs = (o0, o1, o2, o3)
     cores, ys, xs, zs_ = (c0, c1, c2, c3), (y0, y1), (x0, x1, x2, x3), (z0, z1, z2, z3)
     dense, expert = (0, 1), (2, 3)
     waits = []
@@ -304,73 +562,100 @@
         pltpu.make_async_copy(ref, ref, sem).wait()
 
     at.greet()
-    order = [at.by_distance(nz - 1 - k) for k in range(nz)]
-
-    def core_part(a, k, c):
-        return grads[a].at[order[k], :, c]
-
+
+    far = [[d for d in sorted(range(nz), key=lambda d: (-abs(d - z), d))] for z in range(nz)]
+    order_e = [at.pick([far[z][k] for z in range(nz)]) for k in range(nz)]
+    halves = [[d for d in row if d >= nz // 2] + [d for d in row if d < nz // 2] for row in far]
+    order_d = [at.pick([halves[z][k] for z in range(nz)]) for k in range(nz)]
+
+    loads = [
+        pltpu.make_async_copy(gein_hbm.at[:, :, at.c], own2, load_sem.at[0]),
+        pltpu.make_async_copy(geout_hbm.at[:, :, at.c], own3, load_sem.at[1]),
+        pltpu.make_async_copy(wout_hbm, wout, load_sem.at[2]),
+        pltpu.make_async_copy(win_hbm, win, load_sem.at[3]),
+    ]
     for k in range(nz):
-        for a in range(4):
-            send(core_part(a, k, 1 - at.c), cores[a].at[k], core_send.at[a, k], core_recv.at[a, k], c=1 - at.c)
-
-    def stage_core(k):
-        for a in expert + dense:
-            arrive(cores[a].at[k], core_recv.at[a, k])
-            add_into(cores[a].at[k], core_part(a, k, at.c))
-            if a in expert:
-                for j, x in enumerate(at.other_x()):
-                    send(cores[a].at[k, x], xs[a].at[k, nx - 2 - j], x_send.at[a, k, j], x_recv.at[a, k, nx - 2 - j], x=x)
-            else:
-                for j, y in enumerate(at.other_y()):
-                    send(cores[a].at[k, :, y], ys[a].at[k, ny - 2 - j], y_send.at[a, k, j], y_recv.at[a, k, ny - 2 - j], y=y)
-
-    def stage_y(k):
+        for a, src in ((2, gein_hbm), (3, geout_hbm)):
+            send(src.at[order_e[k], :, 1 - at.c], cores[a].at[k], core_send.at[a, k, 0], core_recv.at[a, k, 0], c=1 - at.c)
+        if k == 0:
+            for load in loads:
+                load.start()
+
+
+    def core_expert(k):
+        for a, own in ((2, own2), (3, own3)):
+            arrive(cores[a].at[k], core_recv.at[a, k, 0])
+            add_into(cores[a].at[k], own.at[order_e[k]])
+            for j, x in enumerate(at.other_x()):
+                send(cores[a].at[k, x], xs[a].at[k, nx - 2 - j], x_send.at[a, k, j], x_recv.at[a, k, nx - 2 - j], x=x)
+
+    def dense_rows(a, d, x, c):
+        rows = cores[a].shape[2]
+        return (gin, gout)[a].at[pl.ds(pl.multiple_of(((d * nx + x) * 2 + c) * rows, 16), rows)]
+
+    def start_dense(k):
         for a in dense:
+            for x in range(nx):
+                send(dense_rows(a, order_d[k], x, 1 - at.c), cores[a].at[k, x], core_send.at[a, k, x],
+                     core_recv.at[a, k, x], c=1 - at.c)
+
+    def core_dense(k):
+        for a in dense:
+            rows = ys[a].shape[3]
+            for x in range(nx):
+                arrive(cores[a].at[k, x], core_recv.at[a, k, x])
+                add_into(cores[a].at[k, x], dense_rows(a, order_d[k], x, at.c))
+            for j, y in enumerate(at.other_y()):
+                send(cores[a].at[k, :, pl.ds(pl.multiple_of(y * rows, 16), rows)], ys[a].at[k, ny - 2 - j],
+                     y_send.at[a, k, j], y_recv.at[a, k, ny - 2 - j], y=y)
+
+    def y_dense(k):
+        for a in dense:
+            rows = ys[a].shape[3]
             for j in range(ny - 1):
                 arrive(ys[a].at[k, j], y_recv.at[a, k, j])
-                add_into(ys[a].at[k, 0], ys[a].at[k, j] if j else cores[a].at[k, :, at.y])
+                own = cores[a].at[k, :, pl.ds(pl.multiple_of(at.y * rows, 16), rows)]
+                add_into(ys[a].at[k, 0], ys[a].at[k, j] if j else own)
             for j, x in enumerate(at.other_x()):
                 send(ys[a].at[k, 0, x], xs[a].at[k, nx - 2 - j], x_send.at[a, k, j], x_recv.at[a, k, nx - 2 - j], x=x)
 
-    def stage_x(k):
-        for a in expert + dense:
+    def x_and_line(kind, k):
+        d = (order_e if kind is expert else order_d)[k]
+        for a in kind:
+            total = xs[a].at[k, 0]
             for j in range(nx - 1):
                 arrive(xs[a].at[k, j], x_recv.at[a, k, j])
                 own = cores[a].at[k, at.x] if a in expert else ys[a].at[k, 0, at.x]
-                add_into(xs[a].at[k, 0], xs[a].at[k, j] if j else own)
-
-    def stage_z(k):
-        d = order[k]
-        for a in expert + dense:
-            total = xs[a].at[k, 0]
-            for side, here in enumerate((at.z > 0, at.z < nz - 1)):
-                feeds = here & ((d >= at.z) if side == 0 else (d <= at.z))
+                add_into(total, xs[a].at[k, j] if j else own)
+            for side in range(2):
+                feeds = (at.z > 0) & (d >= at.z) if side == 0 else (at.z < nz - 1) & (d <= at.z)
+                slot = d if side == 0 else jnp.where(d == at.z, nz, d)
 
                 @pl.when(feeds)
-                def _(a=a, side=side, total=total):
-                    arrive(zs_[a].at[side, d], z_recv.at[a, side, d])
-                    add_into(total, zs_[a].at[side, d])
-
-            if k == nz - 1:
-                outs[a][...] = total[...].astype(F32)
-                continue
-
-            def hop(side, a=a, total=total):
-                return copy(total, zs_[a].at[1 - side, d], z_send.at[a, d], z_recv.at[a, 1 - side, d],
-                            z=at.z - 1 if side == 0 else at.z + 1)
+                def _(a=a, slot=slot, total=total):
+                    arrive(zs_[a].at[slot], z_recv.at[a, slot])
+                    add_into(total, zs_[a].at[slot])
+
+            def hop(to, a=a, total=total):
+                slot = d if to > 0 else jnp.where(d == at.z - 1, nz, d)
+                return copy(total, zs_[a].at[slot], z_send.at[a, k], z_recv.at[a, slot], z=at.z + to)
 
             @pl.when(d < at.z)
             def _():
-                hop(0).start()
+                hop(-1).start()
 
             @pl.when(d > at.z)
             def _():
                 hop(1).start()
 
+            @pl.when(d == at.z)
+            def _(a=a, total=total):
+                outs[a][...] = total[...].astype(F32)
+
             def wait(hop=hop):
                 @pl.when(d < at.z)
                 def _():
-                    hop(0).wait_send()
+                    hop(-1).wait_send()
 
                 @pl.when(d > at.z)
                 def _():
@@ -378,62 +663,222 @@
 
             waits.append(wait)
 
-    for t in range(nz + 2):
-        if 0 <= t < nz:
-            stage_core(t)
-        if 0 <= t - 1 < nz:
-            stage_y(t - 1)
-        if 0 <= t - 2 < nz:
-            stage_x(t - 2)
-            stage_z(t - 2)
+    def start_act(w):
+        send(act_part.at[w, :, :, 1 - at.c], act_core.at[w], act_send.at[w, 0], act_recv.at[w, 0], c=1 - at.c)
+
+    def core_act(w):
+        arrive(act_core.at[w], act_recv.at[w, 0])
+        add_into(act_core.at[w], act_part.at[w, :, :, at.c])
+        for j, x in enumerate(at.other_x()):
+            send(act_core.at[w, :, x], act_x.at[w, nx - 2 - j], act_send.at[w, 1 + j], act_recv.at[w, nx - 1 - j], x=x)
+
+    def x_act(w):
+        for j in range(nx - 1):
+            arrive(act_x.at[w, j], act_recv.at[w, 1 + j])
+        for p in range(packs):
+            out = act_core[w, p, at.x].astype(F32)
+            for j in range(nx - 1):
+                out = out + act_x[w, j, p].astype(F32)
+            if w == 0:
+                grad_mem[pl.ds(p * tok, tok), :] = out
+            else:
+                gn[pl.ds(p * tok, tok), :] += out
+
+    pair_sums = ((wide_sum, wide_in), (table_sum, table_in))
+    stages = [("c", [1 - at.c]), ("y", at.other_y()), ("x", at.other_x())]
+
+    def start_small(t):
+        axis, peers = stages[t]
+        for i, (total, inbox) in enumerate(pair_sums):
+            for j, peer in enumerate(peers):
+                back = len(peers) - 1 - j
+                base = [0, 1, ny][t]
+                send(total.at[t], inbox.at[base + back], small_send.at[i, base + j], small_recv.at[i, base + back], **{axis: peer})
+
+    def end_small(t):
+        axis, peers = stages[t]
+        base = [0, 1, ny][t]
+        for i, (total, inbox) in enumerate(pair_sums):
+            out = total[t]
+            for j in range(len(peers)):
+                arrive(inbox.at[base + j], small_recv.at[i, base + j])
+                out = out + inbox[base + j]
+            total[t + 1] = out
+
+    tail = ny + nx - 1
+
+    def start_line():
+        for i, (total, inbox) in enumerate(pair_sums):
+            for j in range(1, nz):
+                z = lax.rem(at.z + j, nz)
+                send(total.at[3], inbox.at[tail + at.z], small_send.at[i, tail + j], small_recv.at[i, tail + at.z], z=z)
+
+    def end_line():
+        for i, (total, inbox) in enumerate(pair_sums):
+            for j in range(1, nz):
+                z = lax.rem(at.z + j, nz)
+                arrive(inbox.at[tail + z], small_recv.at[i, tail + z])
+            out = None
+            for z in range(nz):
+                term = jnp.where(at.z == z, total[3], inbox[tail + z])
+                out = term if out is None else out + term
+            (sum_wide, sum_table)[i][...] = out
+
+    diagonal[...] = jnp.zeros_like(diagonal)
+    for i, (_, inbox) in enumerate(pair_sums):
+        inbox[pl.ds(tail + at.z, 1)] = jnp.zeros_like(inbox[pl.ds(0, 1)])
+    wide_sum[0] = jnp.zeros_like(wide_sum[0])
+    wide_sum[0, 2:3, :] = gain3[...]
+    wide_sum[0, pl.ds(3, grouter.shape[0]), :] = grouter[...]
+    gb[...] = gh2[...].astype(BF)
+    loads[0].wait()
+    loads[1].wait()
+    core_expert(0)
+    loads[2].wait()
+    product_t(gb, wout, width, ga)
+    outer_product(cross_mixed, gb, gout, width)
+    core_expert(1)
+    attend_pairs_back(qc, kc, vc, pr_cross, ga, gq, gk, gv, None)
+    core_expert(2)
+    loads[3].wait()
+    outer_product(n2, gq, gin, 3 * width)
+    outer_product(m_all, gk, gin, 4 * width)
+    outer_product(m_all, gv, gin, 5 * width)
+    core_expert(3)
+    for k in range(nz // 2):
+        start_dense(k)
+    two_products_t(gk, 4 * width, gv, 5 * width, win, act_part.at[0])
+    start_act(0)
+    x_and_line(expert, 0)
+    product_t(gq, win, 3 * width, gn)
+    grad_x[...] = gh2[...]
+    norm_back_rows(h1, gains[1:2], gn, grad_x, gain_row)
+    wide_sum[0, 1:2, :] = gain_row[...]
+    gb[...] = grad_x[...].astype(BF)
+    product_t(gb, wout, 0, ga)
+    core_dense(0)
+    outer_product(mixed, gb, gout, 0)
+    core_act(0)
+    core_dense(1)
+    x_and_line(expert, 1)
+    attend_pairs_back(q, k_, v, pr_self, ga, gq, gk, gv, diagonal)
+    outer_product(n1, gq, gin, 0)
+    outer_product(n1_all, gk, gin, width)
+    outer_product(n1_all, gv, gin, 2 * width)
+    for k in range(nz // 2, nz):
+        start_dense(k)
+    two_products_t(gk, width, gv, 2 * width, win, act_part.at[1])
+    start_act(1)
+    y_dense(0)
+    x_and_line(expert, 2)
+    core_act(1)
+    y_dense(1)
+    for k in range(nz // 2, nz):
+        core_dense(k)
+    product_t(gq, win, 0, gn)
+    table_sum[0] = table_grad(rel, diagonal, at.s, tok, group, buckets)
+    x_and_line(expert, 3)
+    x_act(0)
+    x_and_line(dense, 0)
+    x_act(1)
+    norm_back_rows(x_rows, gains[0:1], gn, grad_x, gain_row)
+    wide_sum[0, 0:1, :] = gain_row[...]
+    start_small(0)
+    y_dense(2)
+    end_small(0)
+    start_small(1)
+    x_and_line(dense, 1)
+    end_small(1)
+    start_small(2)
+    y_dense(3)
+    end_small(2)
+    start_line()
+    x_and_line(dense, 2)
+    end_line()
+    x_and_line(dense, 3)
     for wait in waits:
         wait()
 
 
-def collect(gin, gout, gein, geout):
+def backward(rel, gains, x_rows, w_in, w_out, gein, geout, acts, heads, buckets):
     nz, ns, ny = (lax.axis_size(a) for a in ("dp", "seq", "expert"))
     nx = ns // 2
-    width = gin.shape[-1]
-    parts = (
-        gin.reshape(nz, nx, 2, ny, -1, width),
-        gout.reshape(nz, nx, 2, ny, -1, width),
-        gein.reshape(nz, nx, 2, -1, gein.shape[-1]),
-        geout.reshape(nz, nx, 2, -1, width),
-    )
-    ends = [p.shape[-2:] for p in parts]
-    if not in_tiles(*parts):
-        everywhere, peers = ("dp", "seq", "expert"), ("dp", "seq")
-        return [
-            lax.psum_scatter(a, over, scatter_dimension=0, tiled=True).astype(F32)
-            for a, over in ((gin, everywhere), (gout, everywhere), (gein, peers), (geout, peers))
-        ]
+    width = gains.shape[1]
+    m_all, q, pr = acts[0], acts[3], acts[8]
+    packs, group = pr.shape[0], pr.shape[3]
+    tok = group // ns
+    extra = -(-(3 + acts[-1].shape[0]) // 8) * 8
+    ends = [
+        (w_in.shape[0] // (nz * ns * ny), width),
+        (w_out.shape[0] // (nz * ns * ny), width),
+        (gein.shape[0] // (nz * ns), gein.shape[1]),
+        (geout.shape[0] // (nz * ns), width),
+    ]
+    any_ = pl.BlockSpec(memory_space=pl.ANY)
     vmem = pl.BlockSpec(memory_space=pltpu.VMEM)
     dma = pltpu.SemaphoreType.DMA
+    low = lambda *shape: pltpu.VMEM(shape, BF)
+    wide = lambda *shape: pltpu.VMEM(shape, F32)
+    small = 1 + ny - 1 + nx - 1 + nz
     return pl.pallas_call(
-        collect_kernel,
-        out_shape=[jax.ShapeDtypeStruct(e, F32) for e in ends],
-        in_specs=[vmem] * 4,
-        out_specs=[vmem] * 4,
+        backward_kernel,
+        out_shape=[
+            *[jax.ShapeDtypeStruct(e, F32) for e in ends],
+            jax.ShapeDtypeStruct((packs * tok, width), F32),
+            jax.ShapeDtypeStruct((packs * tok, width), F32),
+            jax.ShapeDtypeStruct((extra, width), F32),
+            jax.ShapeDtypeStruct((buckets, 128), F32),
+        ],
+        in_specs=[*[vmem] * 3, *[any_] * 4, *[vmem] * len(acts)],
+        out_specs=[vmem] * 8,
         scratch_shapes=[
-            *[pltpu.VMEM((nz, nx, ny, *e), BF) for e in ends[:2]],
-            *[pltpu.VMEM((nz, nx, *e), BF) for e in ends[2:]],
-            *[pltpu.VMEM((nz, ny - 1, nx, *e), BF) for e in ends[:2]],
-            *[pltpu.VMEM((nz, nx - 1, *e), BF) for e in ends],
-            *[pltpu.VMEM((2, nz, *e), BF) for e in ends],
-            dma((4, nz)),
-            dma((4, nz)),
+            low(*w_in.shape),
+            low(*w_out.shape),
+            low(*w_in.shape),
+            low(*w_out.shape),
+            *[low(nz, nx, *e) for e in ends[2:]],
+            *[low(nz, nx, ny * e[0], e[1]) for e in ends[:2]],
+            *[low(nz, nx, *e) for e in ends[2:]],
+            *[low(nz, ny - 1, nx, *e) for e in ends[:2]],
+            *[low(nz, nx - 1, *e) for e in ends],
+            *[low(nz + 1, *e) for e in ends],
+            low(packs * tok, width),
+            low(packs * tok, width),
+            low(packs * tok, width),
+            low(packs * group, width),
+            low(packs * group, width),
+            wide(packs * tok, width),
+            wide(128, group + 128),
+            wide(1, width),
+            low(2, packs, nx, 2, tok, width),
+            low(2, packs, nx, tok, width),
+            low(2, nx - 1, packs, tok, width),
+            wide(4, extra, width),
+            wide(4, buckets, 128),
+            wide(small, extra, width),
+            wide(small, buckets, 128),
+            dma((4,)),
+            dma((4, nz, nx)),
+            dma((4, nz, nx)),
             dma((2, nz, ny - 1)),
             dma((2, nz, ny - 1)),
             dma((4, nz, nx - 1)),
             dma((4, nz, nx - 1)),
             dma((4, nz)),
-            dma((4, 2, nz)),
+            dma((4, nz + 1)),
+            dma((2, nx)),
+            dma((2, nx)),
+            dma((2, small)),
+            dma((2, small)),
         ],
         compiler_params=pltpu.CompilerParams(
-            collective_id=1, has_side_effects=True, vmem_limit_bytes=60 * 2**20
+            collective_id=1, has_side_effects=True, vmem_limit_bytes=62 * 2**20
         ),
-        name="collect",
-    )(*parts)
+        name="backward",
+    )(
+        rel.reshape(1, -1), gains, x_rows, w_in, w_out,
+        gein.reshape(nz, nx, 2, *ends[2]), geout.reshape(nz, nx, 2, *ends[3]), *acts,
+    )
 
 
 def norm_apply(value, gain):
@@ -503,45 +948,59 @@
     buckets = bias_table.shape[0]
     rank = lax.axis_index("seq")
 
-    x_all, m_all, w_in, w_out, e_in, e_out = spread(
-        layer_input[:, 0, 0], memory[:, 0, 0], attn_in, attn_out, expert_in[0], expert_out[0]
-    )
+    x_in, m_in, e_in, e_out = layer_input[:, 0, 0], memory[:, 0, 0], expert_in[0], expert_out[0]
+    fits = in_tiles(x_in, attn_in, attn_out, e_in, e_out)
+    x_rows = x_in.reshape(packs * rows, width).astype(F32)
+    if fits:
+        (
+            w_in, w_out, e_in, e_out, x_all, m_all, normed1_all, query, keys, values, mem_keys, mem_values,
+            chances_self, chances_cross, mixed, normed2, cross_query, cross_mixed, hidden1, hidden2, normed3, normed1,
+        ) = forward(
+            doc_lengths[:, 0, 0], rel_buckets, gains, bias_table, x_in, m_in, attn_in, attn_out, e_in, e_out
+        )
+        pairs_self, pairs_cross = chances_self, chances_cross
+        chances_self, chances_cross = (a.reshape(packs, HEADS, rows, group) for a in (chances_self, chances_cross))
+    else:
+        everywhere, peers = ("dp", "seq", "expert"), ("dp", "seq")
+        x_all, m_all = (lax.all_gather(a, "seq", axis=1, tiled=True) for a in (x_in, m_in))
+        w_in, w_out = (lax.all_gather(a, everywhere, axis=0, tiled=True) for a in (attn_in, attn_out))
+        e_in, e_out = (lax.all_gather(a, peers, axis=0, tiled=True) for a in (e_in, e_out))
     w_in = w_in.reshape(6, width, width)
     w_out = w_out.reshape(2, width, width)
     x_all = x_all.reshape(packs * group, width)
     m_all = m_all.reshape(packs * group, width)
-    x_rows = layer_input.reshape(packs * rows, width).astype(F32)
-
-    query_pos = rank * rows + jnp.arange(rows, dtype=jnp.int32)
-    key_pos = jnp.arange(group, dtype=jnp.int32)
-    ends = jnp.cumsum(doc_lengths[:, 0, 0], axis=1)
-    query_doc = jnp.sum((query_pos[None, :, None] >= ends[:, None, :]).astype(jnp.int32), axis=2)
-    key_doc = jnp.sum((key_pos[None, :, None] >= ends[:, None, :]).astype(jnp.int32), axis=2)
-    same = query_doc[:, :, None] == key_doc[:, None, :]
-    causal = same & (key_pos[None, None, :] <= query_pos[None, :, None])
-    bucket_hot = (rel_buckets[:, None] == jnp.arange(buckets, dtype=jnp.int32)).astype(F32)
-    line_at = jnp.arange(group + rows, dtype=jnp.int32) - (group - 1) + rank * rows
-    line_hot = (jnp.take(rel_buckets, jnp.clip(line_at, 0, group - 1))[None, :] == jnp.arange(buckets)[:, None]).astype(F32)
-    line = jnp.einsum("bh,bj->hj", bias_table, line_hot, precision=HIGHEST)
-    line = line[:, ::-1]
     wide = group + rows
-    tiled = jnp.broadcast_to(line[:, None, :], (HEADS, rows, wide)).reshape(HEADS, rows * wide)
-    skew = tiled[:, rows : rows + rows * (wide - 1)].reshape(HEADS, rows, wide - 1)[:, :, :group]
-
-    normed1_all = norm_apply(x_all.astype(F32), gains[0]).astype(BF)
-    normed1 = norm_apply(x_rows, gains[0]).astype(BF)
-    query = times(normed1, w_in[0]).astype(BF)
-    keys = times(normed1_all, w_in[1]).astype(BF)
-    values = times(normed1_all, w_in[2]).astype(BF)
-    mem_keys = times(m_all, w_in[4]).astype(BF)
-    mem_values = times(m_all, w_in[5]).astype(BF)
-    mixed, chances_self = attend(query, keys, values, causal, skew[None], packs)
-    hidden1 = x_rows + times(mixed, w_out[0])
-    normed2 = norm_apply(hidden1, gains[1]).astype(BF)
-    cross_query = times(normed2, w_in[3]).astype(BF)
-    cross_mixed, chances_cross = attend(cross_query, mem_keys, mem_values, same, 0.0, packs)
-    hidden2 = hidden1 + times(cross_mixed, w_out[1])
-    normed3 = norm_apply(hidden2, gains[2]).astype(BF)
+    if not fits:
+        query_pos = rank * rows + jnp.arange(rows, dtype=jnp.int32)
+        key_pos = jnp.arange(group, dtype=jnp.int32)
+        ends = jnp.cumsum(doc_lengths[:, 0, 0], axis=1)
+        query_doc = jnp.sum((query_pos[None, :, None] >= ends[:, None, :]).astype(jnp.int32), axis=2)
+        key_doc = jnp.sum((key_pos[None, :, None] >= ends[:, None, :]).astype(jnp.int32), axis=2)
+        same = query_doc[:, :, None] == key_doc[:, None, :]
+        causal = same & (key_pos[None, None, :] <= query_pos[None, :, None])
+        bucket_hot = (rel_buckets[:, None] == jnp.arange(buckets, dtype=jnp.int32)).astype(F32)
+        line_at = jnp.arange(group + rows, dtype=jnp.int32) - (group - 1) + rank * rows
+        line_hot = (jnp.take(rel_buckets, jnp.clip(line_at, 0, group - 1))[None, :] == jnp.arange(buckets)[:, None]).astype(F32)
+        line = jnp.einsum("bh,bj->hj", bias_table, line_hot, precision=HIGHEST)
+        line = line[:, ::-1]
+        wide = group + rows
+        tiled = jnp.broadcast_to(line[:, None, :], (HEADS, rows, wide)).reshape(HEADS, rows * wide)
+        skew = tiled[:, rows : rows + rows * (wide - 1)].reshape(HEADS, rows, wide - 1)[:, :, :group]
+
+        normed1_all = norm_apply(x_all.astype(F32), gains[0]).astype(BF)
+        normed1 = norm_apply(x_rows, gains[0]).astype(BF)
+        query = times(normed1, w_in[0]).astype(BF)
+        keys = times(normed1_all, w_in[1]).astype(BF)
+        values = times(normed1_all, w_in[2]).astype(BF)
+        mem_keys = times(m_all, w_in[4]).astype(BF)
+        mem_values = times(m_all, w_in[5]).astype(BF)
+        mixed, chances_self = attend(query, keys, values, causal, skew[None], packs)
+        hidden1 = x_rows + times(mixed, w_out[0])
+        normed2 = norm_apply(hidden1, gains[1]).astype(BF)
+        cross_query = times(normed2, w_in[3]).astype(BF)
+        cross_mixed, chances_cross = attend(cross_query, mem_keys, mem_values, same, 0.0, packs)
+        hidden2 = hidden1 + times(cross_mixed, w_out[1])
+        normed3 = norm_apply(hidden2, gains[2]).astype(BF)
 
     routing = jax.nn.softmax(times(normed3, router), axis=1)
     route = routes[:, 0, 0, :, 0]
@@ -578,6 +1037,28 @@
     )
     back3, gain3 = norm_back(hidden2, gains[2], grad_normed3)
     grad_h2 = grad_top + back3
+    shape = (packs, 1, 1, rows, width)
+    if fits:
+        acts = (
+            m_all, normed1_all, normed1, query, keys, values, mem_keys, mem_values, pairs_self, pairs_cross, mixed,
+            normed2, cross_query, cross_mixed, hidden1, grad_h2, gain3[None], grad_router.T,
+        )
+        *shards, grad_x, grad_memory, sums, table = backward(
+            rel_buckets, gains, x_rows, w_in.reshape(-1, width), w_out.reshape(-1, width), grad_ein, grad_eout,
+            acts, HEADS, buckets,
+        )
+        return (
+            out_rows.reshape(shape),
+            grad_x.reshape(shape),
+            grad_memory.reshape(shape),
+            sums[:3],
+            table[:, :HEADS],
+            sums[3 : 3 + experts].T,
+            shards[0],
+            shards[1],
+            shards[2][None],
+            shards[3][None],
+        )
     grad_h2_low = grad_h2.astype(BF)
     grad_wco = times_left(cross_mixed, grad_h2_low)
     grad_cross = times_right(grad_h2_low, w_out[1]).astype(BF)
@@ -615,7 +1096,10 @@
         ]
     ).astype(BF)
     grad_out = jnp.concatenate([grad_wso, grad_wco]).astype(BF)
-    shards = collect(grad_in, grad_out, grad_ein, grad_eout)
+    shards = [
+        lax.psum_scatter(a, over, scatter_dimension=0, tiled=True).astype(F32)
+        for a, over in ((grad_in, everywhere), (grad_out, everywhere), (grad_ein, peers), (grad_eout, peers))
+    ]
     small = lax.psum((jnp.stack([gain1, gain2, gain3]), grad_table, grad_router), ("dp", "seq", "expert"))
     shape = (packs, 1, 1, rows, width)
     return (

time: 488 us -> 288 us (0.59); the launches traced: 479 us -> 287 us
  matrix products: 109 us -> 28.6 us
  blocking collectives: 41 us -> 0 us
  local copies, waits for them, and re-layouts: 55.3 us -> 14.4 us
  other arithmetic: 28.8 us -> 5.09 us
  between operations: 15.7 us -> 0.85 us
  Pallas kernels: 210 us -> 216 us
    psum x1 -> x0, blocking collectives: 41 us -> none  [per_device(): lax.psum((jnp.stack([gain1, gain2, gain3]), grad_table, grad_router), ('d...]
    dot_general x13 -> x0, matrix products: 20.3 us -> none  [the longest x2 7.17 us: attend_back(): jnp.einsum('phqk,pqhd->pkhd', chances.astype(BF), g4, preferred_element_t...]
    dot_general x13 -> x5, matrix products: 28.8 us -> 8.83 us  [times(): return jnp.dot(left, right, preferred_element_type=F32)]
    reshape x16 -> x0, local copies, waits for them, and re-layouts: 19.2 us -> none  [the longest x12 13.5 us: split(): return a.reshape(packs, -1, HEADS, HEAD)]
    dot_general x12 -> x4, matrix products: 29.2 us -> 10.7 us  [times_left(): return jnp.einsum('td,te->de', left, right, preferred_element_type=F32)]
    dot_general x10 -> x2, matrix products: 25.3 us -> 7.77 us  [times_right(): return jnp.einsum('te,de->td', left, right, preferred_element_type=F32)]
    convert_element_type x16 -> x0, local copies, waits for them, and re-layouts: 14.7 us -> none  [the longest x4 5.45 us: attend_back(): grad_query.reshape(query.shape).astype(BF)]
    gather x2 -> x0, local copies, waits for them, and re-layouts: 6.36 us -> none  [the longest x1 3.71 us: per_device(): jnp.take(rel_buckets, at)[:, None] == jnp.arange(buckets)]
  transfers between devices with their start and end apart: 6 -> 4, of which waited for: 1 -> 2; matrix products, arithmetic and copies ran while one was open for 13% -> 4% of each run, Pallas kernels for 25% -> 0%
where the time goes in v2:
time: 288 us; the launch traced here: 287 us
  Pallas kernels  216 us (75%)
  matrix products  28.6 us (10%)
  starting transfers between devices  17.7 us (6%)
  local copies, waits for them, and re-layouts  14.4 us (5%)
  other arithmetic  5.09 us (2%)
  waiting for transfers between devices  3.47 us (1%)
    pallas_call x1, Pallas kernels, backward(): pl.pallas_call(backward_kernel, out_shape=[*[jax.ShapeDtypeStruct(e, F32)...  119 us
    pallas_call x1, Pallas kernels, forward(): pl.pallas_call(forward_kernel, out_shape=[low(*full[0]), low(*full[1]), l...  97.9 us
    all_to_all x4, starting transfers between devices, swap(): lax.all_to_all(a.reshape(shape), 'expert', split_axis=0, concat_axis=0, t...  17.7 us
    dot_general x4, matrix products, times_left(): return jnp.einsum('td,te->de', left, right, preferred_element_type=F32)  10.7 us
    unnamed x35, local copies, waits for them, and re-layouts  10.1 us
    dot_general x5, matrix products, times(): return jnp.dot(left, right, preferred_element_type=F32)  8.83 us
    dot_general x2, matrix products, times_right(): return jnp.einsum('te,de->td', left, right, preferred_element_type=F32)  7.77 us
  transfers between devices with their start and end apart: 4, of which 2 were waited for; matrix products, arithmetic and copies ran while one was open for 4% of the time, Pallas kernels for 0%

profile of v2, /device:TPU:12, one launch (start us, length us, event | category | flops | bytes accessed | tf_op | source)
XLA Modules:
  0.0 286.5 jit_solution(13766129508392526262)
XLA Ops:
  0.6 0.0 copy-start
  0.7 0.0 copy-start.4
  0.7 0.0 copy-start.2
  0.7 1.4 copy.23.table
  2.1 0.5 broadcast.102
  2.6 1.3 reduce.5
  4.0 0.1 eq.37
  4.1 0.8 fusion.17
  4.8 0.1 reduce_window_sum.11
  4.9 0.9 select_reduce_fusion
  5.8 0.1 reduce_sum.68
  5.9 0.1 add.52
  6.0 97.9 %forward.1 = (bf16[4608,768]{1,0:T(8,128)(2,1)}, bf16[1536,768]{1,0:T(8,128)(2,1)}, bf16[768,3072]{1,0:T(8,128)(2,1)}, bf16[3072,768]{1,0:T(8,128)(2,1)}, bf16[2...) custom-call(s32[2,3]{1,0:T(2,128)} %bitcast.85, ...), custom_call_target="tpu_custom_call" | custom-call | tf_op jit(solution)/shard_map/forward/pallas_call | solution.py:374
  103.8 0.0 copy-start.1
  103.9 0.0 copy-done
  103.9 1.1 fusion.23
  105.0 0.1 fusion.20
  105.1 0.0 copy-done.2
  105.1 1.0 convolution_convert_fusion.3
  106.1 3.9 %all-to-all-start.2 = ((bf16[2,80,768]{2,1,0:T(8,128)(2,1)}), bf16[2,80,768]{2,1,0:T(8,128)(2,1)S(1)}, u32[]{:S(2)}, u32[]{:S(2)}) async-start(bf16[2,80,768]{2,1,0:T(8,128)(2,1)} %bitcast.15), calls=%async_computation.2 | async-start | bytes 491520 | tf_op jit(solution)/shard_map/all_to_all | solution.py:1016
  110.1 2.0 convolution_convert_fusion.5
  112.0 0.0 copy-done.4
  112.0 0.8 bitcast_convert_fusion.x_rows
  112.8 0.0 copy-done.1
  112.8 0.1 multiply_reduce_fusion.2
  113.0 0.7 slice_reduce_fusion
  113.7 0.6 all-to-all-done.2
  114.3 5.2 %all-to-all-start = ((bf16[2,80,768]{2,1,0:T(8,128)(2,1)}), bf16[2,80,768]{2,1,0:T(8,128)(2,1)S(1)}, u32[]{:S(2)}, u32[]{:S(2)}) async-start(bf16[2,80,768]{2,1,0:T(8,128)(2,1)} %bitcast.7), calls=%async_computation | async-start | bytes 491520 | tf_op jit(solution)/shard_map/all_to_all | solution.py:1016
  119.5 5.4 %fusion.24 = f32[160,3072]{1,0:T(8,128)} fusion(bf16[160,768]{1,0:T(8,128)(2,1)S(1)} %bitcast.68, bf16[3072,768]{1,0:T(8,128)(2,1)} %get-tuple-element.42), kind=kOutput, calls=%fused_computation.53 | convolution fusion | flops 754974720 | bytes 6930432 | tf_op jit(solution)/shard_map/te,de->td/dot_general | solution.py:904
  124.9 0.0 all-to-all-done
  124.9 5.1 %fusion.6 = (bf16[160,3072]{1,0:T(8,128)(2,1)S(1)}, f32[160,3072]{1,0:T(8,128)S(1)}) fusion(f32[160,3072]{1,0:T(8,128)} %fusion.24, bf16[160,768]{1,0:T(8,128)(2,1)S(1)} %bitcast.64, bf16[768,3072]{1,0:T(8,128)(2,1)} %get-tuple-element.41), kind=kOutput, calls=%fused_computation.10 | convolution fusion | flops 764805120 | bytes 9879552 | tf_op jit(solution)/shard_map/dot_general | solution.py:900
  130.0 0.0 slice-done.2
  130.0 0.0 slice-done.3
  130.1 0.0 slice-start
  130.1 2.0 convolution_convert_fusion.4
  132.1 4.1 %convolution_convert_fusion = bf16[3072,768]{1,0:T(8,128)(2,1)} fusion(bf16[160,768]{1,0:T(8,128)(2,1)S(1)} %bitcast.69, f32[160,3072]{1,0:T(8,128)S(1)} %get-tuple-element.89), kind=kOutput, calls=%fused_computation | convolution fusion | flops 761757696 | bytes 6930432 | tf_op jit(solution)/shard_map/td,te->de/dot_general | solution.py:908
  136.1 0.0 slice-done.1
  136.1 2.4 convolution_convert_fusion.2
  138.5 3.6 %all-to-all-start.3 = ((bf16[2,80,768]{2,1,0:T(8,128)(2,1)}), bf16[2,80,768]{2,1,0:T(8,128)(2,1)S(1)}, u32[]{:S(2)}, u32[]{:S(2)}) async-start(bf16[2,80,768]{2,1,0:T(8,128)(2,1)} %bitcast.21), calls=%async_computation.3 | async-start | bytes 491520 | tf_op jit(solution)/shard_map/all_to_all | solution.py:1016
  142.1 3.6 %convolution_convert_fusion.1 = bf16[768,3072]{1,0:T(8,128)(2,1)} fusion(bf16[160,768]{1,0:T(8,128)(2,1)S(1)} %bitcast.65, bf16[160,3072]{1,0:T(8,128)(2,1)S(1)} %get-tuple-element.88), kind=kOutput, calls=%fused_computation.1 | convolution fusion | flops 757334016 | bytes 5947392 | tf_op jit(solution)/shard_map/td,te->de/dot_general | solution.py:908
  145.8 0.0 all-to-all-done.3
  145.8 5.0 %all-to-all-start.1 = ((bf16[2,80,768]{2,1,0:T(8,128)(2,1)}), bf16[2,80,768]{2,1,0:T(8,128)(2,1)S(1)}, u32[]{:S(2)}, u32[]{:S(2)}) async-start(bf16[2,80,768]{2,1,0:T(8,128)(2,1)} %bitcast.9), calls=%async_computation.1 | async-start | bytes 491520 | tf_op jit(solution)/shard_map/all_to_all | solution.py:1016
  150.8 0.2 fusion.11
  151.0 2.8 all-to-all-done.1
  153.9 0.3 fusion.8
  154.2 0.0 copy-done.3
  154.2 0.8 fusion.21.grouter
  155.0 0.5 multiply_reduce_fusion
  155.5 0.6 broadcast_in_dim.11.gain3
  156.1 1.0 convert_add_fusion
  157.1 118.5 %backward.1 = (f32[144,768]{1,0:T(8,128)}, f32[48,768]{1,0:T(8,128)}, f32[48,3072]{1,0:T(8,128)}, f32[192,768]{1,0:T(8,128)}, f32[128,768]{1,0:T(8,128)}, /*inde...) custom-call(s32[1,256]{1,0:T(1,128)} %bitcast.84, f32[3,768]{1,0:T(4,128)} %gains.3, ...), custom_call_target="tpu_custom_call" | custom-call | tf_op jit(solution)/shard_map/backward/pallas_call | solution.py:823
  275.7 0.0 copy-start.7
  275.7 0.0 copy-start.8
  275.7 0.0 copy-start.6
  275.7 1.4 slice.13
  277.1 1.3 slice_bitcast_fusion
  278.5 1.4 copy.27
  279.9 1.8 copy.34
  281.7 1.8 copy.35
  283.5 0.8 copy.36
  284.2 0.0 copy-done.8
  284.2 0.7 copy.37
  284.9 0.8 copy.38
  285.7 0.8 copy.39
  (16 shorter events, 0.1 us)
Async XLA Ops:
  0.6 103.2 %copy-start = (bf16[768,2]{0,1:T(2,128)(2,1)S(1)}, bf16[768,2]{0,1:T(2,128)(2,1)}, u32[]{:S(2)}) copy-start(bf16[768,2]{0,1:T(2,128)(2,1)} %param.21) | copy-start | bytes 9220
  0.7 111.4 %copy-start.4 = (bf16[2,1,1,64,768]{4,3,2,1,0:T(8,128)(2,1)S(1)}, bf16[2,1,1,64,768]{4,3,2,1,0:T(8,128)(2,1)}, u32[]{:S(2)}) copy-start(bf16[2,1,1,64,768]{4,3,2,1,0:T(8,128)(2,1)} %param.13) | copy-start | bytes 589828
  0.7 104.4 %copy-start.2 = (bf16[2,1,1,64,768]{4,3,2,1,0:T(8,128)(2,1)S(1)}, bf16[2,1,1,64,768]{4,3,2,1,0:T(8,128)(2,1)}, u32[]{:S(2)}) copy-start(bf16[2,1,1,64,768]{4,3,2,1,0:T(8,128)(2,1)} %param.15) | copy-start | bytes 589828
  103.8 9.0 %copy-start.1 = (f32[128,768]{1,0:T(8,128)S(1)}, f32[128,768]{1,0:T(8,128)}, u32[]{:S(2)}) copy-start(f32[128,768]{1,0:T(8,128)} %get-tuple-element.39) | copy-start | bytes 1179652
  106.1 8.2 %all-to-all-start.2 = ((bf16[2,80,768]{2,1,0:T(8,128)(2,1)}), bf16[2,80,768]{2,1,0:T(8,128)(2,1)S(1)}, u32[]{:S(2)}, u32[]{:S(2)}) async-start(bf16[2,80,768]{2,1,0:T(8,128)(2,1)} %bitcast.15), calls=%async_computation.2 | async-start | bytes 491520 | tf_op jit(solution)/shard_map/all_to_all | solution.py:1016
  114.3 10.5 %all-to-all-start = ((bf16[2,80,768]{2,1,0:T(8,128)(2,1)}), bf16[2,80,768]{2,1,0:T(8,128)(2,1)S(1)}, u32[]{:S(2)}, u32[]{:S(2)}) async-start(bf16[2,80,768]{2,1,0:T(8,128)(2,1)} %bitcast.7), calls=%async_computation | async-start | bytes 491520 | tf_op jit(solution)/shard_map/all_to_all | solution.py:1016
  119.5 10.5 %slice-start.2 = ((s8[4718592]{0:T(1024)(128)(4,1)}), s8[524288]{0:T(1024)(128)(4,1)S(1)}, s32[]{:S(2)}) async-start(s8[4718592]{0:T(1024)(128)(4,1)} %bitcast.60), calls=%async_computation.6 | async-start | bytes 1048576
  124.9 5.2 %slice-start.3 = ((s8[4718592]{0:T(1024)(128)(4,1)}), s8[4194304]{0:T(1024)(128)(4,1)S(1)}, s32[]{:S(2)}) async-start(s8[4718592]{0:T(1024)(128)(4,1)} %bitcast.60), calls=%async_computation.7 | async-start | bytes 8388608
  130.1 6.1 %slice-start = ((s8[4718592]{0:T(1024)(128)(4,1)}), s8[4194304]{0:T(1024)(128)(4,1)S(1)}, s32[]{:S(2)}) async-start(s8[4718592]{0:T(1024)(128)(4,1)} %bitcast.58), calls=%async_computation.4 | async-start | bytes 8388608
  132.1 4.1 %slice-start.1 = ((s8[4718592]{0:T(1024)(128)(4,1)}), s8[524288]{0:T(1024)(128)(4,1)S(1)}, s32[]{:S(2)}) async-start(s8[4718592]{0:T(1024)(128)(4,1)} %bitcast.58), calls=%async_computation.5 | async-start | bytes 1048576
  138.5 7.2 %all-to-all-start.3 = ((bf16[2,80,768]{2,1,0:T(8,128)(2,1)}), bf16[2,80,768]{2,1,0:T(8,128)(2,1)S(1)}, u32[]{:S(2)}, u32[]{:S(2)}) async-start(bf16[2,80,768]{2,1,0:T(8,128)(2,1)} %bitcast.21), calls=%async_computation.3 | async-start | bytes 491520 | tf_op jit(solution)/shard_map/all_to_all | solution.py:1016
  145.8 8.5 %copy-start.3 = (bf16[128,768]{1,0:T(8,128)(2,1)S(1)}, bf16[128,768]{1,0:T(8,128)(2,1)}, u32[]{:S(2)}) copy-start(bf16[128,768]{1,0:T(8,128)(2,1)} %get-tuple-element.40) | copy-start | bytes 589828
  145.8 8.1 %all-to-all-start.1 = ((bf16[2,80,768]{2,1,0:T(8,128)(2,1)}), bf16[2,80,768]{2,1,0:T(8,128)(2,1)S(1)}, u32[]{:S(2)}, u32[]{:S(2)}) async-start(bf16[2,80,768]{2,1,0:T(8,128)(2,1)} %bitcast.9), calls=%async_computation.1 | async-start | bytes 491520 | tf_op jit(solution)/shard_map/all_to_all | solution.py:1016
  275.7 7.8 %copy-start.7 = (f32[144,768]{1,0:T(8,128)S(1)}, f32[144,768]{1,0:T(8,128)}, u32[]{:S(2)}) copy-start(f32[144,768]{1,0:T(8,128)} %get-tuple-element.109) | copy-start | bytes 1327108
  275.7 8.5 %copy-start.8 = (f32[48,768]{1,0:T(8,128)S(1)}, f32[48,768]{1,0:T(8,128)}, u32[]{:S(2)}) copy-start(f32[48,768]{1,0:T(8,128)} %get-tuple-element.110) | copy-start | bytes 442372
  275.7 9.2 %copy-start.6 = (f32[48,3072]{1,0:T(8,128)S(1)}, f32[48,3072]{1,0:T(8,128)}, u32[]{:S(2)}) copy-start(f32[48,3072]{1,0:T(8,128)} %get-tuple-element.66) | copy-start | bytes 1769476
  279.9 5.8 %copy-start.5 = (f32[192,768]{1,0:T(8,128)S(1)}, f32[192,768]{1,0:T(8,128)}, u32[]{:S(2)}) copy-start(f32[192,768]{1,0:T(8,128)} %get-tuple-element.67) | copy-start | bytes 1769476

commit v3 on v2

v3 whole, which is shorter than its diff:
```python
import functools

import jax
import jax.numpy as jnp
from jax import lax
from jax.experimental import pallas as pl
from jax.experimental.pallas import tpu as pltpu
from jax.sharding import PartitionSpec as P

HEADS = 12
HEAD = 64

EPS = 1e-06
NEG = -1e30
HIGHEST = lax.Precision.HIGHEST
MESH = pl.DeviceIdType.MESH
BF = jnp.bfloat16
F32 = jnp.float32


class Place:
    def __init__(self):
        self.nz, self.ns, self.ny = (lax.axis_size(a) for a in ("dp", "seq", "expert"))
        self.nx = self.ns // 2
        self.z, self.s, self.y = (lax.axis_index(a) for a in ("dp", "seq", "expert"))
        self.x, self.c = self.s // 2, lax.rem(self.s, 2)

    def device(self, z=None, x=None, c=None, y=None):
        z = self.z if z is None else z
        x = self.x if x is None else x
        c = self.c if c is None else c
        y = self.y if y is None else y
        return (z, x * 2 + c, y)

    def other_x(self):
        return [lax.rem(self.x + k, self.nx) for k in range(1, self.nx)]

    def other_y(self):
        return [lax.rem(self.y + k, self.ny) for k in range(1, self.ny)]

    def by_distance(self, k):
        order = [sorted(range(self.nz), key=lambda d: (abs(d - z), d)) for z in range(self.nz)]
        return self.pick([row[k] for row in order])

    def pick(self, values):
        out = jnp.int32(values[0])
        for z in range(1, self.nz):
            out = jnp.where(self.z == z, jnp.int32(values[z]), out)
        return out

    def greet(self):
        barrier = pltpu.get_barrier_semaphore()
        for x in self.other_x():
            pl.semaphore_signal(barrier, inc=1, device_id=self.device(x=x), device_id_type=MESH)
        for y in self.other_y():
            pl.semaphore_signal(barrier, inc=1, device_id=self.device(y=y), device_id_type=MESH)
        pl.semaphore_signal(barrier, inc=1, device_id=self.device(c=1 - self.c), device_id_type=MESH)

        for k in range(1, self.nz):
            z = lax.rem(self.z + k, self.nz)
            pl.semaphore_signal(barrier, inc=1, device_id=self.device(z=z), device_id_type=MESH)
        pl.semaphore_wait(barrier, self.nx - 1 + self.ny - 1 + 1 + self.nz - 1)


def rms_rows(src, gain, dst, rows, step=64):
    @pl.loop(0, rows // step)
    def _(i):
        at = pl.ds(pl.multiple_of(i * step, step), step)
        value = src[at, :].astype(F32)
        r = lax.rsqrt(jnp.mean(value * value, axis=-1, keepdims=True) + EPS)
        dst[at, :] = (value * r * gain).astype(BF)


def block(weight, index, lanes=slice(None), share=(0, 1)):
    unit, width = weight.shape[-2:]
    count = width // unit // share[1]
    first = pl.multiple_of(index * (width // unit) + share[0] * count, count)
    value = weight[pl.ds(first, count), :, lanes]
    return value.reshape(count * unit, value.shape[-1])


def project(left, weight, index, dst):
    width = dst.shape[-1]
    step = 256 if width % 256 == 0 else width

    @pl.loop(0, width // step)
    def _(j):
        at = pl.ds(pl.multiple_of(j * step, step), step)
        dst[:, at] = jnp.dot(left[...], block(weight, index, at), preferred_element_type=F32).astype(dst.dtype)


def prepare_bias(rel, table, bias, rank, rows, group):
    buckets, heads = table.shape
    wide = group + 128
    lane = lax.broadcasted_iota(jnp.int32, (group, wide), 1)
    shift = jnp.where(lane < group, lane, lane - wide)
    distance = jnp.clip(rank * rows - shift, 0, group - 1)
    hot = (lax.broadcasted_iota(jnp.int32, (group, wide), 0) == distance).astype(F32).astype(BF)
    which = jnp.dot(jnp.broadcast_to(rel[...].astype(F32), (8, group)).astype(BF), hot, preferred_element_type=F32)
    picks = (lax.broadcasted_iota(jnp.int32, (buckets, wide), 0) == which[0:1].astype(jnp.int32)).astype(F32)
    line = lax.dot_general(table[...], picks, (((0,), (0,)), ((), ())), precision=HIGHEST, preferred_element_type=F32)
    for h in range(heads):
        band = pltpu.roll(jnp.broadcast_to(line[h : h + 1], (rows, wide)), 0, 1, stride=1, stride_axis=0)
        bias[h // 2, pl.ds((h % 2) * rows, rows), :] = band[:, :group]


def prepare_masks(lengths, same, causal, rank, rows, group):
    key = lax.broadcasted_iota(jnp.int32, (rows, group), 1)
    query = rank * rows + lax.broadcasted_iota(jnp.int32, (rows, group), 0)
    for p in range(same.shape[0]):
        end = jnp.int32(0)
        kd = jnp.zeros((rows, group), jnp.int32)
        qd = jnp.zeros((rows, group), jnp.int32)
        for n in range(lengths.shape[1]):
            end = end + lengths[p, n]
            kd = kd + jnp.where(key >= end, 1, 0)
            qd = qd + jnp.where(query >= end, 1, 0)
        same[p] = jnp.where(kd == qd, 0.0, NEG)
        causal[p] = jnp.where((kd == qd) & (key <= query), 0.0, NEG)


def two_heads(pair):
    first = lax.broadcasted_iota(jnp.int32, pair.shape, 1) < HEAD
    zero = jnp.zeros_like(pair)
    return jnp.concatenate([jnp.where(first, pair, zero), jnp.where(first, zero, pair)], axis=0)


def one_pair(stacked):
    rows = stacked.shape[0] // 2
    first = lax.broadcasted_iota(jnp.int32, (rows, stacked.shape[1]), 1) < HEAD
    return jnp.where(first, stacked[:rows], stacked[rows:])


def attend_pairs(query, keys, values, bias, mask, chances, mixed):
    packs, pairs, double, group = chances.shape
    rows = double // 2

    def body(i, carry):
        p, j = i // pairs, lax.rem(i, pairs)
        mine = pl.ds(pl.multiple_of(p * rows, rows), rows)
        theirs = pl.ds(pl.multiple_of(p * group, group), group)
        lanes = pl.ds(pl.multiple_of(j * 128, 128), 128)
        scores = lax.dot_general(
            two_heads(query[mine, lanes]), keys[theirs, lanes], (((1,), (1,)), ((), ())), preferred_element_type=F32
        )
        scores = scores * HEAD**-0.5
        if bias is not None:
            scores = scores + bias[j]
        scores = (scores.reshape(2, rows, group) + mask[p][None]).reshape(double, group)
        raised = jnp.exp(scores - jnp.max(scores, axis=1, keepdims=True))
        weights = (raised * (1.0 / jnp.sum(raised, axis=1, keepdims=True))).astype(BF)
        chances[p, j] = weights
        out = jnp.dot(weights, values[theirs, lanes], preferred_element_type=F32)
        mixed[mine, lanes] = one_pair(out).astype(BF)
        return carry

    lax.fori_loop(0, packs * pairs, body, 0, unroll=2)


def add_product(total, left, weight, index):
    width = total.shape[-1]
    step = 256 if width % 256 == 0 else width

    @pl.loop(0, width // step)
    def _(j):
        at = pl.ds(pl.multiple_of(j * step, step), step)
        total[:, at] += jnp.dot(left[...], block(weight, index, at), preferred_element_type=F32)


def product_t(left, weight, index, dst):
    halves = 2
    step = weight.shape[-1] // halves

    @pl.loop(0, halves)
    def _(j):
        rows = block(weight, index, share=(j, halves))
        out = lax.dot_general(left[...], rows, (((1,), (1,)), ((), ())), preferred_element_type=F32)
        dst[:, pl.ds(pl.multiple_of(j * step, step), step)] = out.astype(dst.dtype)


def two_products_t(left1, index1, left2, index2, weight, dst):
    halves = 2
    step = weight.shape[-1] // halves

    @pl.loop(0, halves)
    def _(j):
        out = 0.0
        for left, index in ((left1, index1), (left2, index2)):
            rows = block(weight, index, share=(j, halves))
            out = out + lax.dot_general(left[...], rows, (((1,), (1,)), ((), ())), preferred_element_type=F32)
        dst[:, pl.ds(pl.multiple_of(j * step, step), step)] = out.astype(dst.dtype)


def outer_product(left, right, dst, index):
    unit, width = dst.shape[-2:]
    halves = 2
    step, count = width // halves, width // unit // halves

    @pl.loop(0, halves)
    def _(j):
        part = left[:, pl.ds(pl.multiple_of(j * step, step), step)]
        out = lax.dot_general(part, right[...], (((0,), (0,)), ((), ())), preferred_element_type=F32)
        first = index * (width // unit) + j * count
        dst[pl.ds(first, count)] = out.astype(dst.dtype).reshape(count, unit, width)


def add_into(total, other):
    lead = total.shape[:-2]
    count = 1
    for n in lead:
        count *= n
    rows = total.shape[-2]
    step = next(n for n in ((48, 32, 16) if total.shape[-1] <= 1024 else (16,)) if rows % n == 0)

    def body(i, carry):
        index = []
        rest = i // (rows // step)
        for n in reversed(lead):
            index.insert(0, lax.rem(rest, n))
            rest = rest // n
        r = pl.ds(pl.multiple_of(lax.rem(i, rows // step) * step, 16), step)
        at = (*index, r)
        total[at] = (total[at].astype(F32) + other[at].astype(F32)).astype(total.dtype)
        return carry

    lax.fori_loop(0, count * (rows // step), body, 0)


def norm_back_rows(value, gain, grad, total, gain_grad, step=64):
    gain_grad[...] = jnp.zeros_like(gain_grad)

    @pl.loop(0, value.shape[0] // step)
    def _(i):
        at = pl.ds(pl.multiple_of(i * step, step), step)
        v, g = value[at, :].astype(F32), grad[at, :]
        r = lax.rsqrt(jnp.mean(v * v, axis=-1, keepdims=True) + EPS)
        scaled = g * gain
        total[at, :] += r * scaled - v * (r * r * r) * jnp.mean(scaled * v, axis=-1, keepdims=True)
        gain_grad[...] += jnp.sum(g * v * r, axis=0, keepdims=True)


def attend_pairs_back(query, keys, values, chances, grad, grad_q, grad_k, grad_v, diagonal):
    packs, pairs, double, group = chances.shape
    rows = double // 2
    scale = HEAD**-0.5

    def body(i, carry):
        p, j = i // pairs, lax.rem(i, pairs)
        mine = pl.ds(pl.multiple_of(p * rows, rows), rows)
        theirs = pl.ds(pl.multiple_of(p * group, group), group)
        lanes = pl.ds(pl.multiple_of(j * 128, 128), 128)
        ga = two_heads(grad[mine, lanes])
        low = chances[p, j]
        wide = low.astype(F32)
        gp = lax.dot_general(ga, values[theirs, lanes], (((1,), (1,)), ((), ())), preferred_element_type=F32)
        gs = (wide * (gp - jnp.sum(wide * gp, axis=1, keepdims=True))).astype(BF)
        gq = jnp.dot(gs, keys[theirs, lanes], preferred_element_type=F32)
        grad_q[mine, lanes] = (one_pair(gq) * scale).astype(BF)
        gk = lax.dot_general(gs, two_heads(query[mine, lanes]), (((0,), (0,)), ((), ())), preferred_element_type=F32)
        grad_k[theirs, lanes] = (gk * scale).astype(BF)
        gv = lax.dot_general(low, ga, (((0,), (0,)), ((), ())), preferred_element_type=F32)
        grad_v[theirs, lanes] = gv.astype(BF)
        if diagonal is not None:
            a = lax.broadcasted_iota(jnp.int32, (rows, rows), 0)
            b = lax.broadcasted_iota(jnp.int32, (rows, rows), 1)
            flip = (a + b == rows - 1).astype(F32).astype(BF)
            for half in range(2):
                turned = jnp.dot(flip, gs[half * rows : (half + 1) * rows], preferred_element_type=F32)
                turned = jnp.concatenate([turned, jnp.zeros((rows, 128), F32)], axis=1)
                band = pltpu.roll(turned, 0, 1, stride=1, stride_axis=0)
                diagonal[pl.ds(2 * j + half, 1), :] += jnp.sum(band, axis=0, keepdims=True)
        return carry

    lax.fori_loop(0, packs * pairs, body, 0, unroll=2)


def table_grad(rel, diagonal, rank, rows, group, buckets):
    wide = group + 128
    lane = lax.broadcasted_iota(jnp.int32, (group, wide), 1)
    distance = jnp.clip(rank * rows + rows - 1 - lane, 0, group - 1)
    hot = (lax.broadcasted_iota(jnp.int32, (group, wide), 0) == distance).astype(F32).astype(BF)
    which = jnp.dot(jnp.broadcast_to(rel[...].astype(F32), (8, group)).astype(BF), hot, preferred_element_type=F32)
    picks = (lax.broadcasted_iota(jnp.int32, (buckets, wide), 0) == which[0:1].astype(jnp.int32)).astype(F32)
    return lax.dot_general(picks, diagonal[...], (((1,), (1,)), ((), ())), precision=HIGHEST, preferred_element_type=F32)


def route_slots(route, packs, experts, capacity):
    count = route.shape[0]
    hot = (route[...] == lax.broadcasted_iota(jnp.int32, (count, experts), 1)).astype(F32)
    a = lax.broadcasted_iota(jnp.int32, (count, count), 0)
    b = lax.broadcasted_iota(jnp.int32, (count, count), 1)
    rows = count // packs
    earlier = ((b < a) & (a // rows == b // rows)).astype(F32).astype(BF)
    before = jnp.dot(earlier, hot.astype(BF), preferred_element_type=F32)
    slot = jnp.sum(before * hot, axis=1, keepdims=True).astype(jnp.int32)
    pack = lax.broadcasted_iota(jnp.int32, (count, 1), 0) // rows
    target = jnp.where(slot < capacity, (route[...] * packs + pack) * capacity + slot, -1)
    slots = lax.broadcasted_iota(jnp.int32, (count, experts * packs * capacity), 1)
    return hot, (target == slots).astype(F32).astype(BF)


def gelu_both(z):
    c = 0.7978845608028654
    t = jnp.tanh(c * (z + 0.044715 * (z * z * z)))
    half = 0.5 * (1.0 + t)
    slope = half + 0.5 * z * (1.0 - t * t) * (c * (1.0 + 3 * 0.044715 * (z * z)))
    return z * half, slope


def layer_body(lengths, rel, gains, table, router_t, route, x_ref, m_ref, g_ref, ain, aout, ein, eout,
               out_rows, o0, o1, o2, o3, grad_x, grad_mem, sum_wide, sum_table,
               w, big, ge, c2, c3, y0, y1, x0, x1, x2, x3, z0, z1, z2, z3,
               xo, mo, n1_all, k_, v, kc, vc, gv, n1, q, mixed, n2, qc, cross_mixed, n3, gb, ga, gq,
               pr_self, pr_cross, h1, h2, gn, bias, same, causal, diagonal, gain_row,
               act_core, act_x, wide_sum, table_sum, wide_in, table_in,
               slots_out, slots_in, slots_acc, back_in, hid, gin_,
               act_send, act_recv, line_send, side_send, spread_send, ici_recv, spread_recv, own_sem,
               core_send, core_recv, y_send, y_recv, x_send, x_recv, z_send, z_recv,
               sum_send, sum_recv, small_send, small_recv, swap_send, swap_recv, free_sem):
    at = Place()
    nz, nx, ny = at.nz, at.nx, at.ny
    packs, tok, width = x_ref.shape
    group = xo.shape[0] // packs
    experts = router_t.shape[0]
    unit = ain.shape[1]
    panels = eout.shape[0]
    buckets = table.shape[0]
    gk = xo
    units = (ain.shape[0], aout.shape[0], panels, panels)
    tall = nz * nx * 2
    bases = (0, tall * ny * units[0], 0, tall * panels)
    dense, e_in, e_out = (0, 1), 2, 3
    experts_ = (e_in, e_out)
    waits = []

    def remote(src, dst, ssem, rsem, **where):
        return pltpu.make_async_remote_copy(
            src_ref=src, dst_ref=dst, send_sem=ssem, recv_sem=rsem,
            device_id=at.device(**where), device_id_type=MESH,
        )

    def send(*args, **where):
        one = remote(*args, **where)
        one.start()
        waits.append(one.wait_send)
        return one

    def arrive(ref, sem):
        pltpu.make_async_copy(ref, ref, sem).wait()

    def spot(a, z, x, c, y):
        index = (z * nx + x) * 2 + c
        index = index * ny + y if a in dense else index
        return (w if a in dense else big).at[pl.ds(bases[a] + index * units[a], units[a])]

    shards = {0: ain, 1: aout, 3: eout}
    acts = ((x_ref, xo), (m_ref, mo))

    at.greet()

    def act_rows(full, p, x, c):
        return full.at[pl.ds(pl.multiple_of(p * group + (x * 2 + c) * tok, 16), tok)]

    own_waits = []
    for i, (src, full) in enumerate(acts):
        for p in range(packs):
            dst = act_rows(full, p, at.x, at.c)
            for k, x in enumerate(at.other_x()):
                send(src.at[p], dst, act_send.at[i, p, k], act_recv.at[i, p, at.x, at.c], x=x)
            send(src.at[p], dst, act_send.at[i, p, nx - 1 + at.x], act_recv.at[i, p, at.x, at.c], c=1 - at.c)
            own = pltpu.make_async_copy(src.at[p], dst, own_sem.at[4 + i, p])
            own.start()
            own_waits.append(own.wait)

    def along_line(a, z, src):
        dst = spot(a, z, at.x, at.c, at.y)
        sem = ici_recv.at[a, z, at.x, at.y]
        left = (z >= at.z) & (at.z > 0)
        right = (z <= at.z) & (at.z < nz - 1)

        def one(side):
            return remote(src, dst, line_send.at[a, z, side], sem, z=at.z + 2 * side - 1)

        @pl.when(left)
        def _():
            one(0).start()

        @pl.when(right)
        def _():
            one(1).start()

        def wait():
            @pl.when(left)
            def _():
                one(0).wait_send()

            @pl.when(right)
            def _():
                one(1).wait_send()

        waits.append(wait)

    def to_sides(a, z, src):
        dst = spot(a, z, at.x, at.c, at.y)
        for k, x in enumerate(at.other_x()):
            send(src, dst, side_send.at[a, z, k], ici_recv.at[a, z, at.x, at.y], x=x)
        if a in dense:
            for k, y in enumerate(at.other_y()):
                send(src, dst, side_send.at[a, z, nx - 1 + k], ici_recv.at[a, z, at.x, at.y], y=y)

    def to_core(a, z, x, y, src):
        send(src, spot(a, z, x, at.c, y), spread_send.at[a, z, x, y], spread_recv.at[a, z, x, y], c=1 - at.c)

    zs = [at.by_distance(k) for k in range(nz)]
    for a in dense:
        along_line(a, at.z, shards[a])
    own_ein = spot(e_in, at.z, at.x, at.c, at.y)
    first = bases[e_in] + ((at.z * nx + at.x) * 2 + at.c) * panels
    for f in range(panels):
        big[first + f] = ein[:, f * width : (f + 1) * width]
    shards[2] = own_ein
    for a in experts_:
        along_line(a, at.z, shards[a])

    def shard_events(kind, k):
        for a in kind:
            here = spot(a, zs[k], at.x, at.c, at.y)
            if k:
                arrive(here, ici_recv.at[a, zs[k], at.x, at.y])
                along_line(a, zs[k], here)
            elif a != e_in:
                own = pltpu.make_async_copy(shards[a], here, own_sem.at[a, 0])
                own.start()
                own_waits.append(own.wait)
            src = here if k else shards[a]
            to_sides(a, zs[k], src)
            to_core(a, zs[k], at.x, at.y, src)

    for k in range(nz):
        shard_events(dense, k)
        if k == 0:
            for i, (src, full) in enumerate(acts):
                for p in range(packs):
                    for x in at.other_x():
                        dst = act_rows(full, p, x, at.c)
                        arrive(dst, act_recv.at[i, p, x, at.c])
                        send(dst, dst, act_send.at[i, p, nx - 1 + x], act_recv.at[i, p, x, at.c], c=1 - at.c)

    def diagonal_events(k):
        for a in dense:
            for x in at.other_x():
                here = spot(a, zs[k], x, at.c, at.y)
                arrive(here, ici_recv.at[a, zs[k], x, at.y])
                for j, y in enumerate(at.other_y()):
                    send(here, here, side_send.at[a, zs[k], nx - 1 + ny - 1 + j + (ny - 1) * x],
                         ici_recv.at[a, zs[k], x, at.y], y=y)
                to_core(a, zs[k], x, at.y, here)

    for k in range(nz):
        shard_events(experts_, k)
        diagonal_events(k)

    prepare_bias(rel, table, bias, at.s, tok, group)
    prepare_masks(lengths, same, causal, at.s, tok, group)
    for i, (src, full) in enumerate(acts):
        for p in range(packs):
            for x in range(nx):
                arrive(act_rows(full, p, x, 1 - at.c), act_recv.at[i, p, x, 1 - at.c])
    for wait in own_waits:
        wait()
    rms_rows(xo, gains[0:1], n1_all, packs * group)
    for p in range(packs):
        h1[pl.ds(p * tok, tok), :] = x_ref[p].astype(F32)
        n1[pl.ds(p * tok, tok), :] = n1_all[pl.ds(pl.multiple_of(p * group + at.s * tok, tok), tok), :]
    for k in range(nz):
        for a in dense:
            for y in at.other_y():
                for x in range(nx):
                    here = spot(a, zs[k], x, at.c, y)
                    arrive(here, ici_recv.at[a, zs[k], x, y])
                    to_core(a, zs[k], x, y, here)
    for a in dense:
        for z in range(nz):
            for x in range(nx):
                for y in range(ny):
                    arrive(spot(a, z, x, 1 - at.c, y), spread_recv.at[a, z, x, y])

    project(n1, w, 0, q)
    project(n1_all, w, 1, k_)
    project(n1_all, w, 2, v)
    project(mo, w, 4, kc)
    project(mo, w, 5, vc)
    attend_pairs(q, k_, v, bias, causal, pr_self, mixed)
    add_product(h1, mixed, w, 6)
    rms_rows(h1, gains[1:2], n2, packs * tok)
    project(n2, w, 3, qc)
    attend_pairs(qc, kc, vc, None, same, pr_cross, cross_mixed)
    h2[...] = h1[...]
    add_product(h2, cross_mixed, w, 7)
    rms_rows(h2, gains[2:3], n3, packs * tok)

    each = slots_in.shape[2]
    hot, dispatch = route_slots(route, packs, experts, each // packs)
    logits = lax.dot_general(n3[...], router_t[...].astype(BF), (((1,), (1,)), ((), ())), preferred_element_type=F32)
    raised = jnp.exp(logits - jnp.max(logits, axis=1, keepdims=True))
    routing = raised / jnp.sum(raised, axis=1, keepdims=True)
    gate = jnp.sum(routing * hot, axis=1, keepdims=True)
    top = g_ref[...].astype(F32).reshape(packs * tok, width)

    def by_slot(rows):
        out = lax.dot_general(dispatch, rows, (((0,), (0,)), ((), ())), preferred_element_type=F32)
        return out.astype(BF).reshape(ny, each, width)

    def swap(t, source, target):
        for j, y in enumerate(at.other_y()):
            one = remote(source.at[t % 2, y], target.at[t % 2, at.y], swap_send.at[t, j], swap_recv.at[t, ny - 2 - j], y=y)
            one.start()
            (waits if t >= 2 else swap_waits).append(one.wait_send)

    swap_waits = []

    def swapped(t, target):
        for j, y in enumerate(at.other_y()):
            arrive(target.at[t % 2, y], swap_recv.at[t, j])

    slots_out[0] = by_slot(n3[...])
    swap(0, slots_out, slots_in)
    slots_out[1] = by_slot((gate * top).astype(BF))
    swap(1, slots_out, slots_in)
    for t in range(2):
        slots_in[t, at.y] = slots_out[t, at.y]

    for k in range(nz):
        for a in experts_:
            for x in at.other_x():
                here = spot(a, zs[k], x, at.c, at.y)
                arrive(here, ici_recv.at[a, zs[k], x, at.y])
                to_core(a, zs[k], x, at.y, here)
    for a in experts_:
        for z in range(nz):
            for x in range(nx):
                arrive(spot(a, z, x, 1 - at.c, at.y), spread_recv.at[a, z, x, at.y])
    for t in range(2):
        swapped(t, slots_in)
    for wait in waits:
        wait()
    waits.clear()

    cores, ys, xs, zs_ = {2: c2, 3: c3}, (y0, y1), (x0, x1, x2, x3), (z0, z1, z2, z3)
    outs = (o0, o1, o2, o3)
    far = [sorted(range(nz), key=lambda d: (-abs(d - z), d)) for z in range(nz)]
    order_e = [at.pick([far[z][k] for z in range(nz)]) for k in range(nz)]
    halves = [[d for d in row if d >= nz // 2] + [d for d in row if d < nz // 2] for row in far]
    order_d = [at.pick([halves[z][k] for z in range(nz)]) for k in range(nz)]
    e_waits = []

    def expert_part(a, d, x, c):
        return ge.at[pl.ds(bases[a] + ((d * nx + x) * 2 + c) * panels, panels)]

    def start_expert(a, k):
        for x in range(nx):
            one = remote(expert_part(a, order_e[k], x, 1 - at.c), cores[a].at[k, x], core_send.at[a, k, x],
                         core_recv.at[a, k, x], c=1 - at.c)
            one.start()
            e_waits.append(one.wait_send)

    def core_expert(a, k):
        for x in range(nx):
            arrive(cores[a].at[k, x], core_recv.at[a, k, x])
            add_into(cores[a].at[k, x], expert_part(a, order_e[k], x, at.c))
        for j, x in enumerate(at.other_x()):
            send(cores[a].at[k, x], xs[a].at[k, nx - 2 - j], x_send.at[a, k, j], x_recv.at[a, k, nx - 2 - j], x=x)

    def free_experts():
        for wait in e_waits:
            wait()
        pl.semaphore_signal(free_sem, inc=1, device_id=at.device(c=1 - at.c), device_id_type=MESH)

    def dense_part(a, d, x, c):
        return big.at[pl.ds(bases[a] + ((d * nx + x) * 2 + c) * ny * units[a], ny * units[a])]

    def dense_core(a, k, x, y=None):
        first = bases[a] // 2 + (k * nx + x) * ny * units[a]
        if y is None:
            return ge.at[pl.ds(first, ny * units[a])]
        return ge.at[pl.ds(first + y * units[a], units[a])]

    def start_dense(k):
        for a in dense:
            for x in range(nx):
                send(dense_part(a, order_d[k], x, 1 - at.c), dense_core(a, k, x), core_send.at[a, k, x],
                     core_recv.at[a, k, x], c=1 - at.c)

    def core_dense(k):
        for a in dense:
            for x in range(nx):
                arrive(dense_core(a, k, x), core_recv.at[a, k, x])
                add_into(dense_core(a, k, x), dense_part(a, order_d[k], x, at.c))
                for j, y in enumerate(at.other_y()):
                    send(dense_core(a, k, x, y), ys[a].at[k, ny - 2 - j, x],
                         y_send.at[a, k, j, x], y_recv.at[a, k, ny - 2 - j, x], y=y)

    def y_dense(k):
        for a in dense:
            for x in range(nx):
                for j in range(ny - 1):
                    arrive(ys[a].at[k, j, x], y_recv.at[a, k, j, x])
                    add_into(ys[a].at[k, 0, x], ys[a].at[k, j, x] if j else dense_core(a, k, x, at.y))
            for j, x in enumerate(at.other_x()):
                send(ys[a].at[k, 0, x], xs[a].at[k, nx - 2 - j], x_send.at[a, k, j], x_recv.at[a, k, nx - 2 - j], x=x)

    def write_out(a, total):
        value = total[...].astype(F32)
        if a == e_in:
            for f in range(panels):
                outs[a][:, f * width : (f + 1) * width] = value[f]
        else:
            outs[a][...] = value.reshape(outs[a].shape)

    def x_and_line(kind, k):
        for a in kind:
            d = (order_d if a in dense else order_e)[k]
            total = xs[a].at[k, 0]
            for j in range(nx - 1):
                arrive(xs[a].at[k, j], x_recv.at[a, k, j])
                own = ys[a].at[k, 0, at.x] if a in dense else cores[a].at[k, at.x]
                add_into(total, xs[a].at[k, j] if j else own)
            for side in range(2):
                feeds = (at.z > 0) & (d >= at.z) if side == 0 else (at.z < nz - 1) & (d <= at.z)
                slot = d if side == 0 else jnp.where(d == at.z, nz, d)

                @pl.when(feeds)
                def _(a=a, slot=slot, total=total):
                    arrive(zs_[a].at[slot], z_recv.at[a, slot])
                    add_into(total, zs_[a].at[slot])

            def hop(to, a=a, total=total, d=d):
                slot = d if to > 0 else jnp.where(d == at.z - 1, nz, d)
                return remote(total, zs_[a].at[slot], z_send.at[a, k], z_recv.at[a, slot], z=at.z + to)

            @pl.when(d < at.z)
            def _(hop=hop):
                hop(-1).start()

            @pl.when(d > at.z)
            def _(hop=hop):
                hop(1).start()

            @pl.when(d == at.z)
            def _(a=a, total=total):
                write_out(a, total)

            def wait(hop=hop, d=d):
                @pl.when(d < at.z)
                def _():
                    hop(-1).wait_send()

                @pl.when(d > at.z)
                def _():
                    hop(1).wait_send()

            waits.append(wait)

    def start_act(i):
        for p in range(packs):
            for x in range(nx):
                send(act_rows((kc, k_)[i], p, x, 1 - at.c), act_core.at[i, p, x], sum_send.at[i, p, x],
                     sum_recv.at[i, p, x], c=1 - at.c)

    def core_act(i):
        for p in range(packs):
            for x in range(nx):
                arrive(act_core.at[i, p, x], sum_recv.at[i, p, x])
                add_into(act_core.at[i, p, x], act_rows((kc, k_)[i], p, x, at.c))
        for j, x in enumerate(at.other_x()):
            send(act_core.at[i, :, x], act_x.at[i, nx - 2 - j], sum_send.at[i, packs, j], sum_recv.at[i, packs, nx - 2 - j], x=x)

    def x_act(i):
        for j in range(nx - 1):
            arrive(act_x.at[i, j], sum_recv.at[i, packs, j])
        for p in range(packs):
            out = act_core[i, p, at.x].astype(F32)
            for j in range(nx - 1):
                out = out + act_x[i, j, p].astype(F32)
            if i == 0:
                grad_mem[pl.ds(p * tok, tok), :] = out
            else:
                gn[pl.ds(p * tok, tok), :] += out

    pair_sums = ((wide_sum, wide_in), (table_sum, table_in))
    stages = [("c", [1 - at.c]), ("y", at.other_y()), ("x", at.other_x())]

    def start_small(t):
        axis, peers = stages[t]
        base = [0, 1, ny][t]
        for i, (total, inbox) in enumerate(pair_sums):
            for j, peer in enumerate(peers):
                back = base + len(peers) - 1 - j
                send(total.at[t], inbox.at[back], small_send.at[i, base + j], small_recv.at[i, back], **{axis: peer})

    def end_small(t):
        axis, peers = stages[t]
        base = [0, 1, ny][t]
        for i, (total, inbox) in enumerate(pair_sums):
            out = total[t]
            for j in range(len(peers)):
                arrive(inbox.at[base + j], small_recv.at[i, base + j])
                out = out + inbox[base + j]
            total[t + 1] = out

    tail = ny + nx - 1

    def start_line():
        for i, (total, inbox) in enumerate(pair_sums):
            for j in range(1, nz):
                z = lax.rem(at.z + j, nz)
                send(total.at[3], inbox.at[tail + at.z], small_send.at[i, tail + j], small_recv.at[i, tail + at.z], z=z)

    def end_line():
        for i, (total, inbox) in enumerate(pair_sums):
            for j in range(1, nz):
                z = lax.rem(at.z + j, nz)
                arrive(inbox.at[tail + z], small_recv.at[i, tail + z])
            out = None
            for z in range(nz):
                term = jnp.where(at.z == z, total[3], inbox[tail + z])
                out = term if out is None else out + term
            (sum_wide, sum_table)[i][...] = out

    count = ny * each
    row_units = width // unit
    for k in range(nz):
        f = order_e[k]
        here = slots_in[0].reshape(count, width)
        grad_here = slots_in[1].reshape(count, width)

        def in_rows(start, n, f=f):
            return jnp.concatenate([big[(start + i) * panels + f] for i in range(n)], axis=0)

        first_out = bases[e_out] + f * row_units
        inner = jnp.dot(here, in_rows(0, row_units), preferred_element_type=F32)
        hidden, slope = gelu_both(inner)
        hid[...] = hidden.astype(BF)
        out_panel = big[pl.ds(first_out, row_units)].reshape(width, width)
        grad_hidden = lax.dot_general(grad_here, out_panel, (((1,), (1,)), ((), ())), preferred_element_type=F32)
        gin_[...] = (grad_hidden * slope).astype(BF)
        result = jnp.dot(hid[...], out_panel, preferred_element_type=F32)
        grad_slots = lax.dot_general(gin_[...], in_rows(0, row_units), (((1,), (1,)), ((), ())), preferred_element_type=F32)
        if k:
            slots_acc[0] += result
            slots_acc[1] += grad_slots
        else:
            slots_acc[0] = result
            slots_acc[1] = grad_slots
        grad = lax.dot_general(hid[...], grad_here, (((0,), (0,)), ((), ())), preferred_element_type=F32).astype(BF)
        ge[pl.ds(first_out, row_units)] = grad.reshape(row_units, unit, width)
        start_expert(e_out, k)
        grad = lax.dot_general(here, gin_[...], (((0,), (0,)), ((), ())), preferred_element_type=F32).astype(BF)
        for i in range(row_units):
            ge[i * panels + f] = grad[i * unit : (i + 1) * unit]
        if k:
            core_expert(e_out, k - 1)
    for wait in swap_waits:
        wait()
    for t in range(2):
        slots_out[t] = slots_acc[t].astype(BF).reshape(ny, each, width)
        swap(2 + t, slots_out, back_in)
    for k in range(nz):
        start_expert(e_in, k)
    core_expert(e_out, nz - 1)
    core_expert(e_in, 0)
    for t in range(2):
        swapped(2 + t, back_in)
        back_in[t, at.y] = slots_out[t, at.y]
    combined = jnp.dot(dispatch, back_in[0].reshape(count, width), preferred_element_type=F32)
    rows_out = (h2[...] + gate * combined).astype(BF)
    for p in range(packs):
        out_rows[p] = rows_out[p * tok : (p + 1) * tok]
    grad_gate = jnp.sum(top * combined, axis=1, keepdims=True)
    grad_logits = grad_gate * routing * (hot - gate)
    diagonal[...] = jnp.zeros_like(diagonal)
    for i, (_, inbox) in enumerate(pair_sums):
        inbox[pl.ds(tail + at.z, 1)] = jnp.zeros_like(inbox[pl.ds(0, 1)])
    wide_sum[0] = jnp.zeros_like(wide_sum[0])
    wide_sum[0, pl.ds(3, experts), :] = lax.dot_general(
        grad_logits, n3[...].astype(F32), (((0,), (0,)), ((), ())), precision=HIGHEST, preferred_element_type=F32
    )
    grad_n3 = jnp.dot(dispatch, back_in[1].reshape(count, width), preferred_element_type=F32)
    for e in range(experts):
        grad_n3 = grad_n3 + grad_logits[:, e : e + 1] * router_t[e : e + 1, :]
    gn[...] = grad_n3
    grad_x[...] = top
    norm_back_rows(h2, gains[2:3], gn, grad_x, gain_row)
    wide_sum[0, 2:3, :] = gain_row[...]
    gb[...] = grad_x[...].astype(BF)

    product_t(gb, w, 7, ga)
    core_expert(e_in, 1)
    core_expert(e_in, 2)
    core_expert(e_in, 3)
    free_experts()
    outer_product(cross_mixed, gb, big, 7)
    x_and_line((e_out,), 0)
    attend_pairs_back(qc, kc, vc, pr_cross, ga, gq, gk, gv, None)
    outer_product(n2, gq, big, 3)
    outer_product(mo, gk, big, 4)
    outer_product(mo, gv, big, 5)
    pl.semaphore_wait(free_sem, 1)
    for k in range(nz // 2):
        start_dense(k)
    x_and_line((e_out,), 1)
    two_products_t(gk, 4, gv, 5, w, kc)
    start_act(0)
    product_t(gq, w, 3, gn)
    norm_back_rows(h1, gains[1:2], gn, grad_x, gain_row)
    wide_sum[0, 1:2, :] = gain_row[...]
    gb[...] = grad_x[...].astype(BF)
    product_t(gb, w, 6, ga)
    core_dense(0)
    x_and_line((e_out,), 2)
    outer_product(mixed, gb, big, 6)
    core_act(0)
    core_dense(1)
    x_and_line((e_out,), 3)
    attend_pairs_back(q, k_, v, pr_self, ga, gq, gk, gv, diagonal)
    x_and_line((e_in,), 0)
    outer_product(n1, gq, big, 0)
    outer_product(n1_all, gk, big, 1)
    outer_product(n1_all, gv, big, 2)
    for k in range(nz // 2, nz):
        start_dense(k)
    y_dense(0)
    two_products_t(gk, 1, gv, 2, w, k_)
    start_act(1)
    x_and_line((e_in,), 1)
    y_dense(1)
    for k in range(nz // 2, nz):
        core_dense(k)
    core_act(1)
    product_t(gq, w, 0, gn)
    table_sum[0] = table_grad(rel, diagonal, at.s, tok, group, buckets)
    x_and_line((e_in,), 2)
    x_and_line((e_in,), 3)
    x_act(0)
    x_and_line(dense, 0)
    x_act(1)
    for p in range(packs):
        h1[pl.ds(p * tok, tok), :] = x_ref[p].astype(F32)
    norm_back_rows(h1, gains[0:1], gn, grad_x, gain_row)
    wide_sum[0, 0:1, :] = gain_row[...]
    start_small(0)
    y_dense(2)
    end_small(0)
    start_small(1)
    x_and_line(dense, 1)
    end_small(1)
    start_small(2)
    y_dense(3)
    end_small(2)
    start_line()
    x_and_line(dense, 2)
    end_line()
    x_and_line(dense, 3)
    for wait in waits:
        wait()


def shapes_of(layer_input, routes, attn_in, attn_out, expert_in, expert_out):
    nz, ns, ny = (lax.axis_size(a) for a in ("dp", "seq", "expert"))
    packs, tok, width = layer_input.shape[0], layer_input.shape[3], layer_input.shape[4]
    return nz, ns, ny, packs, tok, width


def fits_kernel(layer_input, routes, attn_in, attn_out, expert_in, expert_out):
    nz, ns, ny, packs, tok, width = shapes_of(layer_input, routes, attn_in, attn_out, expert_in, expert_out)
    unit, hidden = expert_in.shape[1:]
    capacity = (5 * tok + 4 * ny - 1) // (4 * ny)
    return (
        unit % 16 == 0
        and tok % 16 == 0
        and packs * capacity % 16 == 0
        and attn_in.shape[0] % unit == 0
        and attn_out.shape[0] % unit == 0
        and width % (2 * unit) == 0
        and hidden == nz * width
        and expert_in.shape[0] == 1
    )


def layer_kernel(layer_input, memory, cotangent, routes, doc_lengths, rel_buckets, gains, bias_table, router,
                 attn_in, attn_out, expert_in, expert_out):
    nz, ns, ny, packs, tok, width = shapes_of(layer_input, routes, attn_in, attn_out, expert_in, expert_out)
    nx = ns // 2
    group, pairs = ns * tok, width // 128
    unit = expert_in.shape[1]
    panels = expert_in.shape[2] // width
    experts, buckets = router.shape[1], bias_table.shape[0]
    each = packs * ((5 * tok + 4 * experts - 1) // (4 * experts))
    tall = nz * ns
    units = (attn_in.shape[0] // unit, attn_out.shape[0] // unit, panels, panels)
    total = tall * ny * (units[0] + units[1])
    extra = -(-(3 + experts) // 8) * 8
    small = ny + nx - 1 + nz
    mine, every = packs * tok, packs * group
    any_ = pl.BlockSpec(memory_space=pl.ANY)
    vmem = pl.BlockSpec(memory_space=pltpu.VMEM)
    smem = pl.BlockSpec(memory_space=pltpu.SMEM)
    dma = pltpu.SemaphoreType.DMA
    low = lambda *shape: pltpu.VMEM(shape, BF)
    wide = lambda *shape: pltpu.VMEM(shape, F32)
    shape = lambda *dims: jax.ShapeDtypeStruct(dims, F32)
    out_rows, g0, g1, g2, g3, grad_x, grad_mem, sums, table = pl.pallas_call(
        layer_body,
        out_shape=[
            jax.ShapeDtypeStruct((packs, tok, width), BF),
            shape(*attn_in.shape),
            shape(*attn_out.shape),
            shape(*expert_in.shape[1:]),
            shape(*expert_out.shape[1:]),
            shape(mine, width),
            shape(mine, width),
            shape(extra, width),
            shape(buckets, 128),
        ],
        in_specs=[smem, *[vmem] * 8, any_, any_, vmem, any_],
        out_specs=[vmem] * 9,
        scratch_shapes=[
            low(total, unit, width),
            low(total, unit, width),
            low(2 * tall * panels, unit, width),
            *[low(nz, nx, panels, unit, width)] * 2,
            *[low(nz, ny - 1, nx, u, unit, width) for u in units[:2]],
            *[low(nz, nx - 1, u, unit, width) for u in units],
            *[low(nz + 1, u, unit, width) for u in units],
            *[low(every, width)] * 8,
            *[low(mine, width)] * 10,
            *[low(packs, pairs, 2 * tok, group)] * 2,
            *[wide(mine, width)] * 3,
            wide(pairs, 2 * tok, group),
            wide(packs, tok, group),
            wide(packs, tok, group),
            wide(128, group + 128),
            wide(1, width),
            low(2, packs, nx, tok, width),
            low(2, nx - 1, packs, tok, width),
            wide(4, extra, width),
            wide(4, buckets, 128),
            wide(small, extra, width),
            wide(small, buckets, 128),
            low(2, ny, each, width),
            low(2, ny, each, width),
            wide(2, ny * each, width),
            low(2, ny, each, width),
            low(ny * each, width),
            low(ny * each, width),
            dma((2, packs, 2 * nx)),
            dma((2, packs, nx, 2)),
            dma((4, nz, 2)),
            dma((4, nz, nx - 1 + (ny - 1) * (1 + nx))),
            dma((4, nz, nx, ny)),
            dma((4, nz, nx, ny)),
            dma((4, nz, nx, ny)),
            dma((6, packs)),
            dma((4, nz, nx)),
            dma((4, nz, nx)),
            dma((2, nz, ny - 1, nx)),
            dma((2, nz, ny - 1, nx)),
            dma((4, nz, nx - 1)),
            dma((4, nz, nx - 1)),
            dma((4, nz)),
            dma((4, nz + 1)),
            dma((2, packs + 1, nx)),
            dma((2, packs + 1, nx)),
            dma((2, small)),
            dma((2, small)),
            dma((4, ny - 1)),
            dma((4, ny - 1)),
            pltpu.SemaphoreType.REGULAR,
        ],
        compiler_params=pltpu.CompilerParams(
            collective_id=0, has_side_effects=True, vmem_limit_bytes=64 * 2**20
        ),
        name="layer",
    )(
        doc_lengths[:, 0, 0],
        rel_buckets.reshape(1, -1),
        gains,
        bias_table,
        router.T.astype(F32),
        routes.reshape(mine, 1),
        layer_input[:, 0, 0],
        memory[:, 0, 0],
        cotangent[:, 0, 0],
        attn_in.reshape(units[0], unit, width),
        attn_out.reshape(units[1], unit, width),
        expert_in[0],
        expert_out.reshape(panels, unit, width),
    )
    spread = (packs, 1, 1, tok, width)
    return (
        out_rows.reshape(spread),
        grad_x.reshape(spread),
        grad_mem.reshape(spread),
        sums[:3],
        table[:, : 2 * pairs],
        sums[3 : 3 + experts].T,
        g0,
        g1,
        g2[None],
        g3[None],
    )


def norm_apply(value, gain):
    return value * lax.rsqrt(jnp.mean(value * value, axis=-1, keepdims=True) + EPS) * gain


def norm_back(value, gain, grad):
    r = lax.rsqrt(jnp.mean(value * value, axis=-1, keepdims=True) + EPS)
    scaled = grad * gain
    back = r * scaled - value * (r * r * r) * jnp.mean(scaled * value, axis=-1, keepdims=True)
    return back, jnp.sum(grad * value * r, axis=0)


def gelu_tanh(value):
    return jax.nn.gelu(value, approximate=True)


def times(left, right):
    return jnp.dot(left, right, preferred_element_type=F32)


def times_right(left, right):
    return jnp.einsum("te,de->td", left, right, preferred_element_type=F32)


def times_left(left, right):
    return jnp.einsum("td,te->de", left, right, preferred_element_type=F32)


def split(a, packs):
    return a.reshape(packs, -1, HEADS, HEAD)


def attend(query, keys, values, allowed, bias, packs):
    scores = jnp.einsum("pqhd,pkhd->phqk", split(query, packs), split(keys, packs), preferred_element_type=F32)
    masked = jnp.where(allowed[:, None], scores * HEAD**-0.5 + bias, NEG)
    raised = jnp.exp(masked - jnp.max(masked, axis=3, keepdims=True))
    chances = raised / jnp.sum(raised, axis=3, keepdims=True)
    mixed = jnp.einsum("phqk,pkhd->pqhd", chances.astype(BF), split(values, packs), preferred_element_type=F32)
    return mixed.reshape(query.shape).astype(BF), chances


def attend_back(query, keys, values, chances, grad, packs):
    scale = HEAD**-0.5
    g4 = split(grad, packs)
    grad_chances = jnp.einsum("pqhd,pkhd->phqk", g4, split(values, packs), preferred_element_type=F32)
    spread_ = jnp.sum(chances * grad_chances, axis=3, keepdims=True)
    grad_scores = (chances * (grad_chances - spread_)).astype(BF)
    grad_query = jnp.einsum("phqk,pkhd->pqhd", grad_scores, split(keys, packs), preferred_element_type=F32) * scale
    grad_keys = jnp.einsum("phqk,pqhd->pkhd", grad_scores, split(query, packs), preferred_element_type=F32) * scale
    grad_values = jnp.einsum("phqk,pqhd->pkhd", chances.astype(BF), g4, preferred_element_type=F32)
    return (
        grad_query.reshape(query.shape).astype(BF),
        grad_keys.reshape(keys.shape).astype(BF),
        grad_values.reshape(keys.shape).astype(BF),
        grad_scores,
    )


def per_device(layer_input, memory, cotangent, routes, doc_lengths, rel_buckets, gains, bias_table, router,
               attn_in, attn_out, expert_in, expert_out):
    packs, rows, width = layer_input.shape[0], layer_input.shape[3], layer_input.shape[4]
    seqs = lax.axis_size("seq")
    group = rows * seqs
    experts = router.shape[1]
    capacity = (5 * rows + 4 * experts - 1) // (4 * experts)
    buckets = bias_table.shape[0]
    rank = lax.axis_index("seq")

    x_in, m_in, e_in, e_out = layer_input[:, 0, 0], memory[:, 0, 0], expert_in[0], expert_out[0]
    if fits_kernel(layer_input, routes, attn_in, attn_out, expert_in, expert_out):
        return layer_kernel(layer_input, memory, cotangent, routes, doc_lengths, rel_buckets, gains, bias_table, router,
                            attn_in, attn_out, expert_in, expert_out)
    x_rows = x_in.reshape(packs * rows, width).astype(F32)
    everywhere, peers = ("dp", "seq", "expert"), ("dp", "seq")
    x_all, m_all = (lax.all_gather(a, "seq", axis=1, tiled=True) for a in (x_in, m_in))
    w_in, w_out = (lax.all_gather(a, everywhere, axis=0, tiled=True) for a in (attn_in, attn_out))
    e_in, e_out = (lax.all_gather(a, peers, axis=0, tiled=True) for a in (e_in, e_out))
    w_in = w_in.reshape(6, width, width)
    w_out = w_out.reshape(2, width, width)
    x_all = x_all.reshape(packs * group, width)
    m_all = m_all.reshape(packs * group, width)
    wide = group + rows
    query_pos = rank * rows + jnp.arange(rows, dtype=jnp.int32)
    key_pos = jnp.arange(group, dtype=jnp.int32)
    ends = jnp.cumsum(doc_lengths[:, 0, 0], axis=1)
    query_doc = jnp.sum((query_pos[None, :, None] >= ends[:, None, :]).astype(jnp.int32), axis=2)
    key_doc = jnp.sum((key_pos[None, :, None] >= ends[:, None, :]).astype(jnp.int32), axis=2)
    same = query_doc[:, :, None] == key_doc[:, None, :]
    causal = same & (key_pos[None, None, :] <= query_pos[None, :, None])
    bucket_hot = (rel_buckets[:, None] == jnp.arange(buckets, dtype=jnp.int32)).astype(F32)
    line_at = jnp.arange(group + rows, dtype=jnp.int32) - (group - 1) + rank * rows
    line_hot = (jnp.take(rel_buckets, jnp.clip(line_at, 0, group - 1))[None, :] == jnp.arange(buckets)[:, None]).astype(F32)
    line = jnp.einsum("bh,bj->hj", bias_table, line_hot, precision=HIGHEST)
    line = line[:, ::-1]
    wide = group + rows
    tiled = jnp.broadcast_to(line[:, None, :], (HEADS, rows, wide)).reshape(HEADS, rows * wide)
    skew = tiled[:, rows : rows + rows * (wide - 1)].reshape(HEADS, rows, wide - 1)[:, :, :group]

    normed1_all = norm_apply(x_all.astype(F32), gains[0]).astype(BF)
    normed1 = norm_apply(x_rows, gains[0]).astype(BF)
    query = times(normed1, w_in[0]).astype(BF)
    keys = times(normed1_all, w_in[1]).astype(BF)
    values = times(normed1_all, w_in[2]).astype(BF)
    mem_keys = times(m_all, w_in[4]).astype(BF)
    mem_values = times(m_all, w_in[5]).astype(BF)
    mixed, chances_self = attend(query, keys, values, causal, skew[None], packs)
    hidden1 = x_rows + times(mixed, w_out[0])
    normed2 = norm_apply(hidden1, gains[1]).astype(BF)
    cross_query = times(normed2, w_in[3]).astype(BF)
    cross_mixed, chances_cross = attend(cross_query, mem_keys, mem_values, same, 0.0, packs)
    hidden2 = hidden1 + times(cross_mixed, w_out[1])
    normed3 = norm_apply(hidden2, gains[2]).astype(BF)

    routing = jax.nn.softmax(times(normed3, router), axis=1)
    route = routes[:, 0, 0, :, 0]
    route_hot = (route[:, :, None] == jnp.arange(experts, dtype=jnp.int32)).astype(jnp.int32)
    slot = jnp.sum((jnp.cumsum(route_hot, axis=1) - route_hot) * route_hot, axis=2)
    hot = route_hot.reshape(packs * rows, experts).astype(F32)
    gate = jnp.sum(routing * hot, axis=1)
    target = jnp.where(slot < capacity, (route * packs + jnp.arange(packs)[:, None]) * capacity + slot, -1).reshape(-1)
    dispatch = (target[:, None] == jnp.arange(experts * packs * capacity, dtype=jnp.int32)).astype(BF)

    def swap(a):
        shape = (experts, packs * capacity, width)
        return lax.all_to_all(a.reshape(shape), "expert", split_axis=0, concat_axis=0, tiled=True).reshape(-1, width)

    received = swap(times_left(dispatch, normed3).astype(BF))
    inner = times(received, e_in)
    hidden, pull = jax.vjp(gelu_tanh, inner)
    hidden = hidden.astype(BF)
    result = times(hidden, e_out).astype(BF)
    combined = times(dispatch, swap(result))
    out_rows = (hidden2 + gate[:, None] * combined).astype(BF)
    grad_top = cotangent.reshape(packs * rows, width).astype(F32)
    grad_gate = jnp.sum(grad_top * combined, axis=1)
    grad_result = swap(times_left(dispatch, (gate[:, None] * grad_top).astype(BF)).astype(BF))
    grad_hidden = times_right(grad_result, e_out)
    grad_eout = times_left(hidden, grad_result).astype(BF)
    grad_inner = pull(grad_hidden)[0].astype(BF)
    grad_ein = times_left(received, grad_inner).astype(BF)
    grad_send = swap(times_right(grad_inner, e_in).astype(BF))
    grad_logits = grad_gate[:, None] * routing * (hot - gate[:, None])
    grad_router = jnp.einsum("td,te->de", normed3.astype(F32), grad_logits, precision=HIGHEST)
    grad_normed3 = times(dispatch, grad_send) + jnp.einsum(
        "te,de->td", grad_logits, router.astype(F32), precision=HIGHEST
    )
    back3, gain3 = norm_back(hidden2, gains[2], grad_normed3)
    grad_h2 = grad_top + back3
    grad_h2_low = grad_h2.astype(BF)
    grad_wco = times_left(cross_mixed, grad_h2_low)
    grad_cross = times_right(grad_h2_low, w_out[1]).astype(BF)
    grad_cq, grad_ck, grad_cv, _ = attend_back(cross_query, mem_keys, mem_values, chances_cross, grad_cross, packs)
    back2, gain2 = norm_back(hidden1, gains[1], times_right(grad_cq, w_in[3]))
    grad_h1 = grad_h2 + back2
    grad_h1_low = grad_h1.astype(BF)
    grad_wso = times_left(mixed, grad_h1_low)
    grad_mixed = times_right(grad_h1_low, w_out[0]).astype(BF)
    grad_q, grad_k, grad_v, grad_scores = attend_back(query, keys, values, chances_self, grad_mixed, packs)

    total = jnp.sum(grad_scores.astype(F32), axis=0)[:, ::-1]
    padded = jnp.pad(total, ((0, 0), (0, 0), (0, wide - group))).reshape(HEADS, rows * wide)
    diagonal = padded[:, : rows * (wide - 1)].reshape(HEADS, rows, wide - 1).sum(axis=1)
    at = jnp.clip(rank * rows + (rows - 1) - jnp.arange(wide - 1, dtype=jnp.int32), 0, group - 1)
    diagonal_hot = (jnp.take(rel_buckets, at)[:, None] == jnp.arange(buckets)).astype(F32)
    grad_table = jnp.einsum("jb,hj->bh", diagonal_hot, diagonal, precision=HIGHEST)

    def to_owner(a):
        return lax.psum_scatter(a.reshape(packs, group, width), "seq", scatter_dimension=1, tiled=True)

    grad_memory = to_owner((times_right(grad_ck, w_in[4]) + times_right(grad_cv, w_in[5])).astype(BF))
    part1 = to_owner((times_right(grad_k, w_in[1]) + times_right(grad_v, w_in[2])).astype(BF))
    grad_normed1 = times_right(grad_q, w_in[0]) + part1.reshape(packs * rows, width).astype(F32)
    back1, gain1 = norm_back(x_rows, gains[0], grad_normed1)
    grad_x = grad_h1 + back1
    grad_in = jnp.concatenate(
        [
            times_left(normed1, grad_q),
            times_left(normed1_all, grad_k),
            times_left(normed1_all, grad_v),
            times_left(normed2, grad_cq),
            times_left(m_all, grad_ck),
            times_left(m_all, grad_cv),
        ]
    ).astype(BF)
    grad_out = jnp.concatenate([grad_wso, grad_wco]).astype(BF)
    shards = [
        lax.psum_scatter(a, over, scatter_dimension=0, tiled=True).astype(F32)
        for a, over in ((grad_in, everywhere), (grad_out, everywhere), (grad_ein, peers), (grad_eout, peers))
    ]
    small = lax.psum((jnp.stack([gain1, gain2, gain3]), grad_table, grad_router), ("dp", "seq", "expert"))
    shape = (packs, 1, 1, rows, width)
    return (
        out_rows.reshape(shape),
        grad_x.reshape(shape),
        grad_memory.astype(F32).reshape(shape),
        *small,
        shards[0],
        shards[1],
        shards[2][None],
        shards[3][None],
    )


def solution(mesh):
    tokens = P(None, "dp", "expert", "seq", None)
    dense = P(("dp", "seq", "expert"), None)
    expert = P("expert", ("dp", "seq"), None)
    return jax.shard_map(
        per_device,
        mesh=mesh,
        in_specs=(tokens, tokens, tokens, tokens, P(None, "dp", "expert", None), P(), P(), P(), P(),
                  dense, dense, expert, expert),
        out_specs=(tokens, tokens, tokens, P(), P(), P(), dense, dense, expert, expert),
        check_vma=False,
    )
```

time: 288 us -> 234 us (0.81)
  matrix products: 28.6 us -> 0 us
  starting transfers between devices: 17.7 us -> 0 us
  other arithmetic: 5.09 us -> 1.26 us
  waiting for transfers between devices: 3.47 us -> 0 us
    dot_general x13 -> x0, matrix products: 28.6 us -> none  [the longest x4 10.7 us: times_left(): return jnp.einsum('td,te->de', left, right, preferred_element_type=F32)]
    all_to_all x4 -> x0, starting transfers between devices: 17.7 us -> none  [swap(): lax.all_to_all(a.reshape(shape), 'expert', split_axis=0, concat_axis=0, t...]
    all_to_all x4 -> x0, waiting for transfers between devices: 3.47 us -> none  [swap(): lax.all_to_all(a.reshape(shape), 'expert', split_axis=0, concat_axis=0, t...]
    pallas_call x2 -> x1, Pallas kernels: 216 us -> 217 us  [layer_kernel(): pl.pallas_call(layer_body, out_shape=[jax.ShapeDtypeStruct((packs, tok, w...]
    unnamed x35 -> x28, local copies, waits for them, and re-layouts: 10.1 us -> 10.4 us
  transfers between devices with their start and end apart: 4 -> 0, of which waited for: 2 -> 0; matrix products, arithmetic and copies ran while one was open for 4% -> 0% of each run, Pallas kernels for 0% -> 0%
where the time goes in v3:
time: 234 us; the launch traced here: 233 us
  Pallas kernels  217 us (93%)
  local copies, waits for them, and re-layouts  13.9 us (6%)
    pallas_call x1, Pallas kernels, layer_kernel(): pl.pallas_call(layer_body, out_shape=[jax.ShapeDtypeStruct((packs, tok, w...  217 us
    unnamed x28, local copies, waits for them, and re-layouts  10.4 us

profile of v3, /device:TPU:12, one launch (start us, length us, event | category | flops | bytes accessed | tf_op | source)
XLA Modules:
  0.0 233.1 jit_solution(1369505445133709646)
XLA Ops:
  0.6 0.0 copy-start.8
  0.7 0.0 copy-start.7
  0.7 0.0 copy-start.6
  0.7 0.5 broadcast.3
  1.2 0.1 copy-done.8
  1.3 0.7 reduce.3
  2.0 0.0 copy-done.7
  2.0 0.6 convert_bitcast_fusion.router_t
  2.6 0.0 copy-done.6
  2.6 0.7 copy.23.table
  3.3 0.8 reshape.52.route
  4.1 217.2 %layer.1 = (bf16[2,64,768]{2,1,0:T(8,128)(2,1)}, f32[144,768]{1,0:T(8,128)}, f32[48,768]{1,0:T(8,128)}, f32[48,3072]{1,0:T(8,128)}, f32[192,768]{1,0:T(8,128)}, ...) custom-call(s32[2,3]{1,0:T(2,128)} %bitcast.39, s32[1,256]{1,0:T(1,128)} %bitcast.40, ...), custom_call_target="tpu_custom_call" | custom-call | tf_op jit(solution)/shard_map/layer/pallas_call | solution.py:912
  221.2 0.0 copy-start.4
  221.3 1.4 slice_bitcast_fusion
  222.6 1.3 slice.9
  224.0 1.4 copy.28
  225.4 1.6 copy.36
  227.0 0.0 copy-done.4
  227.0 0.0 copy-start.3
  227.0 0.7 copy.37
  227.7 0.4 copy-done.3
  228.1 0.0 copy-start.2
  228.1 0.7 copy.38
  228.9 0.4 copy-done.2
  229.3 0.0 copy-start.5
  229.3 0.0 copy-start.1
  229.3 0.8 copy.39
  230.0 0.3 copy-done.5
  230.3 0.7 copy.40
  231.0 0.0 copy-done.1
  231.0 0.0 copy-start
  231.0 0.8 copy.41
  231.8 0.5 copy-done
  232.3 0.8 copy.42
Async XLA Ops:
  0.6 0.7 copy-start.8
  0.7 1.3 copy-start.7
  0.7 1.9 copy-start.6
  221.2 5.7 %copy-start.4 = (f32[128,768]{1,0:T(8,128)S(1)}, f32[128,768]{1,0:T(8,128)}, u32[]{:S(2)}) copy-start(f32[128,768]{1,0:T(8,128)} %get-tuple-element.20) | copy-start | bytes 1179652
  227.0 1.1 copy-start.3
  228.1 1.2 copy-start.2
  229.3 1.0 copy-start.5
  229.3 1.7 copy-start.1
  231.0 1.3 copy-start

commit v4 on v3

--- a/solution.py
+++ b/solution.py
@@ -39,7 +39,10 @@
         return [lax.rem(self.y + k, self.ny) for k in range(1, self.ny)]
 
     def by_distance(self, k):
-        order = [sorted(range(self.nz), key=lambda d: (abs(d - z), d)) for z in range(self.nz)]
+        half = self.nz // 2
+        order = [
+            sorted(range(self.nz), key=lambda d: (abs(d - z), (d < half) != (z < half), d)) for z in range(self.nz)
+        ]
         return self.pick([row[k] for row in order])
 
     def pick(self, values):
@@ -90,7 +93,7 @@
 
 
 def prepare_bias(rel, table, bias, rank, rows, group):
-    buckets, heads = table.shape
+    heads, buckets = table.shape
     wide = group + 128
     lane = lax.broadcasted_iota(jnp.int32, (group, wide), 1)
     shift = jnp.where(lane < group, lane, lane - wide)
@@ -98,7 +101,7 @@
     hot = (lax.broadcasted_iota(jnp.int32, (group, wide), 0) == distance).astype(F32).astype(BF)
     which = jnp.dot(jnp.broadcast_to(rel[...].astype(F32), (8, group)).astype(BF), hot, preferred_element_type=F32)
     picks = (lax.broadcasted_iota(jnp.int32, (buckets, wide), 0) == which[0:1].astype(jnp.int32)).astype(F32)
-    line = lax.dot_general(table[...], picks, (((0,), (0,)), ((), ())), precision=HIGHEST, preferred_element_type=F32)
+    line = jnp.dot(table[...], picks, precision=HIGHEST, preferred_element_type=F32)
     for h in range(heads):
         band = pltpu.roll(jnp.broadcast_to(line[h : h + 1], (rows, wide)), 0, 1, stride=1, stride_axis=0)
         bias[h // 2, pl.ds((h % 2) * rows, rows), :] = band[:, :group]
@@ -154,7 +157,7 @@
         mixed[mine, lanes] = one_pair(out).astype(BF)
         return carry
 
-    lax.fori_loop(0, packs * pairs, body, 0, unroll=2)
+    lax.fori_loop(0, packs * pairs, body, 0, unroll=6)
 
 
 def add_product(total, left, weight, index):
@@ -271,30 +274,34 @@
                 diagonal[pl.ds(2 * j + half, 1), :] += jnp.sum(band, axis=0, keepdims=True)
         return carry
 
-    lax.fori_loop(0, packs * pairs, body, 0, unroll=2)
-
-
-def table_grad(rel, diagonal, rank, rows, group, buckets):
+    lax.fori_loop(0, packs * pairs, body, 0, unroll=6)
+
+
+def table_grad(rel, diagonal, rank, rows, group):
     wide = group + 128
     lane = lax.broadcasted_iota(jnp.int32, (group, wide), 1)
     distance = jnp.clip(rank * rows + rows - 1 - lane, 0, group - 1)
     hot = (lax.broadcasted_iota(jnp.int32, (group, wide), 0) == distance).astype(F32).astype(BF)
     which = jnp.dot(jnp.broadcast_to(rel[...].astype(F32), (8, group)).astype(BF), hot, preferred_element_type=F32)
-    picks = (lax.broadcasted_iota(jnp.int32, (buckets, wide), 0) == which[0:1].astype(jnp.int32)).astype(F32)
-    return lax.dot_general(picks, diagonal[...], (((1,), (1,)), ((), ())), precision=HIGHEST, preferred_element_type=F32)
-
-
-def route_slots(route, packs, experts, capacity):
-    count = route.shape[0]
-    hot = (route[...] == lax.broadcasted_iota(jnp.int32, (count, experts), 1)).astype(F32)
+    picks = (lax.broadcasted_iota(jnp.int32, (128, wide), 0) == which[0:1].astype(jnp.int32)).astype(F32)
+    return lax.dot_general(diagonal[...], picks, (((1,), (1,)), ((), ())), precision=HIGHEST, preferred_element_type=F32)
+
+
+def route_slots(route, experts, capacity):
+    packs, _, rows = route.shape
+    count = packs * rows
+    same = lax.broadcasted_iota(jnp.int32, (rows, rows), 0) == lax.broadcasted_iota(jnp.int32, (rows, rows), 1)
+    column = jnp.concatenate(
+        [jnp.sum(jnp.where(same, route[p], 0), axis=1, keepdims=True) for p in range(packs)], axis=0
+    )
+    hot = (column == lax.broadcasted_iota(jnp.int32, (count, experts), 1)).astype(F32)
     a = lax.broadcasted_iota(jnp.int32, (count, count), 0)
     b = lax.broadcasted_iota(jnp.int32, (count, count), 1)
-    rows = count // packs
     earlier = ((b < a) & (a // rows == b // rows)).astype(F32).astype(BF)
     before = jnp.dot(earlier, hot.astype(BF), preferred_element_type=F32)
     slot = jnp.sum(before * hot, axis=1, keepdims=True).astype(jnp.int32)
     pack = lax.broadcasted_iota(jnp.int32, (count, 1), 0) // rows
-    target = jnp.where(slot < capacity, (route[...] * packs + pack) * capacity + slot, -1)
+    target = jnp.where(slot < capacity, (column * packs + pack) * capacity + slot, -1)
     slots = lax.broadcasted_iota(jnp.int32, (count, experts * packs * capacity), 1)
     return hot, (target == slots).astype(F32).astype(BF)
 
@@ -307,28 +314,43 @@
     return z * half, slope
 
 
+def continue_waits(waits, hop, d, at):
+    def wait():
+        @pl.when(d < at.z)
+        def _():
+            hop(-1).wait_send()
+
+        @pl.when(d > at.z)
+        def _():
+            hop(1).wait_send()
+
+    waits.append(wait)
+
+
 def layer_body(lengths, rel, gains, table, router_t, route, x_ref, m_ref, g_ref, ain, aout, ein, eout,
-               out_rows, o0, o1, o2, o3, grad_x, grad_mem, sum_wide, sum_table,
-               w, big, ge, c2, c3, y0, y1, x0, x1, x2, x3, z0, z1, z2, z3,
+               out_rows, o0, o1, o2, o3, grad_x, grad_mem, sum_gains, sum_router, sum_table,
+               w, big, ge, prep, c2, c3, y0, y1, x0, x1, ex_in, z0, z1, z2, z3,
                xo, mo, n1_all, k_, v, kc, vc, gv, n1, q, mixed, n2, qc, cross_mixed, n3, gb, ga, gq,
                pr_self, pr_cross, h1, h2, gn, bias, same, causal, diagonal, gain_row,
                act_core, act_x, wide_sum, table_sum, wide_in, table_in,
-               slots_out, slots_in, slots_acc, back_in, hid, gin_,
-               act_send, act_recv, line_send, side_send, spread_send, ici_recv, spread_recv, own_sem,
-               core_send, core_recv, y_send, y_recv, x_send, x_recv, z_send, z_recv,
-               sum_send, sum_recv, small_send, small_recv, swap_send, swap_recv, free_sem):
+               slots_out, slots_in, slots_acc, ret_out, ret_in, back_in, hid, gin_,
+               act_send, act_recv, prep_send, prep_recv, line_send, side_send, spread_send, ici_recv, spread_recv, own_sem,
+               core_send, core_recv, y_send, y_recv, x_send, x_recv, ex_send, ex_recv, z_send, z_recv, zd_send, zd_recv,
+               sum_send, sum_recv, small_send, small_recv, slot_send, slot_recv, free_sem):
     at = Place()
     nz, nx, ny = at.nz, at.nx, at.ny
     packs, tok, width = x_ref.shape
     group = xo.shape[0] // packs
     experts = router_t.shape[0]
     unit = ain.shape[1]
-    panels = eout.shape[0]
-    buckets = table.shape[0]
+    block_units = eout.shape[0]
+    panels = block_units // nx
+    columns = ein.shape[1] // (nz * nx)
+    buckets = table.shape[1]
     gk = xo
-    units = (ain.shape[0], aout.shape[0], panels, panels)
+    units = (ain.shape[0], aout.shape[0])
     tall = nz * nx * 2
-    bases = (0, tall * ny * units[0], 0, tall * panels)
+    bases = (0, tall * ny * units[0], 0, 2 * nz * block_units)
     dense, e_in, e_out = (0, 1), 2, 3
     experts_ = (e_in, e_out)
     waits = []
@@ -349,11 +371,13 @@
         pltpu.make_async_copy(ref, ref, sem).wait()
 
     def spot(a, z, x, c, y):
-        index = (z * nx + x) * 2 + c
-        index = index * ny + y if a in dense else index
-        return (w if a in dense else big).at[pl.ds(bases[a] + index * units[a], units[a])]
-
-    shards = {0: ain, 1: aout, 3: eout}
+        index = ((z * nx + x) * 2 + c) * ny + y
+        return w.at[pl.ds(bases[a] + index * units[a], units[a])]
+
+    def pack_of(a, z, c):
+        return big.at[pl.ds(bases[a] + (z * 2 + c) * block_units, block_units)]
+
+    shards = (ain, aout)
     acts = ((x_ref, xo), (m_ref, mo))
 
     at.greet()
@@ -362,18 +386,20 @@
         return full.at[pl.ds(pl.multiple_of(p * group + (x * 2 + c) * tok, 16), tok)]
 
     own_waits = []
-    for i, (src, full) in enumerate(acts):
-        for p in range(packs):
-            dst = act_rows(full, p, at.x, at.c)
-            for k, x in enumerate(at.other_x()):
-                send(src.at[p], dst, act_send.at[i, p, k], act_recv.at[i, p, at.x, at.c], x=x)
-            send(src.at[p], dst, act_send.at[i, p, nx - 1 + at.x], act_recv.at[i, p, at.x, at.c], c=1 - at.c)
-            own = pltpu.make_async_copy(src.at[p], dst, own_sem.at[4 + i, p])
-            own.start()
-            own_waits.append(own.wait)
+
+    def send_acts():
+        for i, (src, full) in enumerate(acts):
+            for p in range(packs):
+                dst = act_rows(full, p, at.x, at.c)
+                for k, x in enumerate(at.other_x()):
+                    send(src.at[p], dst, act_send.at[i, p, k], act_recv.at[i, p, at.x, at.c], x=x)
+                send(src.at[p], dst, act_send.at[i, p, nx - 1 + at.x], act_recv.at[i, p, at.x, at.c], c=1 - at.c)
+                own = pltpu.make_async_copy(src.at[p], dst, own_sem.at[4 + i, p])
+                own.start()
+                own_waits.append(own.wait)
 
     def along_line(a, z, src):
-        dst = spot(a, z, at.x, at.c, at.y)
+        dst = spot(a, z, at.x, at.c, at.y) if a in dense else pack_of(a, z, at.c)
         sem = ici_recv.at[a, z, at.x, at.y]
         left = (z >= at.z) & (at.z > 0)
         right = (z <= at.z) & (at.z < nz - 1)
@@ -400,153 +426,168 @@
 
         waits.append(wait)
 
-    def to_sides(a, z, src):
-        dst = spot(a, z, at.x, at.c, at.y)
-        for k, x in enumerate(at.other_x()):
-            send(src, dst, side_send.at[a, z, k], ici_recv.at[a, z, at.x, at.y], x=x)
-        if a in dense:
-            for k, y in enumerate(at.other_y()):
-                send(src, dst, side_send.at[a, z, nx - 1 + k], ici_recv.at[a, z, at.x, at.y], y=y)
-
     def to_core(a, z, x, y, src):
-        send(src, spot(a, z, x, at.c, y), spread_send.at[a, z, x, y], spread_recv.at[a, z, x, y], c=1 - at.c)
+        dst = spot(a, z, x, at.c, y) if a in dense else pack_of(a, z, at.c)
+        send(src, dst, spread_send.at[a, z, x, y], spread_recv.at[a, z, x, y], c=1 - at.c)
 
     zs = [at.by_distance(k) for k in range(nz)]
-    for a in dense:
-        along_line(a, at.z, shards[a])
-    own_ein = spot(e_in, at.z, at.x, at.c, at.y)
-    first = bases[e_in] + ((at.z * nx + at.x) * 2 + at.c) * panels
-    for f in range(panels):
-        big[first + f] = ein[:, f * width : (f + 1) * width]
-    shards[2] = own_ein
-    for a in experts_:
-        along_line(a, at.z, shards[a])
-
-    def shard_events(kind, k):
-        for a in kind:
-            here = spot(a, zs[k], at.x, at.c, at.y)
+
+    def dense_events(k):
+        z = zs[k]
+        for a in dense:
+            here = spot(a, z, at.x, at.c, at.y)
+            src = here if k else shards[a]
             if k:
-                arrive(here, ici_recv.at[a, zs[k], at.x, at.y])
-                along_line(a, zs[k], here)
-            elif a != e_in:
+                arrive(here, ici_recv.at[a, z, at.x, at.y])
+            else:
                 own = pltpu.make_async_copy(shards[a], here, own_sem.at[a, 0])
                 own.start()
                 own_waits.append(own.wait)
-            src = here if k else shards[a]
-            to_sides(a, zs[k], src)
-            to_core(a, zs[k], at.x, at.y, src)
-
-    for k in range(nz):
-        shard_events(dense, k)
-        if k == 0:
-            for i, (src, full) in enumerate(acts):
-                for p in range(packs):
-                    for x in at.other_x():
-                        dst = act_rows(full, p, x, at.c)
-                        arrive(dst, act_recv.at[i, p, x, at.c])
-                        send(dst, dst, act_send.at[i, p, nx - 1 + x], act_recv.at[i, p, x, at.c], c=1 - at.c)
-
-    def diagonal_events(k):
-        for a in dense:
-            for x in at.other_x():
-                here = spot(a, zs[k], x, at.c, at.y)
-                arrive(here, ici_recv.at[a, zs[k], x, at.y])
-                for j, y in enumerate(at.other_y()):
-                    send(here, here, side_send.at[a, zs[k], nx - 1 + ny - 1 + j + (ny - 1) * x],
-                         ici_recv.at[a, zs[k], x, at.y], y=y)
-                to_core(a, zs[k], x, at.y, here)
-
-    for k in range(nz):
-        shard_events(experts_, k)
-        diagonal_events(k)
-
-    prepare_bias(rel, table, bias, at.s, tok, group)
-    prepare_masks(lengths, same, causal, at.s, tok, group)
-    for i, (src, full) in enumerate(acts):
-        for p in range(packs):
-            for x in range(nx):
-                arrive(act_rows(full, p, x, 1 - at.c), act_recv.at[i, p, x, 1 - at.c])
-    for wait in own_waits:
-        wait()
-    rms_rows(xo, gains[0:1], n1_all, packs * group)
-    for p in range(packs):
-        h1[pl.ds(p * tok, tok), :] = x_ref[p].astype(F32)
-        n1[pl.ds(p * tok, tok), :] = n1_all[pl.ds(pl.multiple_of(p * group + at.s * tok, tok), tok), :]
-    for k in range(nz):
+            along_line(a, z, src)
+            for j, x in enumerate(at.other_x()):
+                send(src, here, side_send.at[a, z, j], ici_recv.at[a, z, at.x, at.y], x=x)
+            for j, y in enumerate(at.other_y()):
+                send(src, here, side_send.at[a, z, nx - 1 + j], ici_recv.at[a, z, at.x, at.y], y=y)
+            to_core(a, z, at.x, at.y, src)
+
+    def side_y(k):
+        z = zs[k]
+        for y in at.other_y():
+            for a in dense:
+                here = spot(a, z, at.x, at.c, y)
+                arrive(here, ici_recv.at[a, z, at.x, y])
+                if a == 1:
+                    for j, x in enumerate(at.other_x()):
+                        send(here, here, side_send.at[a, z, nx - 1 + ny - 1 + j + (nx - 1) * y],
+                             ici_recv.at[a, z, at.x, y], x=x)
+                to_core(a, z, at.x, y, here)
+
+    def side_x(k):
+        z = zs[k]
+        for x in at.other_x():
+            for a in dense:
+                here = spot(a, z, x, at.c, at.y)
+                arrive(here, ici_recv.at[a, z, x, at.y])
+                if a == 0:
+                    for j, y in enumerate(at.other_y()):
+                        send(here, here, side_send.at[a, z, nx - 1 + ny - 1 + j + (ny - 1) * x],
+                             ici_recv.at[a, z, x, at.y], y=y)
+                to_core(a, z, x, at.y, here)
+
+    def corner_events(k):
+        z = zs[k]
         for a in dense:
             for y in at.other_y():
+                for x in at.other_x():
+                    here = spot(a, z, x, at.c, y)
+                    arrive(here, ici_recv.at[a, z, x, y])
+                    to_core(a, z, x, y, here)
+
+    def act_events():
+        for i, (src, full) in enumerate(acts):
+            for p in range(packs):
+                for x in at.other_x():
+                    dst = act_rows(full, p, x, at.c)
+                    arrive(dst, act_recv.at[i, p, x, at.c])
+                    send(dst, dst, act_send.at[i, p, nx - 1 + x], act_recv.at[i, p, x, at.c], c=1 - at.c)
+
+    def in_unit(z, c, x, n=1):
+        return pl.ds(bases[e_in] + ((z * 2 + c) * nx + x) * panels, n * panels)
+
+    def start_prep():
+        for x in range(nx):
+            for u in range(panels):
+                each_z = width // columns
+                prep[x, u] = jnp.concatenate(
+                    [ein[:, (z * nx + x) * columns : (z * nx + x + 1) * columns] for z in range(u * each_z, (u + 1) * each_z)],
+                    axis=1,
+                )
+        big[in_unit(at.z, at.c, at.x)] = prep[at.x]
+        for j, x in enumerate(at.other_x()):
+            send(prep.at[x], big.at[in_unit(at.z, at.c, at.x)], prep_send.at[j], prep_recv.at[at.x], x=x)
+
+    def expert_events(k, kinds=experts_):
+        z = zs[k]
+        for a in kinds:
+            here = pack_of(a, z, at.c)
+            src = here
+            if k:
+                arrive(here, ici_recv.at[a, z, at.x, at.y])
+            elif a == e_in:
+                for x in at.other_x():
+                    arrive(big.at[in_unit(at.z, at.c, x)], prep_recv.at[x])
+            else:
+                src = eout
+                own = pltpu.make_async_copy(eout, here, own_sem.at[a, 0])
+                own.start()
+                own_waits.append(own.wait)
+            along_line(a, z, src)
+            to_core(a, z, 0, 0, src)
+
+    def first_norm():
+        for i, (src, full) in enumerate(acts):
+            for p in range(packs):
                 for x in range(nx):
-                    here = spot(a, zs[k], x, at.c, y)
-                    arrive(here, ici_recv.at[a, zs[k], x, y])
-                    to_core(a, zs[k], x, y, here)
-    for a in dense:
-        for z in range(nz):
-            for x in range(nx):
-                for y in range(ny):
-                    arrive(spot(a, z, x, 1 - at.c, y), spread_recv.at[a, z, x, y])
-
-    project(n1, w, 0, q)
-    project(n1_all, w, 1, k_)
-    project(n1_all, w, 2, v)
-    project(mo, w, 4, kc)
-    project(mo, w, 5, vc)
-    attend_pairs(q, k_, v, bias, causal, pr_self, mixed)
-    add_product(h1, mixed, w, 6)
-    rms_rows(h1, gains[1:2], n2, packs * tok)
-    project(n2, w, 3, qc)
-    attend_pairs(qc, kc, vc, None, same, pr_cross, cross_mixed)
-    h2[...] = h1[...]
-    add_product(h2, cross_mixed, w, 7)
-    rms_rows(h2, gains[2:3], n3, packs * tok)
-
-    each = slots_in.shape[2]
-    hot, dispatch = route_slots(route, packs, experts, each // packs)
-    logits = lax.dot_general(n3[...], router_t[...].astype(BF), (((1,), (1,)), ((), ())), preferred_element_type=F32)
-    raised = jnp.exp(logits - jnp.max(logits, axis=1, keepdims=True))
-    routing = raised / jnp.sum(raised, axis=1, keepdims=True)
-    gate = jnp.sum(routing * hot, axis=1, keepdims=True)
-    top = g_ref[...].astype(F32).reshape(packs * tok, width)
-
-    def by_slot(rows):
+                    arrive(act_rows(full, p, x, 1 - at.c), act_recv.at[i, p, x, 1 - at.c])
+        for wait in own_waits:
+            wait()
+        rms_rows(xo, gains[0:1], n1_all, packs * group)
+        for p in range(packs):
+            h1[pl.ds(p * tok, tok), :] = x_ref[p].astype(F32)
+            n1[pl.ds(p * tok, tok), :] = n1_all[pl.ds(pl.multiple_of(p * group + at.s * tok, tok), tok), :]
+
+    places = [((z * 2 + c) * nx + x) * panels for z in range(nz) for x in range(nx) for c in range(2)]
+    each = slots_out.shape[2]
+    count = ny * each
+    row_units = width // unit
+
+    def keys_and_values(for_self):
+        @pl.when(for_self)
+        def _():
+            project(n1_all, w, 1, k_)
+            project(n1_all, w, 2, v)
+
+        @pl.when(jnp.logical_not(for_self))
+        def _():
+            project(mo, w, 4, kc)
+            project(mo, w, 5, vc)
+
+    def by_slot(dispatch, rows):
         out = lax.dot_general(dispatch, rows, (((0,), (0,)), ((), ())), preferred_element_type=F32)
         return out.astype(BF).reshape(ny, each, width)
 
-    def swap(t, source, target):
+    slot_waits = []
+
+    def slot_copy(late, src, dst, sem_from, sem_to, **where):
+        one = remote(src, dst, slot_send.at[sem_from], slot_recv.at[sem_to], **where)
+        one.start()
+        (waits if late else slot_waits).append(one.wait_send)
+
+    def y_sem(t, j):
+        return t * (ny - 1) + j
+
+    def x_sem(t, j, y):
+        return 4 * (ny - 1) + (t * (nx - 1) + j) * ny + y
+
+    def ret_sem(t, j, y):
+        return 4 * (ny - 1) + 2 * (nx - 1) * ny + (t * (nx - 1) + j) * ny + y
+
+    def send_slots(t):
         for j, y in enumerate(at.other_y()):
-            one = remote(source.at[t % 2, y], target.at[t % 2, at.y], swap_send.at[t, j], swap_recv.at[t, ny - 2 - j], y=y)
-            one.start()
-            (waits if t >= 2 else swap_waits).append(one.wait_send)
-
-    swap_waits = []
-
-    def swapped(t, target):
-        for j, y in enumerate(at.other_y()):
-            arrive(target.at[t % 2, y], swap_recv.at[t, j])
-
-    slots_out[0] = by_slot(n3[...])
-    swap(0, slots_out, slots_in)
-    slots_out[1] = by_slot((gate * top).astype(BF))
-    swap(1, slots_out, slots_in)
-    for t in range(2):
-        slots_in[t, at.y] = slots_out[t, at.y]
-
-    for k in range(nz):
-        for a in experts_:
-            for x in at.other_x():
-                here = spot(a, zs[k], x, at.c, at.y)
-                arrive(here, ici_recv.at[a, zs[k], x, at.y])
-                to_core(a, zs[k], x, at.y, here)
-    for a in experts_:
-        for z in range(nz):
-            for x in range(nx):
-                arrive(spot(a, z, x, 1 - at.c, at.y), spread_recv.at[a, z, x, at.y])
-    for t in range(2):
-        swapped(t, slots_in)
-    for wait in waits:
-        wait()
-    waits.clear()
-
-    cores, ys, xs, zs_ = {2: c2, 3: c3}, (y0, y1), (x0, x1, x2, x3), (z0, z1, z2, z3)
+            slot_copy(False, slots_out.at[t, y], slots_in.at[t, at.x, at.y], y_sem(t, j), y_sem(t, ny - 2 - j), y=y)
+        for j, x in enumerate(at.other_x()):
+            slot_copy(False, slots_out.at[t, at.y], slots_in.at[t, at.x, at.y], x_sem(t, j, at.y),
+                      x_sem(t, nx - 2 - j, at.y), x=x)
+        slots_in[t, at.x, at.y] = slots_out[t, at.y]
+
+    def summed(t, y):
+        total = slots_acc[t, at.x, y]
+        for j in range(nx - 1):
+            arrive(ret_in.at[t, j, y], slot_recv.at[ret_sem(t, j, y)])
+            total = total + ret_in[t, j, y].astype(F32)
+        return total.astype(BF)
+
+    cores, ys, xs, zs_ = {2: c2, 3: c3}, (y0, y1), (x0, x1), (z0, z1, z2, z3)
     outs = (o0, o1, o2, o3)
     far = [sorted(range(nz), key=lambda d: (-abs(d - z), d)) for z in range(nz)]
     order_e = [at.pick([far[z][k] for z in range(nz)]) for k in range(nz)]
@@ -554,22 +595,18 @@
     order_d = [at.pick([halves[z][k] for z in range(nz)]) for k in range(nz)]
     e_waits = []
 
-    def expert_part(a, d, x, c):
-        return ge.at[pl.ds(bases[a] + ((d * nx + x) * 2 + c) * panels, panels)]
+    def expert_part(a, d, c):
+        return ge.at[pl.ds(bases[a] + (d * 2 + c) * block_units, block_units)]
 
     def start_expert(a, k):
-        for x in range(nx):
-            one = remote(expert_part(a, order_e[k], x, 1 - at.c), cores[a].at[k, x], core_send.at[a, k, x],
-                         core_recv.at[a, k, x], c=1 - at.c)
-            one.start()
-            e_waits.append(one.wait_send)
+        one = remote(expert_part(a, order_e[k], 1 - at.c), cores[a].at[k], core_send.at[a, k, 0],
+                     core_recv.at[a, k, 0], c=1 - at.c)
+        one.start()
+        e_waits.append(one.wait_send)
 
     def core_expert(a, k):
-        for x in range(nx):
-            arrive(cores[a].at[k, x], core_recv.at[a, k, x])
-            add_into(cores[a].at[k, x], expert_part(a, order_e[k], x, at.c))
-        for j, x in enumerate(at.other_x()):
-            send(cores[a].at[k, x], xs[a].at[k, nx - 2 - j], x_send.at[a, k, j], x_recv.at[a, k, nx - 2 - j], x=x)
+        arrive(cores[a].at[k], core_recv.at[a, k, 0])
+        add_into(cores[a].at[k], expert_part(a, order_e[k], at.c))
 
     def free_experts():
         for wait in e_waits:
@@ -579,11 +616,16 @@
     def dense_part(a, d, x, c):
         return big.at[pl.ds(bases[a] + ((d * nx + x) * 2 + c) * ny * units[a], ny * units[a])]
 
-    def dense_core(a, k, x, y=None):
+    def dense_core(a, k, x, y=None, u=None):
         first = bases[a] // 2 + (k * nx + x) * ny * units[a]
         if y is None:
             return ge.at[pl.ds(first, ny * units[a])]
-        return ge.at[pl.ds(first + y * units[a], units[a])]
+        if u is None:
+            return ge.at[pl.ds(first + y * units[a], units[a])]
+        return ge.at[pl.ds(first + y * units[a] + u, 1)]
+
+    def xs_in_order():
+        return [(x, True) for x in at.other_x()] + [(at.x, False)]
 
     def start_dense(k):
         for a in dense:
@@ -591,40 +633,123 @@
                 send(dense_part(a, order_d[k], x, 1 - at.c), dense_core(a, k, x), core_send.at[a, k, x],
                      core_recv.at[a, k, x], c=1 - at.c)
 
-    def core_dense(k):
-        for a in dense:
-            for x in range(nx):
-                arrive(dense_core(a, k, x), core_recv.at[a, k, x])
-                add_into(dense_core(a, k, x), dense_part(a, order_d[k], x, at.c))
+    def first_dense(k):
+        for x, _ in xs_in_order():
+            arrive(dense_core(0, k, x), core_recv.at[0, k, x])
+            add_into(dense_core(0, k, x), dense_part(0, order_d[k], x, at.c))
+            for u in range(units[0]):
                 for j, y in enumerate(at.other_y()):
-                    send(dense_core(a, k, x, y), ys[a].at[k, ny - 2 - j, x],
-                         y_send.at[a, k, j, x], y_recv.at[a, k, ny - 2 - j, x], y=y)
-
-    def y_dense(k):
-        for a in dense:
-            for x in range(nx):
+                    send(dense_core(0, k, x, y, u), ys[0].at[k, ny - 2 - j, x, pl.ds(u, 1)],
+                         y_send.at[k, j, x, u], y_recv.at[k, ny - 2 - j, x, u], y=y)
+        for x, _ in xs_in_order():
+            arrive(dense_core(1, k, x), core_recv.at[1, k, x])
+            add_into(dense_core(1, k, x), dense_part(1, order_d[k], x, at.c))
+        for j, x in enumerate(at.other_x()):
+            send(dense_core(1, k, x), xs[1].at[k, nx - 2 - j], x_send.at[k, j, units[0]],
+                 x_recv.at[k, nx - 2 - j, units[0]], x=x)
+
+    def second_dense(k):
+        for x, away in xs_in_order():
+            for u in range(units[0]):
+                total = ys[0].at[k, 0, x, pl.ds(u, 1)]
                 for j in range(ny - 1):
-                    arrive(ys[a].at[k, j, x], y_recv.at[a, k, j, x])
-                    add_into(ys[a].at[k, 0, x], ys[a].at[k, j, x] if j else dense_core(a, k, x, at.y))
-            for j, x in enumerate(at.other_x()):
-                send(ys[a].at[k, 0, x], xs[a].at[k, nx - 2 - j], x_send.at[a, k, j], x_recv.at[a, k, nx - 2 - j], x=x)
+                    piece = ys[0].at[k, j, x, pl.ds(u, 1)]
+                    arrive(piece, y_recv.at[k, j, x, u])
+                    add_into(total, piece if j else dense_core(0, k, x, at.y, u))
+                if away:
+                    j = lax.rem(x - at.x + nx, nx) - 1
+                    send(total, xs[0].at[k, nx - 2 - j, pl.ds(u, 1)], x_send.at[k, j, u], x_recv.at[k, nx - 2 - j, u], x=x)
+        for j in range(nx - 1):
+            arrive(xs[1].at[k, j], x_recv.at[k, j, units[0]])
+            add_into(xs[1].at[k, 0], xs[1].at[k, j] if j else dense_core(1, k, at.x))
+        for j, y in enumerate(at.other_y()):
+            send(xs[1].at[k, 0, pl.ds(y * units[1], units[1])], ys[1].at[k, ny - 2 - j],
+                 y_send.at[k, j, nx, 0], y_recv.at[k, ny - 2 - j, nx, 0], y=y)
+
+    def piece_of(k, p):
+        return xs[0].at[k, 0, pl.ds(p, 1)] if p < units[0] else ys[1].at[k, 0]
+
+    def inbox_of(slot, p):
+        return zs_[0].at[slot, pl.ds(p, 1)] if p < units[0] else zs_[1].at[slot]
+
+    def line_dense(k):
+        d = order_d[k]
+        for p in range(units[0] + 1):
+            total = piece_of(k, p)
+            if p < units[0]:
+                for j in range(nx - 1):
+                    piece = xs[0].at[k, j, pl.ds(p, 1)]
+                    arrive(piece, x_recv.at[k, j, p])
+                    add_into(total, piece if j else ys[0].at[k, 0, at.x, pl.ds(p, 1)])
+            else:
+                for j in range(ny - 1):
+                    arrive(ys[1].at[k, j], y_recv.at[k, j, nx, 0])
+                    add_into(total, ys[1].at[k, j] if j else xs[1].at[k, 0, pl.ds(at.y * units[1], units[1])])
+            for side in range(2):
+
+                @pl.when((at.z > 0) & (d > at.z) if side == 0 else (at.z < nz - 1) & (d < at.z))
+                def _(total=total, p=p):
+                    arrive(inbox_of(d, p), zd_recv.at[d, p])
+                    add_into(total, inbox_of(d, p))
+
+            def hop(to, total=total, p=p):
+                slot = d if to > 0 else jnp.where(d == at.z - 1, nz, d)
+                return remote(total, inbox_of(slot, p), zd_send.at[k, p], zd_recv.at[slot, p], z=at.z + to)
+
+            @pl.when(d < at.z)
+            def _(hop=hop):
+                hop(-1).start()
+
+            @pl.when(d > at.z)
+            def _(hop=hop):
+                hop(1).start()
+
+            continue_waits(waits, hop, d, at)
+
+    def finish_dense():
+        for k in (nz // 2 - 1, nz - 1):
+
+            @pl.when(order_d[k] == at.z)
+            def _(k=k):
+                for p in range(units[0] + 1):
+                    total = piece_of(k, p)
+                    for side, here in enumerate((at.z > 0, at.z < nz - 1)):
+                        slot = at.z if side == 0 else nz
+
+                        @pl.when(here)
+                        def _(total=total, slot=slot, p=p):
+                            arrive(inbox_of(slot, p), zd_recv.at[slot, p])
+                            add_into(total, inbox_of(slot, p))
+
+                write_out(0, xs[0].at[k, 0])
+                write_out(1, ys[1].at[k, 0])
 
     def write_out(a, total):
-        value = total[...].astype(F32)
-        if a == e_in:
-            for f in range(panels):
-                outs[a][:, f * width : (f + 1) * width] = value[f]
-        else:
-            outs[a][...] = value.reshape(outs[a].shape)
-
-    def x_and_line(kind, k):
+        if a != e_in:
+            outs[a][...] = total[...].astype(F32).reshape(outs[a].shape)
+            return
+        for j, x in enumerate(at.other_x()):
+            send(total.at[pl.ds(x * panels, panels)], ex_in.at[nx - 2 - j], ex_send.at[j], ex_recv.at[nx - 2 - j], x=x)
+
+    def finish_expert_in():
+        for j in range(nx - 1):
+            arrive(ex_in.at[j], ex_recv.at[j])
+        total = cores[e_in].at[nz - 1]
+        for x in range(nx):
+            for u in range(panels):
+                value = None
+                for j, other in enumerate(at.other_x()):
+                    value = ex_in[j, u] if value is None else jnp.where(other == x, ex_in[j, u], value)
+                mine = total[pl.ds(at.x * panels + u, 1)][0]
+                value = jnp.where(at.x == x, mine.astype(F32), value.astype(F32))
+                for i in range(width // columns):
+                    z = u * (width // columns) + i
+                    outs[e_in][:, (z * nx + x) * columns : (z * nx + x + 1) * columns] = value[:, i * columns : (i + 1) * columns]
+
+    def line(kind, k):
         for a in kind:
-            d = (order_d if a in dense else order_e)[k]
-            total = xs[a].at[k, 0]
-            for j in range(nx - 1):
-                arrive(xs[a].at[k, j], x_recv.at[a, k, j])
-                own = ys[a].at[k, 0, at.x] if a in dense else cores[a].at[k, at.x]
-                add_into(total, xs[a].at[k, j] if j else own)
+            d = order_e[k]
+            total = cores[a].at[k]
             for side in range(2):
                 feeds = (at.z > 0) & (d >= at.z) if side == 0 else (at.z < nz - 1) & (d <= at.z)
                 slot = d if side == 0 else jnp.where(d == at.z, nz, d)
@@ -646,20 +771,9 @@
             def _(hop=hop):
                 hop(1).start()
 
-            @pl.when(d == at.z)
-            def _(a=a, total=total):
+            if k == nz - 1:
                 write_out(a, total)
-
-            def wait(hop=hop, d=d):
-                @pl.when(d < at.z)
-                def _():
-                    hop(-1).wait_send()
-
-                @pl.when(d > at.z)
-                def _():
-                    hop(1).wait_send()
-
-            waits.append(wait)
+            continue_waits(waits, hop, d, at)
 
     def start_act(i):
         for p in range(packs):
@@ -725,53 +839,147 @@
             for z in range(nz):
                 term = jnp.where(at.z == z, total[3], inbox[tail + z])
                 out = term if out is None else out + term
-            (sum_wide, sum_table)[i][...] = out
-
-    count = ny * each
-    row_units = width // unit
-    for k in range(nz):
-        f = order_e[k]
-        here = slots_in[0].reshape(count, width)
-        grad_here = slots_in[1].reshape(count, width)
-
-        def in_rows(start, n, f=f):
-            return jnp.concatenate([big[(start + i) * panels + f] for i in range(n)], axis=0)
-
-        first_out = bases[e_out] + f * row_units
-        inner = jnp.dot(here, in_rows(0, row_units), preferred_element_type=F32)
+            if i == 0:
+                sum_gains[...] = out[: sum_gains.shape[0]]
+                sum_router[...] = out[sum_gains.shape[0] : sum_gains.shape[0] + experts]
+            else:
+                sum_table[...] = out[: sum_table.shape[0], : sum_table.shape[1]]
+
+    dense_events(0)
+    dense_events(1)
+    expert_events(0, (e_out,))
+    send_acts()
+    side_y(0)
+    side_x(0)
+    prepare_bias(rel, table, bias, at.s, tok, group)
+    prepare_masks(lengths, same, causal, at.s, tok, group)
+    hot, dispatch = route_slots(route, experts, each // packs)
+    top = g_ref[...].astype(F32).reshape(packs * tok, width)
+    start_prep()
+    side_y(1)
+    dense_events(2)
+    side_x(1)
+    dense_events(3)
+    expert_events(1, (e_out,))
+    expert_events(2, (e_out,))
+    act_events()
+    expert_events(0, (e_in,))
+    corner_events(1)
+    first_norm()
+    corner_events(0)
+    side_x(2)
+    for a in dense:
+        for z in zs[: nz // 2]:
+            for x in range(nx):
+                for y in range(ny):
+                    arrive(spot(a, z, x, 1 - at.c, y), spread_recv.at[a, z, x, y])
+    side_y(2)
+    keys_and_values(at.z < nz // 2)
+    side_x(3)
+    side_y(3)
+    expert_events(3, (e_out,))
+    corner_events(2)
+    expert_events(1, (e_in,))
+    corner_events(3)
+    for a in dense:
+        for z in zs[nz // 2 :]:
+            for x in range(nx):
+                for y in range(ny):
+                    arrive(spot(a, z, x, 1 - at.c, y), spread_recv.at[a, z, x, y])
+    project(n1, w, 0, q)
+    keys_and_values(at.z >= nz // 2)
+    attend_pairs(q, k_, v, bias, causal, pr_self, mixed)
+    add_product(h1, mixed, w, 6)
+    rms_rows(h1, gains[1:2], n2, packs * tok)
+    project(n2, w, 3, qc)
+    attend_pairs(qc, kc, vc, None, same, pr_cross, cross_mixed)
+    h2[...] = h1[...]
+    add_product(h2, cross_mixed, w, 7)
+    rms_rows(h2, gains[2:3], n3, packs * tok)
+    slots_out[0] = by_slot(dispatch, n3[...])
+    send_slots(0)
+    logits = lax.dot_general(n3[...], router_t[...], (((1,), (1,)), ((), ())), preferred_element_type=F32)
+    raised = jnp.exp(logits - jnp.max(logits, axis=1, keepdims=True))
+    routing = raised / jnp.sum(raised, axis=1, keepdims=True)
+    gate = jnp.sum(routing * hot, axis=1, keepdims=True)
+    slots_out[1] = by_slot(dispatch, (gate * top).astype(BF))
+    send_slots(1)
+    expert_events(2, (e_in,))
+    for t in range(2):
+        for j, y in enumerate(at.other_y()):
+            here = slots_in.at[t, at.x, y]
+            arrive(here, slot_recv.at[y_sem(t, j)])
+            for i, x in enumerate(at.other_x()):
+                slot_copy(False, here, here, x_sem(t, i, y), x_sem(t, nx - 2 - i, y), x=x)
+    expert_events(3, (e_in,))
+    for t in range(2):
+        for i, x in enumerate(at.other_x()):
+            for y in range(ny):
+                arrive(slots_in.at[t, x, y], slot_recv.at[x_sem(t, i, y)])
+    for a in experts_:
+        for z in range(nz):
+            arrive(pack_of(a, z, 1 - at.c), spread_recv.at[a, z, 0, 0])
+    here = slots_in[0].reshape(nx * count, width)
+    grad_here = slots_in[1].reshape(nx * count, width)
+    for u in range(panels):
+        in_panel = jnp.concatenate([big[place + u] for place in places], axis=0)
+        out_panel = big[pl.ds(bases[e_out] + u * row_units, row_units)].reshape(width, width)
+        inner = jnp.dot(here, in_panel, preferred_element_type=F32)
         hidden, slope = gelu_both(inner)
-        hid[...] = hidden.astype(BF)
-        out_panel = big[pl.ds(first_out, row_units)].reshape(width, width)
+        hid[u] = hidden.astype(BF)
         grad_hidden = lax.dot_general(grad_here, out_panel, (((1,), (1,)), ((), ())), preferred_element_type=F32)
-        gin_[...] = (grad_hidden * slope).astype(BF)
-        result = jnp.dot(hid[...], out_panel, preferred_element_type=F32)
-        grad_slots = lax.dot_general(gin_[...], in_rows(0, row_units), (((1,), (1,)), ((), ())), preferred_element_type=F32)
-        if k:
+        gin_[u] = (grad_hidden * slope).astype(BF)
+        result = jnp.dot(hid[u], out_panel, preferred_element_type=F32).reshape(nx, ny, each, width)
+        grad_slots = lax.dot_general(gin_[u], in_panel, (((1,), (1,)), ((), ())), preferred_element_type=F32)
+        grad_slots = grad_slots.reshape(nx, ny, each, width)
+        if u:
             slots_acc[0] += result
             slots_acc[1] += grad_slots
         else:
             slots_acc[0] = result
             slots_acc[1] = grad_slots
-        grad = lax.dot_general(hid[...], grad_here, (((0,), (0,)), ((), ())), preferred_element_type=F32).astype(BF)
-        ge[pl.ds(first_out, row_units)] = grad.reshape(row_units, unit, width)
+    for wait in waits:
+        wait()
+    waits.clear()
+    for y in [*at.other_y(), at.y]:
+        for t in range(2):
+            for j, x in enumerate(at.other_x()):
+                ret_out[t, j, y] = slots_acc[t, x, y].astype(BF)
+                slot_copy(True, ret_out.at[t, j, y], ret_in.at[t, nx - 2 - j, y], ret_sem(t, j, y),
+                          ret_sem(t, nx - 2 - j, y), x=x)
+    for u in range(panels):
+        grad = lax.dot_general(hid[u], grad_here, (((0,), (0,)), ((), ())), preferred_element_type=F32).astype(BF)
+        ge[pl.ds(bases[e_out] + u * row_units, row_units)] = grad.reshape(row_units, unit, width)
+    for k in range(nz):
         start_expert(e_out, k)
-        grad = lax.dot_general(here, gin_[...], (((0,), (0,)), ((), ())), preferred_element_type=F32).astype(BF)
-        for i in range(row_units):
-            ge[i * panels + f] = grad[i * unit : (i + 1) * unit]
-        if k:
-            core_expert(e_out, k - 1)
-    for wait in swap_waits:
-        wait()
-    for t in range(2):
-        slots_out[t] = slots_acc[t].astype(BF).reshape(ny, each, width)
-        swap(2 + t, slots_out, back_in)
+    for u in range(panels):
+        grad = lax.dot_general(here, gin_[u], (((0,), (0,)), ((), ())), preferred_element_type=F32).astype(BF)
+        for i, place in enumerate(places):
+            ge[place + u] = grad[i * unit : (i + 1) * unit]
     for k in range(nz):
         start_expert(e_in, k)
-    core_expert(e_out, nz - 1)
+    core_expert(e_out, 0)
+    line((e_out,), 0)
+    core_expert(e_out, 2)
+    for wait in slot_waits:
+        wait()
+    for j, y in enumerate(at.other_y()):
+        for t in range(2):
+            slots_out[t, y] = summed(t, y)
+            slot_copy(True, slots_out.at[t, y], back_in.at[t, at.y], y_sem(2 + t, j), y_sem(2 + t, ny - 2 - j), y=y)
+    core_expert(e_out, 3)
+    core_expert(e_in, 1)
+    core_expert(e_out, 1)
     core_expert(e_in, 0)
+    core_expert(e_in, 3)
+    line((e_in,), 0)
+    core_expert(e_in, 2)
+    free_experts()
     for t in range(2):
-        swapped(2 + t, back_in)
-        back_in[t, at.y] = slots_out[t, at.y]
+        back_in[t, at.y] = summed(t, at.y)
+    for t in range(2):
+        for j, y in enumerate(at.other_y()):
+            arrive(back_in.at[t, y], slot_recv.at[y_sem(2 + t, j)])
     combined = jnp.dot(dispatch, back_in[0].reshape(count, width), preferred_element_type=F32)
     rows_out = (h2[...] + gate * combined).astype(BF)
     for p in range(packs):
@@ -787,80 +995,75 @@
     )
     grad_n3 = jnp.dot(dispatch, back_in[1].reshape(count, width), preferred_element_type=F32)
     for e in range(experts):
-        grad_n3 = grad_n3 + grad_logits[:, e : e + 1] * router_t[e : e + 1, :]
+        grad_n3 = grad_n3 + grad_logits[:, e : e + 1] * router_t[e : e + 1, :].astype(F32)
     gn[...] = grad_n3
     grad_x[...] = top
     norm_back_rows(h2, gains[2:3], gn, grad_x, gain_row)
     wide_sum[0, 2:3, :] = gain_row[...]
     gb[...] = grad_x[...].astype(BF)
-
     product_t(gb, w, 7, ga)
-    core_expert(e_in, 1)
-    core_expert(e_in, 2)
-    core_expert(e_in, 3)
-    free_experts()
+    attend_pairs_back(qc, kc, vc, pr_cross, ga, gq, gk, gv, None)
     outer_product(cross_mixed, gb, big, 7)
-    x_and_line((e_out,), 0)
-    attend_pairs_back(qc, kc, vc, pr_cross, ga, gq, gk, gv, None)
     outer_product(n2, gq, big, 3)
     outer_product(mo, gk, big, 4)
     outer_product(mo, gv, big, 5)
     pl.semaphore_wait(free_sem, 1)
-    for k in range(nz // 2):
-        start_dense(k)
-    x_and_line((e_out,), 1)
+    start_dense(0)
+    start_dense(1)
     two_products_t(gk, 4, gv, 5, w, kc)
+    line((e_in,), 1)
+    line((e_in,), 2)
+    first_dense(0)
     start_act(0)
     product_t(gq, w, 3, gn)
     norm_back_rows(h1, gains[1:2], gn, grad_x, gain_row)
     wide_sum[0, 1:2, :] = gain_row[...]
     gb[...] = grad_x[...].astype(BF)
     product_t(gb, w, 6, ga)
-    core_dense(0)
-    x_and_line((e_out,), 2)
-    outer_product(mixed, gb, big, 6)
     core_act(0)
-    core_dense(1)
-    x_and_line((e_out,), 3)
+    first_dense(1)
     attend_pairs_back(q, k_, v, pr_self, ga, gq, gk, gv, diagonal)
-    x_and_line((e_in,), 0)
+    two_products_t(gk, 1, gv, 2, w, k_)
+    start_act(1)
     outer_product(n1, gq, big, 0)
     outer_product(n1_all, gk, big, 1)
     outer_product(n1_all, gv, big, 2)
-    for k in range(nz // 2, nz):
-        start_dense(k)
-    y_dense(0)
-    two_products_t(gk, 1, gv, 2, w, k_)
-    start_act(1)
-    x_and_line((e_in,), 1)
-    y_dense(1)
-    for k in range(nz // 2, nz):
-        core_dense(k)
     core_act(1)
+    line((e_out,), 1)
+    line((e_out,), 2)
+    outer_product(mixed, gb, big, 6)
+    start_dense(2)
+    second_dense(0)
     product_t(gq, w, 0, gn)
-    table_sum[0] = table_grad(rel, diagonal, at.s, tok, group, buckets)
-    x_and_line((e_in,), 2)
-    x_and_line((e_in,), 3)
-    x_act(0)
-    x_and_line(dense, 0)
+    table_sum[0] = table_grad(rel, diagonal, at.s, tok, group)
+    first_dense(2)
+    second_dense(1)
     x_act(1)
     for p in range(packs):
         h1[pl.ds(p * tok, tok), :] = x_ref[p].astype(F32)
     norm_back_rows(h1, gains[0:1], gn, grad_x, gain_row)
     wide_sum[0, 0:1, :] = gain_row[...]
     start_small(0)
-    y_dense(2)
+    start_dense(3)
+    line_dense(0)
     end_small(0)
     start_small(1)
-    x_and_line(dense, 1)
+    second_dense(2)
+    line((e_in,), 3)
     end_small(1)
     start_small(2)
-    y_dense(3)
+    first_dense(3)
+    line_dense(1)
+    line_dense(2)
+    line((e_out,), 3)
     end_small(2)
     start_line()
-    x_and_line(dense, 2)
+    second_dense(3)
+    x_act(0)
+    line_dense(3)
+    finish_expert_in()
     end_line()
-    x_and_line(dense, 3)
+    finish_dense()
     for wait in waits:
         wait()
 
@@ -875,16 +1078,39 @@
     nz, ns, ny, packs, tok, width = shapes_of(layer_input, routes, attn_in, attn_out, expert_in, expert_out)
     unit, hidden = expert_in.shape[1:]
     capacity = (5 * tok + 4 * ny - 1) // (4 * ny)
+    nx = ns // 2
     return (
         unit % 16 == 0
         and tok % 16 == 0
         and packs * capacity % 16 == 0
         and attn_in.shape[0] % unit == 0
         and attn_out.shape[0] % unit == 0
+        and expert_out.shape[1] % (unit * nx) == 0
         and width % (2 * unit) == 0
-        and hidden == nz * width
+        and hidden % (nx * width) == 0
+        and width % (hidden // (nz * nx)) == 0
+        and hidden // (nz * nx) % 128 == 0
+        and expert_out.shape[1] * nz * ns == hidden
+        and expert_out.shape[1] * width == hidden * unit
         and expert_in.shape[0] == 1
     )
+
+
+def deliver_body(*refs):
+    count = len(refs) // 2
+    for i in range(count):
+        refs[count + i][...] = refs[i][...]
+
+
+def deliver(arrays):
+    vmem = pl.BlockSpec(memory_space=pltpu.VMEM)
+    return pl.pallas_call(
+        deliver_body,
+        out_shape=[jax.ShapeDtypeStruct(a.shape, a.dtype) for a in arrays],
+        in_specs=[vmem] * len(arrays),
+        out_specs=[vmem] * len(arrays),
+        name="deliver",
+    )(*arrays)
 
 
 def layer_kernel(layer_input, memory, cotangent, routes, doc_lengths, rel_buckets, gains, bias_table, router,
@@ -893,12 +1119,15 @@
     nx = ns // 2
     group, pairs = ns * tok, width // 128
     unit = expert_in.shape[1]
-    panels = expert_in.shape[2] // width
+    hidden = expert_in.shape[2]
+    panels = hidden // width // nx
+    pack_units = nx * panels
     experts, buckets = router.shape[1], bias_table.shape[0]
     each = packs * ((5 * tok + 4 * experts - 1) // (4 * experts))
     tall = nz * ns
-    units = (attn_in.shape[0] // unit, attn_out.shape[0] // unit, panels, panels)
+    units = (attn_in.shape[0] // unit, attn_out.shape[0] // unit)
     total = tall * ny * (units[0] + units[1])
+    grads = max(4 * nz * pack_units, total // 2)
     extra = -(-(3 + experts) // 8) * 8
     small = ny + nx - 1 + nz
     mine, every = packs * tok, packs * group
@@ -909,7 +1138,7 @@
     low = lambda *shape: pltpu.VMEM(shape, BF)
     wide = lambda *shape: pltpu.VMEM(shape, F32)
     shape = lambda *dims: jax.ShapeDtypeStruct(dims, F32)
-    out_rows, g0, g1, g2, g3, grad_x, grad_mem, sums, table = pl.pallas_call(
+    results = pl.pallas_call(
         layer_body,
         out_shape=[
             jax.ShapeDtypeStruct((packs, tok, width), BF),
@@ -919,19 +1148,24 @@
             shape(*expert_out.shape[1:]),
             shape(mine, width),
             shape(mine, width),
-            shape(extra, width),
-            shape(buckets, 128),
+            shape(3, width),
+            shape(experts, width),
+            shape(2 * pairs, buckets),
         ],
         in_specs=[smem, *[vmem] * 8, any_, any_, vmem, any_],
-        out_specs=[vmem] * 9,
+        out_specs=[vmem] * 10,
         scratch_shapes=[
             low(total, unit, width),
             low(total, unit, width),
-            low(2 * tall * panels, unit, width),
-            *[low(nz, nx, panels, unit, width)] * 2,
-            *[low(nz, ny - 1, nx, u, unit, width) for u in units[:2]],
-            *[low(nz, nx - 1, u, unit, width) for u in units],
-            *[low(nz + 1, u, unit, width) for u in units],
+            low(grads, unit, width),
+            low(nx, panels, unit, width),
+            *[low(nz, pack_units, unit, width)] * 2,
+            low(nz, ny - 1, nx, units[0], unit, width),
+            low(nz, ny - 1, units[1], unit, width),
+            low(nz, nx - 1, units[0], unit, width),
+            low(nz, nx - 1, ny * units[1], unit, width),
+            low(nx - 1, panels, unit, width),
+            *[low(nz + 1, u, unit, width) for u in (*units, pack_units, pack_units)],
             *[low(every, width)] * 8,
             *[low(mine, width)] * 10,
             *[low(packs, pairs, 2 * tok, group)] * 2,
@@ -939,42 +1173,50 @@
             wide(pairs, 2 * tok, group),
             wide(packs, tok, group),
             wide(packs, tok, group),
-            wide(128, group + 128),
+            wide(16, group + 128),
             wide(1, width),
             low(2, packs, nx, tok, width),
             low(2, nx - 1, packs, tok, width),
             wide(4, extra, width),
-            wide(4, buckets, 128),
+            wide(4, 16, 128),
             wide(small, extra, width),
-            wide(small, buckets, 128),
+            wide(small, 16, 128),
             low(2, ny, each, width),
+            low(2, nx, ny, each, width),
+            wide(2, nx, ny, each, width),
+            low(2, nx - 1, ny, each, width),
+            low(2, nx - 1, ny, each, width),
             low(2, ny, each, width),
-            wide(2, ny * each, width),
-            low(2, ny, each, width),
-            low(ny * each, width),
-            low(ny * each, width),
+            low(panels, nx * ny * each, width),
+            low(panels, nx * ny * each, width),
             dma((2, packs, 2 * nx)),
             dma((2, packs, nx, 2)),
+            dma((nx - 1,)),
+            dma((nx,)),
             dma((4, nz, 2)),
-            dma((4, nz, nx - 1 + (ny - 1) * (1 + nx))),
+            dma((2, nz, nx - 1 + ny - 1 + max((ny - 1) * nx, (nx - 1) * ny))),
             dma((4, nz, nx, ny)),
             dma((4, nz, nx, ny)),
             dma((4, nz, nx, ny)),
             dma((6, packs)),
             dma((4, nz, nx)),
             dma((4, nz, nx)),
-            dma((2, nz, ny - 1, nx)),
-            dma((2, nz, ny - 1, nx)),
-            dma((4, nz, nx - 1)),
-            dma((4, nz, nx - 1)),
+            dma((nz, ny - 1, nx + 1, units[0])),
+            dma((nz, ny - 1, nx + 1, units[0])),
+            dma((nz, nx - 1, units[0] + 1)),
+            dma((nz, nx - 1, units[0] + 1)),
+            dma((nx - 1,)),
+            dma((nx - 1,)),
             dma((4, nz)),
             dma((4, nz + 1)),
+            dma((nz, units[0] + 1)),
+            dma((nz + 1, units[0] + 1)),
             dma((2, packs + 1, nx)),
             dma((2, packs + 1, nx)),
             dma((2, small)),
             dma((2, small)),
-            dma((4, ny - 1)),
-            dma((4, ny - 1)),
+            dma((4 * (ny - 1) + 4 * (nx - 1) * ny,)),
+            dma((4 * (ny - 1) + 4 * (nx - 1) * ny,)),
             pltpu.SemaphoreType.REGULAR,
         ],
         compiler_params=pltpu.CompilerParams(
@@ -985,25 +1227,26 @@
         doc_lengths[:, 0, 0],
         rel_buckets.reshape(1, -1),
         gains,
-        bias_table,
-        router.T.astype(F32),
-        routes.reshape(mine, 1),
+        bias_table.T,
+        router.T,
+        routes.reshape(packs, 1, tok),
         layer_input[:, 0, 0],
         memory[:, 0, 0],
         cotangent[:, 0, 0],
         attn_in.reshape(units[0], unit, width),
         attn_out.reshape(units[1], unit, width),
         expert_in[0],
-        expert_out.reshape(panels, unit, width),
+        expert_out.reshape(pack_units, unit, width),
     )
+    out_rows, g0, g1, g2, g3, grad_x, grad_mem, gains_sum, router_sum, table_sum = deliver(results)
     spread = (packs, 1, 1, tok, width)
     return (
         out_rows.reshape(spread),
         grad_x.reshape(spread),
         grad_mem.reshape(spread),
-        sums[:3],
-        table[:, : 2 * pairs],
-        sums[3 : 3 + experts].T,
+        gains_sum,
+        table_sum.T,
+        router_sum.T,
         g0,
         g1,
         g2[None],

time: 234 us -> 179 us (0.76)
  Pallas kernels: 217 us -> 178 us
  local copies, waits for them, and re-layouts: 13.9 us -> 0 us
    pallas_call x1, Pallas kernels: 217 us -> 175 us  [layer_kernel(): pl.pallas_call(layer_body, out_shape=[jax.ShapeDtypeStruct((packs, tok, w...]
    unnamed x28 -> x0, local copies, waits for them, and re-layouts: 10.4 us -> none
    pallas_call x0 -> x1, Pallas kernels: none -> 3.3 us  [deliver(): pl.pallas_call(deliver_body, out_shape=[jax.ShapeDtypeStruct(a.shape, a.d...]
where the time goes in v4:
time: 179 us
  Pallas kernels  178 us (99%)
    pallas_call x1, Pallas kernels, layer_kernel(): pl.pallas_call(layer_body, out_shape=[jax.ShapeDtypeStruct((packs, tok, w...  175 us

profile of v4, /device:TPU:12, one launch (start us, length us, event | category | flops | bytes accessed | tf_op | source)
XLA Modules:
  0.0 179.1 jit_solution(17492559844383898520)
XLA Ops:
  0.6 175.0 %layer.1 = (bf16[2,64,768]{2,1,0:T(8,128)(2,1)}, f32[144,768]{1,0:T(8,128)}, f32[48,768]{1,0:T(8,128)}, f32[48,3072]{1,0:T(8,128)}, f32[192,768]{1,0:T(8,128)}, ...) custom-call(s32[2,3]{1,0:T(2,128)} %bitcast.36, ...), custom_call_target="tpu_custom_call" | custom-call | tf_op jit(solution)/shard_map/layer/pallas_call | solution.py:1141
  175.7 3.3 %deliver.1 = (bf16[2,64,768]{2,1,0:T(8,128)(2,1)}, f32[144,768]{1,0:T(8,128)}, f32[48,768]{1,0:T(8,128)}, f32[48,3072]{1,0:T(8,128)}, f32[192,768]{1,0:T(8,128)}...) custom-call(bf16[2,64,768]{2,1,0:T(8,128)(2,1)} %get-tuple-element.30., ...), custom_call_target="tpu_custom_call" | custom-call | tf_op jit(solution)/shard_map/deliver/pallas_call | solution.py:1107

commit v5 on v4

--- a/solution.py
+++ b/solution.py
@@ -363,12 +363,40 @@
 
     def send(*args, **where):
         one = remote(*args, **where)
-        one.start()
+        if acts_now[0]:
+            one.start()
         waits.append(one.wait_send)
-        return one
+
+    acts_now = [True]
+
+    def at_planes(ends, step, last):
+        between = (at.z > 0) & (at.z < nz - 1)
+        mark = len(waits)
+
+        @pl.when(jnp.logical_not(between) if ends else between)
+        def _():
+            step()
+
+        del waits[mark:]
+        if last:
+            acts_now[0] = False
+            step()
+            acts_now[0] = True
+
+    def add(total, other):
+        if acts_now[0]:
+            add_into(total, other)
+
+    def start_when(pred, make):
+        if acts_now[0]:
+
+            @pl.when(pred)
+            def _():
+                make().start()
 
     def arrive(ref, sem):
-        pltpu.make_async_copy(ref, ref, sem).wait()
+        if acts_now[0]:
+            pltpu.make_async_copy(ref, ref, sem).wait()
 
     def spot(a, z, x, c, y):
         index = ((z * nx + x) * 2 + c) * ny + y
@@ -407,13 +435,8 @@
         def one(side):
             return remote(src, dst, line_send.at[a, z, side], sem, z=at.z + 2 * side - 1)
 
-        @pl.when(left)
-        def _():
-            one(0).start()
-
-        @pl.when(right)
-        def _():
-            one(1).start()
+        start_when(left, lambda: one(0))
+        start_when(right, lambda: one(1))
 
         def wait():
             @pl.when(left)
@@ -680,29 +703,24 @@
                 for j in range(nx - 1):
                     piece = xs[0].at[k, j, pl.ds(p, 1)]
                     arrive(piece, x_recv.at[k, j, p])
-                    add_into(total, piece if j else ys[0].at[k, 0, at.x, pl.ds(p, 1)])
+                    add(total, piece if j else ys[0].at[k, 0, at.x, pl.ds(p, 1)])
             else:
                 for j in range(ny - 1):
                     arrive(ys[1].at[k, j], y_recv.at[k, j, nx, 0])
-                    add_into(total, ys[1].at[k, j] if j else xs[1].at[k, 0, pl.ds(at.y * units[1], units[1])])
+                    add(total, ys[1].at[k, j] if j else xs[1].at[k, 0, pl.ds(at.y * units[1], units[1])])
             for side in range(2):
 
                 @pl.when((at.z > 0) & (d > at.z) if side == 0 else (at.z < nz - 1) & (d < at.z))
                 def _(total=total, p=p):
                     arrive(inbox_of(d, p), zd_recv.at[d, p])
-                    add_into(total, inbox_of(d, p))
+                    add(total, inbox_of(d, p))
 
             def hop(to, total=total, p=p):
                 slot = d if to > 0 else jnp.where(d == at.z - 1, nz, d)
                 return remote(total, inbox_of(slot, p), zd_send.at[k, p], zd_recv.at[slot, p], z=at.z + to)
 
-            @pl.when(d < at.z)
-            def _(hop=hop):
-                hop(-1).start()
-
-            @pl.when(d > at.z)
-            def _(hop=hop):
-                hop(1).start()
+            start_when(d < at.z, functools.partial(hop, -1))
+            start_when(d > at.z, functools.partial(hop, 1))
 
             continue_waits(waits, hop, d, at)
 
@@ -726,7 +744,8 @@
 
     def write_out(a, total):
         if a != e_in:
-            outs[a][...] = total[...].astype(F32).reshape(outs[a].shape)
+            if acts_now[0]:
+                outs[a][...] = total[...].astype(F32).reshape(outs[a].shape)
             return
         for j, x in enumerate(at.other_x()):
             send(total.at[pl.ds(x * panels, panels)], ex_in.at[nx - 2 - j], ex_send.at[j], ex_recv.at[nx - 2 - j], x=x)
@@ -757,19 +776,14 @@
                 @pl.when(feeds)
                 def _(a=a, slot=slot, total=total):
                     arrive(zs_[a].at[slot], z_recv.at[a, slot])
-                    add_into(total, zs_[a].at[slot])
+                    add(total, zs_[a].at[slot])
 
             def hop(to, a=a, total=total, d=d):
                 slot = d if to > 0 else jnp.where(d == at.z - 1, nz, d)
                 return remote(total, zs_[a].at[slot], z_send.at[a, k], z_recv.at[a, slot], z=at.z + to)
 
-            @pl.when(d < at.z)
-            def _(hop=hop):
-                hop(-1).start()
-
-            @pl.when(d > at.z)
-            def _(hop=hop):
-                hop(1).start()
+            start_when(d < at.z, functools.partial(hop, -1))
+            start_when(d > at.z, functools.partial(hop, 1))
 
             if k == nz - 1:
                 write_out(a, total)
@@ -846,41 +860,48 @@
                 sum_table[...] = out[: sum_table.shape[0], : sum_table.shape[1]]
 
     dense_events(0)
-    dense_events(1)
-    expert_events(0, (e_out,))
-    send_acts()
-    side_y(0)
-    side_x(0)
+    start_prep()
     prepare_bias(rel, table, bias, at.s, tok, group)
     prepare_masks(lengths, same, causal, at.s, tok, group)
     hot, dispatch = route_slots(route, experts, each // packs)
     top = g_ref[...].astype(F32).reshape(packs * tok, width)
-    start_prep()
+    at_planes(False, lambda: dense_events(1), False)
+    at_planes(True, lambda: dense_events(1), True)
+    side_x(0)
+    at_planes(False, lambda: dense_events(2), False)
+    side_y(0)
+    expert_events(0, (e_out,))
+    send_acts()
+    at_planes(False, lambda: dense_events(3), False)
+    at_planes(True, lambda: dense_events(2), True)
+    expert_events(0, (e_in,))
+    side_x(1)
+    corner_events(0)
+    at_planes(True, lambda: dense_events(3), True)
     side_y(1)
-    dense_events(2)
-    side_x(1)
-    dense_events(3)
-    expert_events(1, (e_out,))
-    expert_events(2, (e_out,))
+    at_planes(False, lambda: expert_events(1, (e_in,)), False)
+    at_planes(False, lambda: expert_events(1, (e_out,)), False)
     act_events()
-    expert_events(0, (e_in,))
+    side_y(2)
+    side_x(2)
+    at_planes(True, lambda: expert_events(1, (e_in,)), True)
+    at_planes(False, lambda: expert_events(2, (e_out,)), False)
+    at_planes(False, lambda: expert_events(2, (e_in,)), False)
+    at_planes(False, lambda: expert_events(3, (e_in,)), False)
+    first_norm()
+    side_x(3)
     corner_events(1)
-    first_norm()
-    corner_events(0)
-    side_x(2)
+    side_y(3)
     for a in dense:
         for z in zs[: nz // 2]:
             for x in range(nx):
                 for y in range(ny):
                     arrive(spot(a, z, x, 1 - at.c, y), spread_recv.at[a, z, x, y])
-    side_y(2)
+    at_planes(True, lambda: expert_events(1, (e_out,)), True)
+    corner_events(2)
     keys_and_values(at.z < nz // 2)
-    side_x(3)
-    side_y(3)
-    expert_events(3, (e_out,))
-    corner_events(2)
-    expert_events(1, (e_in,))
     corner_events(3)
+    at_planes(False, lambda: expert_events(3, (e_out,)), False)
     for a in dense:
         for z in zs[nz // 2 :]:
             for x in range(nx):
@@ -888,6 +909,7 @@
                     arrive(spot(a, z, x, 1 - at.c, y), spread_recv.at[a, z, x, y])
     project(n1, w, 0, q)
     keys_and_values(at.z >= nz // 2)
+    at_planes(True, lambda: expert_events(2, (e_out,)), True)
     attend_pairs(q, k_, v, bias, causal, pr_self, mixed)
     add_product(h1, mixed, w, 6)
     rms_rows(h1, gains[1:2], n2, packs * tok)
@@ -904,21 +926,25 @@
     gate = jnp.sum(routing * hot, axis=1, keepdims=True)
     slots_out[1] = by_slot(dispatch, (gate * top).astype(BF))
     send_slots(1)
-    expert_events(2, (e_in,))
+    at_planes(True, lambda: expert_events(3, (e_out,)), True)
     for t in range(2):
         for j, y in enumerate(at.other_y()):
             here = slots_in.at[t, at.x, y]
             arrive(here, slot_recv.at[y_sem(t, j)])
             for i, x in enumerate(at.other_x()):
                 slot_copy(False, here, here, x_sem(t, i, y), x_sem(t, nx - 2 - i, y), x=x)
-    expert_events(3, (e_in,))
+    at_planes(True, lambda: expert_events(2, (e_in,)), True)
+    at_planes(True, lambda: expert_events(3, (e_in,)), True)
+    for a in experts_:
+        for z in range(nz):
+            arrive(pack_of(a, z, 1 - at.c), spread_recv.at[a, z, 0, 0])
     for t in range(2):
         for i, x in enumerate(at.other_x()):
             for y in range(ny):
                 arrive(slots_in.at[t, x, y], slot_recv.at[x_sem(t, i, y)])
-    for a in experts_:
-        for z in range(nz):
-            arrive(pack_of(a, z, 1 - at.c), spread_recv.at[a, z, 0, 0])
+    for wait in waits:
+        wait()
+    waits.clear()
     here = slots_in[0].reshape(nx * count, width)
     grad_here = slots_in[1].reshape(nx * count, width)
     for u in range(panels):
@@ -938,9 +964,6 @@
         else:
             slots_acc[0] = result
             slots_acc[1] = grad_slots
-    for wait in waits:
-        wait()
-    waits.clear()
     for y in [*at.other_y(), at.y]:
         for t in range(2):
             for j, x in enumerate(at.other_x()):
@@ -948,32 +971,34 @@
                 slot_copy(True, ret_out.at[t, j, y], ret_in.at[t, nx - 2 - j, y], ret_sem(t, j, y),
                           ret_sem(t, nx - 2 - j, y), x=x)
     for u in range(panels):
-        grad = lax.dot_general(hid[u], grad_here, (((0,), (0,)), ((), ())), preferred_element_type=F32).astype(BF)
-        ge[pl.ds(bases[e_out] + u * row_units, row_units)] = grad.reshape(row_units, unit, width)
-    for k in range(nz):
-        start_expert(e_out, k)
-    for u in range(panels):
         grad = lax.dot_general(here, gin_[u], (((0,), (0,)), ((), ())), preferred_element_type=F32).astype(BF)
         for i, place in enumerate(places):
             ge[place + u] = grad[i * unit : (i + 1) * unit]
     for k in range(nz):
         start_expert(e_in, k)
-    core_expert(e_out, 0)
-    line((e_out,), 0)
-    core_expert(e_out, 2)
+    for u in range(panels):
+        grad = lax.dot_general(hid[u], grad_here, (((0,), (0,)), ((), ())), preferred_element_type=F32).astype(BF)
+        ge[pl.ds(bases[e_out] + u * row_units, row_units)] = grad.reshape(row_units, unit, width)
+    for k in range(nz):
+        start_expert(e_out, k)
+    core_expert(e_in, 0)
+    at_planes(True, lambda: line((e_in,), 0), False)
     for wait in slot_waits:
         wait()
     for j, y in enumerate(at.other_y()):
         for t in range(2):
             slots_out[t, y] = summed(t, y)
             slot_copy(True, slots_out.at[t, y], back_in.at[t, at.y], y_sem(2 + t, j), y_sem(2 + t, ny - 2 - j), y=y)
+    core_expert(e_out, 0)
+    core_expert(e_in, 3)
+    core_expert(e_in, 2)
+    at_planes(True, lambda: line((e_out,), 0), False)
+    core_expert(e_in, 1)
+    at_planes(True, lambda: line((e_in,), 1), False)
+    core_expert(e_out, 1)
     core_expert(e_out, 3)
-    core_expert(e_in, 1)
-    core_expert(e_out, 1)
-    core_expert(e_in, 0)
-    core_expert(e_in, 3)
-    line((e_in,), 0)
-    core_expert(e_in, 2)
+    at_planes(True, lambda: line((e_in,), 2), False)
+    core_expert(e_out, 2)
     free_experts()
     for t in range(2):
         back_in[t, at.y] = summed(t, at.y)
@@ -1001,67 +1026,77 @@
     norm_back_rows(h2, gains[2:3], gn, grad_x, gain_row)
     wide_sum[0, 2:3, :] = gain_row[...]
     gb[...] = grad_x[...].astype(BF)
+    at_planes(False, lambda: line((e_in,), 0), True)
     product_t(gb, w, 7, ga)
     attend_pairs_back(qc, kc, vc, pr_cross, ga, gq, gk, gv, None)
-    outer_product(cross_mixed, gb, big, 7)
     outer_product(n2, gq, big, 3)
     outer_product(mo, gk, big, 4)
     outer_product(mo, gv, big, 5)
+    outer_product(cross_mixed, gb, big, 7)
     pl.semaphore_wait(free_sem, 1)
     start_dense(0)
-    start_dense(1)
-    two_products_t(gk, 4, gv, 5, w, kc)
-    line((e_in,), 1)
-    line((e_in,), 2)
-    first_dense(0)
-    start_act(0)
     product_t(gq, w, 3, gn)
     norm_back_rows(h1, gains[1:2], gn, grad_x, gain_row)
     wide_sum[0, 1:2, :] = gain_row[...]
     gb[...] = grad_x[...].astype(BF)
     product_t(gb, w, 6, ga)
-    core_act(0)
+    at_planes(False, lambda: line((e_in,), 1), True)
+    first_dense(0)
+    start_dense(1)
+    at_planes(False, lambda: line((e_in,), 2), True)
+    at_planes(True, lambda: line((e_out,), 1), False)
+    at_planes(True, lambda: line((e_out,), 2), False)
+    two_products_t(gk, 4, gv, 5, w, kc)
+    at_planes(False, lambda: line((e_out,), 0), True)
+    start_act(0)
     first_dense(1)
     attend_pairs_back(q, k_, v, pr_self, ga, gq, gk, gv, diagonal)
+    second_dense(0)
+    at_planes(False, lambda: line((e_in,), 3), False)
     two_products_t(gk, 1, gv, 2, w, k_)
     start_act(1)
+    outer_product(mixed, gb, big, 6)
+    at_planes(False, lambda: line((e_out,), 1), True)
+    table_sum[0] = table_grad(rel, diagonal, at.s, tok, group)
+    at_planes(True, lambda: line((e_in,), 3), True)
     outer_product(n1, gq, big, 0)
     outer_product(n1_all, gk, big, 1)
     outer_product(n1_all, gv, big, 2)
     core_act(1)
-    line((e_out,), 1)
-    line((e_out,), 2)
-    outer_product(mixed, gb, big, 6)
     start_dense(2)
-    second_dense(0)
+    start_dense(3)
+    at_planes(False, lambda: line((e_out,), 2), True)
+    second_dense(1)
     product_t(gq, w, 0, gn)
-    table_sum[0] = table_grad(rel, diagonal, at.s, tok, group)
     first_dense(2)
-    second_dense(1)
+    at_planes(True, lambda: line_dense(0), False)
+    at_planes(False, lambda: line((e_out,), 3), False)
     x_act(1)
     for p in range(packs):
         h1[pl.ds(p * tok, tok), :] = x_ref[p].astype(F32)
     norm_back_rows(h1, gains[0:1], gn, grad_x, gain_row)
     wide_sum[0, 0:1, :] = gain_row[...]
     start_small(0)
-    start_dense(3)
-    line_dense(0)
+    core_act(0)
+    at_planes(False, lambda: line_dense(0), True)
     end_small(0)
     start_small(1)
     second_dense(2)
-    line((e_in,), 3)
     end_small(1)
     start_small(2)
     first_dense(3)
-    line_dense(1)
-    line_dense(2)
-    line((e_out,), 3)
+    finish_expert_in()
+    at_planes(True, lambda: line((e_out,), 3), True)
+    x_act(0)
+    at_planes(False, lambda: line_dense(1), False)
+    at_planes(False, lambda: line_dense(2), False)
+    at_planes(True, lambda: line_dense(1), True)
+    at_planes(True, lambda: line_dense(2), True)
     end_small(2)
     start_line()
     second_dense(3)
-    x_act(0)
-    line_dense(3)
-    finish_expert_in()
+    at_planes(False, lambda: line_dense(3), False)
+    at_planes(True, lambda: line_dense(3), True)
     end_line()
     finish_dense()
     for wait in waits:

time: 179 us -> 172 us (0.961)
  Pallas kernels: 178 us -> 170 us
    pallas_call x1, Pallas kernels: 175 us -> 167 us  [layer_kernel(): pl.pallas_call(layer_body, out_shape=[jax.ShapeDtypeStruct((packs, tok, w...]
where the time goes in v5:
time: 172 us; the launch traced here: 171 us
  Pallas kernels  170 us (99%)
    pallas_call x1, Pallas kernels, layer_kernel(): pl.pallas_call(layer_body, out_shape=[jax.ShapeDtypeStruct((packs, tok, w...  167 us

profile of v5, /device:TPU:12, one launch (start us, length us, event | category | flops | bytes accessed | tf_op | source)
XLA Modules:
  0.0 170.9 jit_solution(7070737832518003175)
XLA Ops:
  0.6 166.8 %layer.1 = (bf16[2,64,768]{2,1,0:T(8,128)(2,1)}, f32[144,768]{1,0:T(8,128)}, f32[48,768]{1,0:T(8,128)}, f32[48,3072]{1,0:T(8,128)}, f32[192,768]{1,0:T(8,128)}, ...) custom-call(s32[2,3]{1,0:T(2,128)} %bitcast.36, ...), custom_call_target="tpu_custom_call" | custom-call | tf_op jit(solution)/shard_map/layer/pallas_call | solution.py:1176
  167.5 3.3 %deliver.1 = (bf16[2,64,768]{2,1,0:T(8,128)(2,1)}, f32[144,768]{1,0:T(8,128)}, f32[48,768]{1,0:T(8,128)}, f32[48,3072]{1,0:T(8,128)}, f32[192,768]{1,0:T(8,128)}...) custom-call(bf16[2,64,768]{2,1,0:T(8,128)(2,1)} %get-tuple-element.30., ...), custom_call_target="tpu_custom_call" | custom-call | tf_op jit(solution)/shard_map/deliver/pallas_call | solution.py:1142

commit v6 on v5

--- a/solution.py
+++ b/solution.py
@@ -157,7 +157,7 @@
         mixed[mine, lanes] = one_pair(out).astype(BF)
         return carry
 
-    lax.fori_loop(0, packs * pairs, body, 0, unroll=6)
+    lax.fori_loop(0, packs * pairs, body, 0, unroll=12)
 
 
 def add_product(total, left, weight, index):
@@ -274,7 +274,7 @@
                 diagonal[pl.ds(2 * j + half, 1), :] += jnp.sum(band, axis=0, keepdims=True)
         return carry
 
-    lax.fori_loop(0, packs * pairs, body, 0, unroll=6)
+    lax.fori_loop(0, packs * pairs, body, 0, unroll=12)
 
 
 def table_grad(rel, diagonal, rank, rows, group):
@@ -650,20 +650,21 @@
     def xs_in_order():
         return [(x, True) for x in at.other_x()] + [(at.x, False)]
 
-    def start_dense(k):
-        for a in dense:
-            for x in range(nx):
-                send(dense_part(a, order_d[k], x, 1 - at.c), dense_core(a, k, x), core_send.at[a, k, x],
+    def start_dense(k, a):
+        for x in range(nx):
+            send(dense_part(a, order_d[k], x, 1 - at.c), dense_core(a, k, x), core_send.at[a, k, x],
                      core_recv.at[a, k, x], c=1 - at.c)
 
-    def first_dense(k):
-        for x, _ in xs_in_order():
-            arrive(dense_core(0, k, x), core_recv.at[0, k, x])
-            add_into(dense_core(0, k, x), dense_part(0, order_d[k], x, at.c))
-            for u in range(units[0]):
-                for j, y in enumerate(at.other_y()):
-                    send(dense_core(0, k, x, y, u), ys[0].at[k, ny - 2 - j, x, pl.ds(u, 1)],
-                         y_send.at[k, j, x, u], y_recv.at[k, ny - 2 - j, x, u], y=y)
+    def first_dense(k, a):
+        if a == 0:
+            for x, _ in xs_in_order():
+                arrive(dense_core(0, k, x), core_recv.at[0, k, x])
+                add_into(dense_core(0, k, x), dense_part(0, order_d[k], x, at.c))
+                for u in range(units[0]):
+                    for j, y in enumerate(at.other_y()):
+                        send(dense_core(0, k, x, y, u), ys[0].at[k, ny - 2 - j, x, pl.ds(u, 1)],
+                             y_send.at[k, j, x, u], y_recv.at[k, ny - 2 - j, x, u], y=y)
+            return
         for x, _ in xs_in_order():
             arrive(dense_core(1, k, x), core_recv.at[1, k, x])
             add_into(dense_core(1, k, x), dense_part(1, order_d[k], x, at.c))
@@ -671,17 +672,19 @@
             send(dense_core(1, k, x), xs[1].at[k, nx - 2 - j], x_send.at[k, j, units[0]],
                  x_recv.at[k, nx - 2 - j, units[0]], x=x)
 
-    def second_dense(k):
-        for x, away in xs_in_order():
-            for u in range(units[0]):
-                total = ys[0].at[k, 0, x, pl.ds(u, 1)]
-                for j in range(ny - 1):
-                    piece = ys[0].at[k, j, x, pl.ds(u, 1)]
-                    arrive(piece, y_recv.at[k, j, x, u])
-                    add_into(total, piece if j else dense_core(0, k, x, at.y, u))
-                if away:
-                    j = lax.rem(x - at.x + nx, nx) - 1
-                    send(total, xs[0].at[k, nx - 2 - j, pl.ds(u, 1)], x_send.at[k, j, u], x_recv.at[k, nx - 2 - j, u], x=x)
+    def second_dense(k, a):
+        if a == 0:
+            for x, away in xs_in_order():
+                for u in range(units[0]):
+                    total = ys[0].at[k, 0, x, pl.ds(u, 1)]
+                    for j in range(ny - 1):
+                        piece = ys[0].at[k, j, x, pl.ds(u, 1)]
+                        arrive(piece, y_recv.at[k, j, x, u])
+                        add_into(total, piece if j else dense_core(0, k, x, at.y, u))
+                    if away:
+                        j = lax.rem(x - at.x + nx, nx) - 1
+                        send(total, xs[0].at[k, nx - 2 - j, pl.ds(u, 1)], x_send.at[k, j, u], x_recv.at[k, nx - 2 - j, u], x=x)
+            return
         for j in range(nx - 1):
             arrive(xs[1].at[k, j], x_recv.at[k, j, units[0]])
             add_into(xs[1].at[k, 0], xs[1].at[k, j] if j else dense_core(1, k, at.x))
@@ -695,9 +698,9 @@
     def inbox_of(slot, p):
         return zs_[0].at[slot, pl.ds(p, 1)] if p < units[0] else zs_[1].at[slot]
 
-    def line_dense(k):
+    def line_dense(k, a):
         d = order_d[k]
-        for p in range(units[0] + 1):
+        for p in range(units[0]) if a == 0 else [units[0]]:
             total = piece_of(k, p)
             if p < units[0]:
                 for j in range(nx - 1):
@@ -861,47 +864,48 @@
 
     dense_events(0)
     start_prep()
+    at_planes(False, lambda: dense_events(1), False)
+    send_acts()
+    side_x(0)
+    side_y(0)
+    at_planes(False, lambda: dense_events(2), False)
+    at_planes(False, lambda: dense_events(3), False)
+    at_planes(True, lambda: dense_events(1), True)
+    expert_events(0, (e_in,))
+    expert_events(0, (e_out,))
+    at_planes(False, lambda: expert_events(1, (e_in,)), False)
     prepare_bias(rel, table, bias, at.s, tok, group)
     prepare_masks(lengths, same, causal, at.s, tok, group)
     hot, dispatch = route_slots(route, experts, each // packs)
     top = g_ref[...].astype(F32).reshape(packs * tok, width)
-    at_planes(False, lambda: dense_events(1), False)
-    at_planes(True, lambda: dense_events(1), True)
-    side_x(0)
-    at_planes(False, lambda: dense_events(2), False)
-    side_y(0)
-    expert_events(0, (e_out,))
-    send_acts()
-    at_planes(False, lambda: dense_events(3), False)
     at_planes(True, lambda: dense_events(2), True)
-    expert_events(0, (e_in,))
+    act_events()
+    at_planes(True, lambda: dense_events(3), True)
+    at_planes(False, lambda: expert_events(2, (e_in,)), False)
+    side_y(1)
+    at_planes(False, lambda: expert_events(1, (e_out,)), False)
     side_x(1)
-    corner_events(0)
-    at_planes(True, lambda: dense_events(3), True)
-    side_y(1)
-    at_planes(False, lambda: expert_events(1, (e_in,)), False)
-    at_planes(False, lambda: expert_events(1, (e_out,)), False)
-    act_events()
     side_y(2)
-    side_x(2)
+    first_norm()
     at_planes(True, lambda: expert_events(1, (e_in,)), True)
     at_planes(False, lambda: expert_events(2, (e_out,)), False)
-    at_planes(False, lambda: expert_events(2, (e_in,)), False)
-    at_planes(False, lambda: expert_events(3, (e_in,)), False)
-    first_norm()
+    corner_events(0)
+    side_x(2)
+    side_y(3)
     side_x(3)
+    at_planes(True, lambda: expert_events(1, (e_out,)), True)
     corner_events(1)
-    side_y(3)
+    at_planes(True, lambda: expert_events(2, (e_in,)), True)
     for a in dense:
         for z in zs[: nz // 2]:
             for x in range(nx):
                 for y in range(ny):
                     arrive(spot(a, z, x, 1 - at.c, y), spread_recv.at[a, z, x, y])
-    at_planes(True, lambda: expert_events(1, (e_out,)), True)
+    at_planes(False, lambda: expert_events(3, (e_out,)), False)
     corner_events(2)
     keys_and_values(at.z < nz // 2)
     corner_events(3)
-    at_planes(False, lambda: expert_events(3, (e_out,)), False)
+    at_planes(False, lambda: expert_events(3, (e_in,)), False)
     for a in dense:
         for z in zs[nz // 2 :]:
             for x in range(nx):
@@ -909,7 +913,6 @@
                     arrive(spot(a, z, x, 1 - at.c, y), spread_recv.at[a, z, x, y])
     project(n1, w, 0, q)
     keys_and_values(at.z >= nz // 2)
-    at_planes(True, lambda: expert_events(2, (e_out,)), True)
     attend_pairs(q, k_, v, bias, causal, pr_self, mixed)
     add_product(h1, mixed, w, 6)
     rms_rows(h1, gains[1:2], n2, packs * tok)
@@ -926,14 +929,14 @@
     gate = jnp.sum(routing * hot, axis=1, keepdims=True)
     slots_out[1] = by_slot(dispatch, (gate * top).astype(BF))
     send_slots(1)
-    at_planes(True, lambda: expert_events(3, (e_out,)), True)
     for t in range(2):
         for j, y in enumerate(at.other_y()):
             here = slots_in.at[t, at.x, y]
             arrive(here, slot_recv.at[y_sem(t, j)])
             for i, x in enumerate(at.other_x()):
                 slot_copy(False, here, here, x_sem(t, i, y), x_sem(t, nx - 2 - i, y), x=x)
-    at_planes(True, lambda: expert_events(2, (e_in,)), True)
+    at_planes(True, lambda: expert_events(2, (e_out,)), True)
+    at_planes(True, lambda: expert_events(3, (e_out,)), True)
     at_planes(True, lambda: expert_events(3, (e_in,)), True)
     for a in experts_:
         for z in range(nz):
@@ -982,7 +985,6 @@
     for k in range(nz):
         start_expert(e_out, k)
     core_expert(e_in, 0)
-    at_planes(True, lambda: line((e_in,), 0), False)
     for wait in slot_waits:
         wait()
     for j, y in enumerate(at.other_y()):
@@ -990,15 +992,15 @@
             slots_out[t, y] = summed(t, y)
             slot_copy(True, slots_out.at[t, y], back_in.at[t, at.y], y_sem(2 + t, j), y_sem(2 + t, ny - 2 - j), y=y)
     core_expert(e_out, 0)
+    at_planes(True, lambda: line((e_out,), 0), False)
     core_expert(e_in, 3)
+    core_expert(e_out, 1)
+    core_expert(e_out, 2)
+    at_planes(True, lambda: line((e_in,), 0), False)
+    at_planes(True, lambda: line((e_out,), 1), False)
+    core_expert(e_out, 3)
     core_expert(e_in, 2)
-    at_planes(True, lambda: line((e_out,), 0), False)
     core_expert(e_in, 1)
-    at_planes(True, lambda: line((e_in,), 1), False)
-    core_expert(e_out, 1)
-    core_expert(e_out, 3)
-    at_planes(True, lambda: line((e_in,), 2), False)
-    core_expert(e_out, 2)
     free_experts()
     for t in range(2):
         back_in[t, at.y] = summed(t, at.y)
@@ -1026,77 +1028,98 @@
     norm_back_rows(h2, gains[2:3], gn, grad_x, gain_row)
     wide_sum[0, 2:3, :] = gain_row[...]
     gb[...] = grad_x[...].astype(BF)
-    at_planes(False, lambda: line((e_in,), 0), True)
     product_t(gb, w, 7, ga)
     attend_pairs_back(qc, kc, vc, pr_cross, ga, gq, gk, gv, None)
     outer_product(n2, gq, big, 3)
     outer_product(mo, gk, big, 4)
     outer_product(mo, gv, big, 5)
+    pl.semaphore_wait(free_sem, 1)
+    start_dense(0, 0)
     outer_product(cross_mixed, gb, big, 7)
-    pl.semaphore_wait(free_sem, 1)
-    start_dense(0)
+    start_dense(0, 1)
+    two_products_t(gk, 4, gv, 5, w, kc)
+    first_dense(0, 0)
+    start_dense(1, 1)
+    first_dense(0, 1)
+    at_planes(True, lambda: line((e_out,), 2), False)
+    at_planes(False, lambda: line((e_in,), 0), True)
     product_t(gq, w, 3, gn)
     norm_back_rows(h1, gains[1:2], gn, grad_x, gain_row)
     wide_sum[0, 1:2, :] = gain_row[...]
+    at_planes(True, lambda: line((e_in,), 1), False)
     gb[...] = grad_x[...].astype(BF)
     product_t(gb, w, 6, ga)
-    at_planes(False, lambda: line((e_in,), 1), True)
-    first_dense(0)
-    start_dense(1)
-    at_planes(False, lambda: line((e_in,), 2), True)
-    at_planes(True, lambda: line((e_out,), 1), False)
-    at_planes(True, lambda: line((e_out,), 2), False)
-    two_products_t(gk, 4, gv, 5, w, kc)
+    first_dense(1, 1)
+    outer_product(mixed, gb, big, 6)
+    start_dense(3, 1)
+    start_dense(2, 1)
+    start_dense(1, 0)
+    attend_pairs_back(q, k_, v, pr_self, ga, gq, gk, gv, diagonal)
+    first_dense(2, 1)
+    first_dense(1, 0)
+    at_planes(True, lambda: line((e_in,), 2), False)
+    second_dense(0, 1)
     at_planes(False, lambda: line((e_out,), 0), True)
-    start_act(0)
-    first_dense(1)
-    attend_pairs_back(q, k_, v, pr_self, ga, gq, gk, gv, diagonal)
-    second_dense(0)
-    at_planes(False, lambda: line((e_in,), 3), False)
+    first_dense(3, 1)
     two_products_t(gk, 1, gv, 2, w, k_)
     start_act(1)
-    outer_product(mixed, gb, big, 6)
-    at_planes(False, lambda: line((e_out,), 1), True)
-    table_sum[0] = table_grad(rel, diagonal, at.s, tok, group)
-    at_planes(True, lambda: line((e_in,), 3), True)
     outer_product(n1, gq, big, 0)
     outer_product(n1_all, gk, big, 1)
     outer_product(n1_all, gv, big, 2)
+    table_sum[0] = table_grad(rel, diagonal, at.s, tok, group)
     core_act(1)
-    start_dense(2)
-    start_dense(3)
-    at_planes(False, lambda: line((e_out,), 2), True)
-    second_dense(1)
+    start_dense(2, 0)
+    start_act(0)
+    second_dense(2, 1)
+    second_dense(0, 0)
     product_t(gq, w, 0, gn)
-    first_dense(2)
-    at_planes(True, lambda: line_dense(0), False)
-    at_planes(False, lambda: line((e_out,), 3), False)
+    first_dense(2, 0)
+    second_dense(3, 1)
+    core_act(0)
+    start_dense(3, 0)
+    at_planes(False, lambda: line((e_out,), 1), True)
+    at_planes(False, lambda: line((e_in,), 1), True)
+    at_planes(False, lambda: line((e_in,), 2), True)
+    second_dense(1, 0)
     x_act(1)
     for p in range(packs):
         h1[pl.ds(p * tok, tok), :] = x_ref[p].astype(F32)
     norm_back_rows(h1, gains[0:1], gn, grad_x, gain_row)
     wide_sum[0, 0:1, :] = gain_row[...]
+    at_planes(True, lambda: line_dense(0, 0), False)
     start_small(0)
-    core_act(0)
-    at_planes(False, lambda: line_dense(0), True)
     end_small(0)
     start_small(1)
-    second_dense(2)
+    first_dense(3, 0)
+    at_planes(False, lambda: line_dense(0, 0), True)
+    second_dense(1, 1)
+    at_planes(True, lambda: line_dense(0, 1), False)
+    at_planes(True, lambda: line_dense(2, 1), False)
+    second_dense(2, 0)
+    at_planes(False, lambda: line_dense(0, 1), True)
+    at_planes(False, lambda: line((e_out,), 2), True)
+    at_planes(True, lambda: line_dense(1, 0), False)
+    at_planes(False, lambda: line_dense(2, 1), True)
+    at_planes(False, lambda: line((e_in,), 3), False)
+    at_planes(False, lambda: line_dense(1, 0), True)
+    at_planes(True, lambda: line((e_in,), 3), True)
+    x_act(0)
     end_small(1)
     start_small(2)
-    first_dense(3)
+    at_planes(True, lambda: line_dense(2, 0), False)
+    at_planes(True, lambda: line_dense(3, 1), False)
+    at_planes(False, lambda: line_dense(2, 0), True)
+    second_dense(3, 0)
+    at_planes(True, lambda: line_dense(3, 0), False)
+    at_planes(True, lambda: line_dense(1, 1), False)
+    at_planes(True, lambda: line((e_out,), 3), False)
+    at_planes(False, lambda: line_dense(3, 1), True)
     finish_expert_in()
-    at_planes(True, lambda: line((e_out,), 3), True)
-    x_act(0)
-    at_planes(False, lambda: line_dense(1), False)
-    at_planes(False, lambda: line_dense(2), False)
-    at_planes(True, lambda: line_dense(1), True)
-    at_planes(True, lambda: line_dense(2), True)
+    at_planes(False, lambda: line((e_out,), 3), True)
     end_small(2)
     start_line()
-    second_dense(3)
-    at_planes(False, lambda: line_dense(3), False)
-    at_planes(True, lambda: line_dense(3), True)
+    at_planes(False, lambda: line_dense(1, 1), True)
+    at_planes(False, lambda: line_dense(3, 0), True)
     end_line()
     finish_dense()
     for wait in waits:
@@ -1132,18 +1155,37 @@
 
 
 def deliver_body(*refs):
-    count = len(refs) // 2
+    count = (len(refs) - 2) // 3
+    came, gone = refs[-2:]
+    copies = []
     for i in range(count):
-        refs[count + i][...] = refs[i][...]
+        place = refs[2 * count + i]
+        copies.append((
+            pltpu.make_async_copy(refs[i], place, came.at[i]),
+            pltpu.make_async_copy(place, refs[count + i], gone.at[i]),
+        ))
+    for first, _ in copies:
+        first.start()
+    for first, second in copies:
+        first.wait()
+        second.start()
+    for _, second in copies:
+        second.wait()
 
 
 def deliver(arrays):
-    vmem = pl.BlockSpec(memory_space=pltpu.VMEM)
+    any_ = pl.BlockSpec(memory_space=pl.ANY)
+    count = len(arrays)
     return pl.pallas_call(
         deliver_body,
         out_shape=[jax.ShapeDtypeStruct(a.shape, a.dtype) for a in arrays],
-        in_specs=[vmem] * len(arrays),
-        out_specs=[vmem] * len(arrays),
+        in_specs=[any_] * count,
+        out_specs=[any_] * count,
+        scratch_shapes=[
+            *[pltpu.VMEM(a.shape, a.dtype) for a in arrays],
+            pltpu.SemaphoreType.DMA((count,)),
+            pltpu.SemaphoreType.DMA((count,)),
+        ],
         name="deliver",
     )(*arrays)
 

time: 172 us -> 167 us (0.971)
  Pallas kernels: 170 us -> 166 us
    pallas_call x1, Pallas kernels: 167 us -> 163 us  [layer_kernel(): pl.pallas_call(layer_body, out_shape=[jax.ShapeDtypeStruct((packs, tok, w...]
where the time goes in v6:
time: 167 us; the launch traced here: 166 us
  Pallas kernels  166 us (99%)
    pallas_call x1, Pallas kernels, layer_kernel(): pl.pallas_call(layer_body, out_shape=[jax.ShapeDtypeStruct((packs, tok, w...  163 us

profile of v6, /device:TPU:12, one launch (start us, length us, event | category | flops | bytes accessed | tf_op | source)
XLA Modules:
  0.0 166.4 jit_solution(10372591968794080107)
XLA Ops:
  0.6 162.7 %layer.1 = (bf16[2,64,768]{2,1,0:T(8,128)(2,1)}, f32[144,768]{1,0:T(8,128)}, f32[48,768]{1,0:T(8,128)}, f32[48,3072]{1,0:T(8,128)}, f32[192,768]{1,0:T(8,128)}, ...) custom-call(s32[2,3]{1,0:T(2,128)} %bitcast.36, ...), custom_call_target="tpu_custom_call" | custom-call | tf_op jit(solution)/shard_map/layer/pallas_call | solution.py:1218
  163.4 2.8 %deliver.1 = (bf16[2,64,768]{2,1,0:T(8,128)(2,1)}, f32[144,768]{1,0:T(8,128)}, f32[48,768]{1,0:T(8,128)}, f32[48,3072]{1,0:T(8,128)}, f32[192,768]{1,0:T(8,128)}...) custom-call(bf16[2,64,768]{2,1,0:T(8,128)(2,1)} %get-tuple-element.30., ...), custom_call_target="tpu_custom_call" | custom-call | tf_op jit(solution)/shard_map/deliver/pallas_call | solution.py:1179

commit v7 on v6

--- a/solution.py
+++ b/solution.py
@@ -306,6 +306,13 @@
     return hot, (target == slots).astype(F32).astype(BF)
 
 
+def chances_of(rows, router_t, own):
+    logits = lax.dot_general(rows, router_t[...], (((1,), (1,)), ((), ())), preferred_element_type=F32)
+    raised = jnp.exp(logits - jnp.max(logits, axis=1, keepdims=True))
+    mine = (lax.broadcasted_iota(jnp.int32, (1, logits.shape[1]), 1) == own).astype(F32)
+    return mine, raised / jnp.sum(raised, axis=1, keepdims=True)
+
+
 def gelu_both(z):
     c = 0.7978845608028654
     t = jnp.tanh(c * (z + 0.044715 * (z * z * z)))
@@ -333,7 +340,7 @@
                xo, mo, n1_all, k_, v, kc, vc, gv, n1, q, mixed, n2, qc, cross_mixed, n3, gb, ga, gq,
                pr_self, pr_cross, h1, h2, gn, bias, same, causal, diagonal, gain_row,
                act_core, act_x, wide_sum, table_sum, wide_in, table_in,
-               slots_out, slots_in, slots_acc, ret_out, ret_in, back_in, hid, gin_,
+               slots_out, slots_in, slots_acc, ret_out, ret_in, back_in, grad_here, hid, gin_,
                act_send, act_recv, prep_send, prep_recv, line_send, side_send, spread_send, ici_recv, spread_recv, own_sem,
                core_send, core_recv, y_send, y_recv, x_send, x_recv, ex_send, ex_recv, z_send, z_recv, zd_send, zd_recv,
                sum_send, sum_recv, small_send, small_recv, slot_send, slot_recv, free_sem):
@@ -865,54 +872,61 @@
     dense_events(0)
     start_prep()
     at_planes(False, lambda: dense_events(1), False)
-    send_acts()
-    side_x(0)
-    side_y(0)
     at_planes(False, lambda: dense_events(2), False)
     at_planes(False, lambda: dense_events(3), False)
+    side_x(0)
     at_planes(True, lambda: dense_events(1), True)
+    expert_events(0, (e_out,))
+    side_y(0)
+    side_x(1)
+    at_planes(True, lambda: dense_events(2), True)
+    at_planes(True, lambda: dense_events(3), True)
     expert_events(0, (e_in,))
-    expert_events(0, (e_out,))
-    at_planes(False, lambda: expert_events(1, (e_in,)), False)
+    send_acts()
+    at_planes(False, lambda: expert_events(1, (e_out,)), False)
+    side_y(1)
     prepare_bias(rel, table, bias, at.s, tok, group)
     prepare_masks(lengths, same, causal, at.s, tok, group)
     hot, dispatch = route_slots(route, experts, each // packs)
     top = g_ref[...].astype(F32).reshape(packs * tok, width)
-    at_planes(True, lambda: dense_events(2), True)
-    act_events()
-    at_planes(True, lambda: dense_events(3), True)
-    at_planes(False, lambda: expert_events(2, (e_in,)), False)
-    side_y(1)
-    at_planes(False, lambda: expert_events(1, (e_out,)), False)
-    side_x(1)
+    side_x(2)
+    side_x(3)
+    at_planes(True, lambda: expert_events(1, (e_out,)), True)
     side_y(2)
-    first_norm()
+    at_planes(False, lambda: expert_events(1, (e_in,)), False)
+    side_y(3)
+    slots_out[1] = by_slot(dispatch, g_ref[...].reshape(packs * tok, width))
+    send_slots(1)
     at_planes(True, lambda: expert_events(1, (e_in,)), True)
     at_planes(False, lambda: expert_events(2, (e_out,)), False)
+    at_planes(False, lambda: expert_events(3, (e_out,)), False)
+    act_events()
     corner_events(0)
-    side_x(2)
-    side_y(3)
-    side_x(3)
-    at_planes(True, lambda: expert_events(1, (e_out,)), True)
+    at_planes(True, lambda: expert_events(2, (e_out,)), True)
     corner_events(1)
-    at_planes(True, lambda: expert_events(2, (e_in,)), True)
+    first_norm()
+    at_planes(False, lambda: expert_events(2, (e_in,)), False)
+    corner_events(2)
+    at_planes(False, lambda: expert_events(3, (e_in,)), False)
     for a in dense:
         for z in zs[: nz // 2]:
             for x in range(nx):
                 for y in range(ny):
                     arrive(spot(a, z, x, 1 - at.c, y), spread_recv.at[a, z, x, y])
-    at_planes(False, lambda: expert_events(3, (e_out,)), False)
-    corner_events(2)
+    corner_events(3)
     keys_and_values(at.z < nz // 2)
-    corner_events(3)
-    at_planes(False, lambda: expert_events(3, (e_in,)), False)
     for a in dense:
         for z in zs[nz // 2 :]:
             for x in range(nx):
                 for y in range(ny):
                     arrive(spot(a, z, x, 1 - at.c, y), spread_recv.at[a, z, x, y])
+    keys_and_values(at.z >= nz // 2)
+    for j, y in enumerate(at.other_y()):
+        here = slots_in.at[1, at.x, y]
+        arrive(here, slot_recv.at[y_sem(1, j)])
+        for i, x in enumerate(at.other_x()):
+            slot_copy(False, here, here, x_sem(1, i, y), x_sem(1, nx - 2 - i, y), x=x)
     project(n1, w, 0, q)
-    keys_and_values(at.z >= nz // 2)
     attend_pairs(q, k_, v, bias, causal, pr_self, mixed)
     add_product(h1, mixed, w, 6)
     rms_rows(h1, gains[1:2], n2, packs * tok)
@@ -923,20 +937,13 @@
     rms_rows(h2, gains[2:3], n3, packs * tok)
     slots_out[0] = by_slot(dispatch, n3[...])
     send_slots(0)
-    logits = lax.dot_general(n3[...], router_t[...], (((1,), (1,)), ((), ())), preferred_element_type=F32)
-    raised = jnp.exp(logits - jnp.max(logits, axis=1, keepdims=True))
-    routing = raised / jnp.sum(raised, axis=1, keepdims=True)
-    gate = jnp.sum(routing * hot, axis=1, keepdims=True)
-    slots_out[1] = by_slot(dispatch, (gate * top).astype(BF))
-    send_slots(1)
-    for t in range(2):
-        for j, y in enumerate(at.other_y()):
-            here = slots_in.at[t, at.x, y]
-            arrive(here, slot_recv.at[y_sem(t, j)])
-            for i, x in enumerate(at.other_x()):
-                slot_copy(False, here, here, x_sem(t, i, y), x_sem(t, nx - 2 - i, y), x=x)
-    at_planes(True, lambda: expert_events(2, (e_out,)), True)
     at_planes(True, lambda: expert_events(3, (e_out,)), True)
+    for j, y in enumerate(at.other_y()):
+        here = slots_in.at[0, at.x, y]
+        arrive(here, slot_recv.at[y_sem(0, j)])
+        for i, x in enumerate(at.other_x()):
+            slot_copy(False, here, here, x_sem(0, i, y), x_sem(0, nx - 2 - i, y), x=x)
+    at_planes(True, lambda: expert_events(2, (e_in,)), True)
     at_planes(True, lambda: expert_events(3, (e_in,)), True)
     for a in experts_:
         for z in range(nz):
@@ -945,18 +952,18 @@
         for i, x in enumerate(at.other_x()):
             for y in range(ny):
                 arrive(slots_in.at[t, x, y], slot_recv.at[x_sem(t, i, y)])
-    for wait in waits:
-        wait()
-    waits.clear()
     here = slots_in[0].reshape(nx * count, width)
-    grad_here = slots_in[1].reshape(nx * count, width)
+    g_here = slots_in[1].reshape(nx * count, width).astype(F32)
+    mine, chances = chances_of(here, router_t, at.y)
+    gate_here = jnp.sum(chances * mine, axis=1, keepdims=True)
+    grad_here[...] = (gate_here * g_here).astype(BF)
     for u in range(panels):
         in_panel = jnp.concatenate([big[place + u] for place in places], axis=0)
         out_panel = big[pl.ds(bases[e_out] + u * row_units, row_units)].reshape(width, width)
         inner = jnp.dot(here, in_panel, preferred_element_type=F32)
         hidden, slope = gelu_both(inner)
         hid[u] = hidden.astype(BF)
-        grad_hidden = lax.dot_general(grad_here, out_panel, (((1,), (1,)), ((), ())), preferred_element_type=F32)
+        grad_hidden = lax.dot_general(grad_here[...], out_panel, (((1,), (1,)), ((), ())), preferred_element_type=F32)
         gin_[u] = (grad_hidden * slope).astype(BF)
         result = jnp.dot(hid[u], out_panel, preferred_element_type=F32).reshape(nx, ny, each, width)
         grad_slots = lax.dot_general(gin_[u], in_panel, (((1,), (1,)), ((), ())), preferred_element_type=F32)
@@ -967,63 +974,62 @@
         else:
             slots_acc[0] = result
             slots_acc[1] = grad_slots
+    grad_gate = jnp.sum(g_here * slots_acc[0].reshape(nx * count, width), axis=1, keepdims=True)
+    grad_logits = grad_gate * chances * (mine - gate_here)
+    extra_grad = 0.0
+    for e in range(experts):
+        extra_grad = extra_grad + grad_logits[:, e : e + 1] * router_t[e : e + 1, :].astype(F32)
+    slots_acc[1] += extra_grad.reshape(nx, ny, each, width)
+    for wait in waits:
+        wait()
+    waits.clear()
     for y in [*at.other_y(), at.y]:
-        for t in range(2):
-            for j, x in enumerate(at.other_x()):
-                ret_out[t, j, y] = slots_acc[t, x, y].astype(BF)
-                slot_copy(True, ret_out.at[t, j, y], ret_in.at[t, nx - 2 - j, y], ret_sem(t, j, y),
-                          ret_sem(t, nx - 2 - j, y), x=x)
+        for j, x in enumerate(at.other_x()):
+            ret_out[1, j, y] = slots_acc[1, x, y].astype(BF)
+            slot_copy(True, ret_out.at[1, j, y], ret_in.at[1, nx - 2 - j, y], ret_sem(1, j, y), ret_sem(1, nx - 2 - j, y), x=x)
     for u in range(panels):
         grad = lax.dot_general(here, gin_[u], (((0,), (0,)), ((), ())), preferred_element_type=F32).astype(BF)
         for i, place in enumerate(places):
             ge[place + u] = grad[i * unit : (i + 1) * unit]
     for k in range(nz):
         start_expert(e_in, k)
+    router_grad = lax.dot_general(
+        grad_logits, here.astype(F32), (((0,), (0,)), ((), ())), precision=HIGHEST, preferred_element_type=F32
+    )
     for u in range(panels):
-        grad = lax.dot_general(hid[u], grad_here, (((0,), (0,)), ((), ())), preferred_element_type=F32).astype(BF)
+        grad = lax.dot_general(hid[u], grad_here[...], (((0,), (0,)), ((), ())), preferred_element_type=F32).astype(BF)
         ge[pl.ds(bases[e_out] + u * row_units, row_units)] = grad.reshape(row_units, unit, width)
     for k in range(nz):
         start_expert(e_out, k)
+    for y in [*at.other_y(), at.y]:
+        for j, x in enumerate(at.other_x()):
+            ret_out[0, j, y] = slots_acc[0, x, y].astype(BF)
+            slot_copy(True, ret_out.at[0, j, y], ret_in.at[0, nx - 2 - j, y], ret_sem(0, j, y), ret_sem(0, nx - 2 - j, y), x=x)
     core_expert(e_in, 0)
+    at_planes(True, lambda: line((e_in,), 0), False)
     for wait in slot_waits:
         wait()
     for j, y in enumerate(at.other_y()):
-        for t in range(2):
-            slots_out[t, y] = summed(t, y)
-            slot_copy(True, slots_out.at[t, y], back_in.at[t, at.y], y_sem(2 + t, j), y_sem(2 + t, ny - 2 - j), y=y)
+        slots_out[1, y] = summed(1, y)
+        slot_copy(True, slots_out.at[1, y], back_in.at[1, at.y], y_sem(3, j), y_sem(3, ny - 2 - j), y=y)
     core_expert(e_out, 0)
+    core_expert(e_in, 1)
+    core_expert(e_out, 1)
+    back_in[1, at.y] = summed(1, at.y)
+    core_expert(e_in, 3)
+    core_expert(e_out, 2)
+    core_expert(e_out, 3)
     at_planes(True, lambda: line((e_out,), 0), False)
-    core_expert(e_in, 3)
-    core_expert(e_out, 1)
-    core_expert(e_out, 2)
-    at_planes(True, lambda: line((e_in,), 0), False)
-    at_planes(True, lambda: line((e_out,), 1), False)
-    core_expert(e_out, 3)
     core_expert(e_in, 2)
-    core_expert(e_in, 1)
     free_experts()
-    for t in range(2):
-        back_in[t, at.y] = summed(t, at.y)
-    for t in range(2):
-        for j, y in enumerate(at.other_y()):
-            arrive(back_in.at[t, y], slot_recv.at[y_sem(2 + t, j)])
-    combined = jnp.dot(dispatch, back_in[0].reshape(count, width), preferred_element_type=F32)
-    rows_out = (h2[...] + gate * combined).astype(BF)
-    for p in range(packs):
-        out_rows[p] = rows_out[p * tok : (p + 1) * tok]
-    grad_gate = jnp.sum(top * combined, axis=1, keepdims=True)
-    grad_logits = grad_gate * routing * (hot - gate)
+    for j, y in enumerate(at.other_y()):
+        arrive(back_in.at[1, y], slot_recv.at[y_sem(3, j)])
     diagonal[...] = jnp.zeros_like(diagonal)
     for i, (_, inbox) in enumerate(pair_sums):
         inbox[pl.ds(tail + at.z, 1)] = jnp.zeros_like(inbox[pl.ds(0, 1)])
     wide_sum[0] = jnp.zeros_like(wide_sum[0])
-    wide_sum[0, pl.ds(3, experts), :] = lax.dot_general(
-        grad_logits, n3[...].astype(F32), (((0,), (0,)), ((), ())), precision=HIGHEST, preferred_element_type=F32
-    )
-    grad_n3 = jnp.dot(dispatch, back_in[1].reshape(count, width), preferred_element_type=F32)
-    for e in range(experts):
-        grad_n3 = grad_n3 + grad_logits[:, e : e + 1] * router_t[e : e + 1, :].astype(F32)
-    gn[...] = grad_n3
+    wide_sum[0, pl.ds(3, experts), :] = router_grad
+    gn[...] = jnp.dot(dispatch, back_in[1].reshape(count, width), preferred_element_type=F32)
     grad_x[...] = top
     norm_back_rows(h2, gains[2:3], gn, grad_x, gain_row)
     wide_sum[0, 2:3, :] = gain_row[...]
@@ -1034,94 +1040,107 @@
     outer_product(mo, gk, big, 4)
     outer_product(mo, gv, big, 5)
     pl.semaphore_wait(free_sem, 1)
-    start_dense(0, 0)
-    outer_product(cross_mixed, gb, big, 7)
-    start_dense(0, 1)
-    two_products_t(gk, 4, gv, 5, w, kc)
-    first_dense(0, 0)
-    start_dense(1, 1)
-    first_dense(0, 1)
-    at_planes(True, lambda: line((e_out,), 2), False)
-    at_planes(False, lambda: line((e_in,), 0), True)
+    start_dense(1, 0)
+    for j, y in enumerate(at.other_y()):
+        slots_out[0, y] = summed(0, y)
+        slot_copy(True, slots_out.at[0, y], back_in.at[0, at.y], y_sem(2, j), y_sem(2, ny - 2 - j), y=y)
+    at_planes(True, lambda: line((e_in,), 1), False)
     product_t(gq, w, 3, gn)
     norm_back_rows(h1, gains[1:2], gn, grad_x, gain_row)
     wide_sum[0, 1:2, :] = gain_row[...]
-    at_planes(True, lambda: line((e_in,), 1), False)
+    back_in[0, at.y] = summed(0, at.y)
+    outer_product(cross_mixed, gb, big, 7)
+    start_dense(0, 1)
+    first_dense(1, 0)
+    start_dense(1, 1)
     gb[...] = grad_x[...].astype(BF)
     product_t(gb, w, 6, ga)
+    outer_product(mixed, gb, big, 6)
+    at_planes(True, lambda: line((e_out,), 1), False)
+    first_dense(0, 1)
+    start_dense(3, 1)
+    at_planes(False, lambda: line((e_in,), 0), True)
+    start_dense(0, 0)
+    at_planes(False, lambda: line((e_out,), 0), True)
+    start_dense(2, 1)
+    two_products_t(gk, 4, gv, 5, w, kc)
     first_dense(1, 1)
-    outer_product(mixed, gb, big, 6)
-    start_dense(3, 1)
-    start_dense(2, 1)
-    start_dense(1, 0)
+    at_planes(True, lambda: line((e_out,), 2), False)
+    first_dense(3, 1)
     attend_pairs_back(q, k_, v, pr_self, ga, gq, gk, gv, diagonal)
+    second_dense(0, 1)
     first_dense(2, 1)
-    first_dense(1, 0)
+    first_dense(0, 0)
+    start_act(0)
+    at_planes(False, lambda: line((e_in,), 1), True)
+    two_products_t(gk, 1, gv, 2, w, k_)
     at_planes(True, lambda: line((e_in,), 2), False)
-    second_dense(0, 1)
-    at_planes(False, lambda: line((e_out,), 0), True)
-    first_dense(3, 1)
-    two_products_t(gk, 1, gv, 2, w, k_)
     start_act(1)
     outer_product(n1, gq, big, 0)
     outer_product(n1_all, gk, big, 1)
     outer_product(n1_all, gv, big, 2)
+    start_dense(2, 0)
+    core_act(1)
     table_sum[0] = table_grad(rel, diagonal, at.s, tok, group)
-    core_act(1)
-    start_dense(2, 0)
-    start_act(0)
+    start_dense(3, 0)
+    product_t(gq, w, 0, gn)
+    for j, y in enumerate(at.other_y()):
+        arrive(back_in.at[0, y], slot_recv.at[y_sem(2, j)])
+    _, routing = chances_of(n3[...], router_t, at.y)
+    gate = jnp.sum(routing * hot, axis=1, keepdims=True)
+    combined = jnp.dot(dispatch, back_in[0].reshape(count, width), preferred_element_type=F32)
+    rows_out = (h2[...] + gate * combined).astype(BF)
+    for p in range(packs):
+        out_rows[p] = rows_out[p * tok : (p + 1) * tok]
+    at_planes(False, lambda: line((e_out,), 1), True)
+    second_dense(3, 1)
+    first_dense(2, 0)
     second_dense(2, 1)
     second_dense(0, 0)
-    product_t(gq, w, 0, gn)
-    first_dense(2, 0)
-    second_dense(3, 1)
-    core_act(0)
-    start_dense(3, 0)
-    at_planes(False, lambda: line((e_out,), 1), True)
-    at_planes(False, lambda: line((e_in,), 1), True)
     at_planes(False, lambda: line((e_in,), 2), True)
-    second_dense(1, 0)
     x_act(1)
     for p in range(packs):
         h1[pl.ds(p * tok, tok), :] = x_ref[p].astype(F32)
     norm_back_rows(h1, gains[0:1], gn, grad_x, gain_row)
     wide_sum[0, 0:1, :] = gain_row[...]
+    at_planes(True, lambda: line_dense(0, 1), False)
+    core_act(0)
+    second_dense(1, 0)
     at_planes(True, lambda: line_dense(0, 0), False)
     start_small(0)
     end_small(0)
     start_small(1)
     first_dense(3, 0)
+    at_planes(False, lambda: line_dense(3, 1), False)
+    at_planes(True, lambda: line_dense(3, 1), True)
     at_planes(False, lambda: line_dense(0, 0), True)
-    second_dense(1, 1)
-    at_planes(True, lambda: line_dense(0, 1), False)
-    at_planes(True, lambda: line_dense(2, 1), False)
     second_dense(2, 0)
     at_planes(False, lambda: line_dense(0, 1), True)
-    at_planes(False, lambda: line((e_out,), 2), True)
     at_planes(True, lambda: line_dense(1, 0), False)
-    at_planes(False, lambda: line_dense(2, 1), True)
-    at_planes(False, lambda: line((e_in,), 3), False)
-    at_planes(False, lambda: line_dense(1, 0), True)
-    at_planes(True, lambda: line((e_in,), 3), True)
+    at_planes(True, lambda: line((e_in,), 3), False)
     x_act(0)
     end_small(1)
     start_small(2)
+    second_dense(1, 1)
+    at_planes(False, lambda: line((e_in,), 3), True)
     at_planes(True, lambda: line_dense(2, 0), False)
-    at_planes(True, lambda: line_dense(3, 1), False)
+    at_planes(False, lambda: line((e_out,), 2), True)
+    at_planes(False, lambda: line_dense(1, 0), True)
+    at_planes(True, lambda: line_dense(2, 1), False)
     at_planes(False, lambda: line_dense(2, 0), True)
     second_dense(3, 0)
+    at_planes(False, lambda: line_dense(2, 1), True)
     at_planes(True, lambda: line_dense(3, 0), False)
     at_planes(True, lambda: line_dense(1, 1), False)
-    at_planes(True, lambda: line((e_out,), 3), False)
-    at_planes(False, lambda: line_dense(3, 1), True)
-    finish_expert_in()
-    at_planes(False, lambda: line((e_out,), 3), True)
     end_small(2)
     start_line()
     at_planes(False, lambda: line_dense(1, 1), True)
+    at_planes(False, lambda: line((e_out,), 3), False)
     at_planes(False, lambda: line_dense(3, 0), True)
+    finish_expert_in()
     end_line()
     finish_dense()
+    at_planes(True, lambda: line((e_out,), 3), True)
     for wait in waits:
         wait()
 
@@ -1264,6 +1283,7 @@
             low(2, nx - 1, ny, each, width),
             low(2, nx - 1, ny, each, width),
             low(2, ny, each, width),
+            low(nx * ny * each, width),
             low(panels, nx * ny * each, width),
             low(panels, nx * ny * each, width),
             dma((2, packs, 2 * nx)),

time: 167 us -> 161 us (0.964)
  Pallas kernels: 166 us -> 160 us
    pallas_call x1, Pallas kernels: 163 us -> 157 us  [layer_kernel(): pl.pallas_call(layer_body, out_shape=[jax.ShapeDtypeStruct((packs, tok, w...]
where the time goes in v7:
time: 161 us
  Pallas kernels  160 us (99%)
    pallas_call x1, Pallas kernels, layer_kernel(): pl.pallas_call(layer_body, out_shape=[jax.ShapeDtypeStruct((packs, tok, w...  157 us

profile of v7, /device:TPU:12, one launch (start us, length us, event | category | flops | bytes accessed | tf_op | source)
XLA Modules:
  0.0 160.7 jit_solution(5708484135079398321)
XLA Ops:
  0.6 157.1 %layer.1 = (bf16[2,64,768]{2,1,0:T(8,128)(2,1)}, f32[144,768]{1,0:T(8,128)}, f32[48,768]{1,0:T(8,128)}, f32[48,3072]{1,0:T(8,128)}, f32[192,768]{1,0:T(8,128)}, ...) custom-call(s32[2,3]{1,0:T(2,128)} %bitcast.36, ...), custom_call_target="tpu_custom_call" | custom-call | tf_op jit(solution)/shard_map/layer/pallas_call | solution.py:1237
  157.8 2.8 %deliver.1 = (bf16[2,64,768]{2,1,0:T(8,128)(2,1)}, f32[144,768]{1,0:T(8,128)}, f32[48,768]{1,0:T(8,128)}, f32[48,3072]{1,0:T(8,128)}, f32[192,768]{1,0:T(8,128)}...) custom-call(bf16[2,64,768]{2,1,0:T(8,128)(2,1)} %get-tuple-element.30., ...), custom_call_target="tpu_custom_call" | custom-call | tf_op jit(solution)/shard_map/deliver/pallas_call | solution.py:1198

commit v8 on v7

--- a/solution.py
+++ b/solution.py
@@ -334,7 +334,7 @@
     waits.append(wait)
 
 
-def layer_body(lengths, rel, gains, table, router_t, route, x_ref, m_ref, g_ref, ain, aout, ein, eout,
+def layer_body(lengths, rel, gains, table, router_t, route, x_ref, m_ref, g_hbm, ain, aout, ein_hbm, eout,
                out_rows, o0, o1, o2, o3, grad_x, grad_mem, sum_gains, sum_router, sum_table,
                w, big, ge, prep, c2, c3, y0, y1, x0, x1, ex_in, z0, z1, z2, z3,
                xo, mo, n1_all, k_, v, kc, vc, gv, n1, q, mixed, n2, qc, cross_mixed, n3, gb, ga, gq,
@@ -343,7 +343,7 @@
                slots_out, slots_in, slots_acc, ret_out, ret_in, back_in, grad_here, hid, gin_,
                act_send, act_recv, prep_send, prep_recv, line_send, side_send, spread_send, ici_recv, spread_recv, own_sem,
                core_send, core_recv, y_send, y_recv, x_send, x_recv, ex_send, ex_recv, z_send, z_recv, zd_send, zd_recv,
-               sum_send, sum_recv, small_send, small_recv, slot_send, slot_recv, free_sem):
+               sum_send, sum_recv, small_send, small_recv, slot_send, slot_recv, free_sem, g_ref, ein, x_keep, load_sem):
     at = Place()
     nz, nx, ny = at.nz, at.nx, at.ny
     packs, tok, width = x_ref.shape
@@ -415,6 +415,10 @@
     shards = (ain, aout)
     acts = ((x_ref, xo), (m_ref, mo))
 
+    load_g = pltpu.make_async_copy(g_hbm, g_ref, load_sem.at[0])
+    load_e = pltpu.make_async_copy(ein_hbm, ein, load_sem.at[1])
+    load_g.start()
+    load_e.start()
     at.greet()
 
     def act_rows(full, p, x, c):
@@ -525,6 +529,7 @@
         return pl.ds(bases[e_in] + ((z * 2 + c) * nx + x) * panels, n * panels)
 
     def start_prep():
+        load_e.wait()
         for x in range(nx):
             for u in range(panels):
                 each_z = width // columns
@@ -563,8 +568,9 @@
             wait()
         rms_rows(xo, gains[0:1], n1_all, packs * group)
         for p in range(packs):
-            h1[pl.ds(p * tok, tok), :] = x_ref[p].astype(F32)
+            x_keep[pl.ds(p * tok, tok), :] = xo[pl.ds(pl.multiple_of(p * group + at.s * tok, tok), tok), :]
             n1[pl.ds(p * tok, tok), :] = n1_all[pl.ds(pl.multiple_of(p * group + at.s * tok, tok), tok), :]
+        h1[...] = x_keep[...].astype(F32)
 
     places = [((z * 2 + c) * nx + x) * panels for z in range(nz) for x in range(nx) for c in range(2)]
     each = slots_out.shape[2]
@@ -888,6 +894,7 @@
     prepare_bias(rel, table, bias, at.s, tok, group)
     prepare_masks(lengths, same, causal, at.s, tok, group)
     hot, dispatch = route_slots(route, experts, each // packs)
+    load_g.wait()
     top = g_ref[...].astype(F32).reshape(packs * tok, width)
     side_x(2)
     side_x(3)
@@ -1099,8 +1106,7 @@
     second_dense(0, 0)
     at_planes(False, lambda: line((e_in,), 2), True)
     x_act(1)
-    for p in range(packs):
-        h1[pl.ds(p * tok, tok), :] = x_ref[p].astype(F32)
+    h1[...] = x_keep[...].astype(F32)
     norm_back_rows(h1, gains[0:1], gn, grad_x, gain_row)
     wide_sum[0, 0:1, :] = gain_row[...]
     at_planes(True, lambda: line_dense(0, 1), False)
@@ -1248,7 +1254,7 @@
             shape(experts, width),
             shape(2 * pairs, buckets),
         ],
-        in_specs=[smem, *[vmem] * 8, any_, any_, vmem, any_],
+        in_specs=[smem, *[vmem] * 5, *[any_] * 7],
         out_specs=[vmem] * 10,
         scratch_shapes=[
             low(total, unit, width),
@@ -1315,6 +1321,10 @@
             dma((4 * (ny - 1) + 4 * (nx - 1) * ny,)),
             dma((4 * (ny - 1) + 4 * (nx - 1) * ny,)),
             pltpu.SemaphoreType.REGULAR,
+            low(packs, tok, width),
+            low(unit, hidden),
+            low(mine, width),
+            dma((2,)),
         ],
         compiler_params=pltpu.CompilerParams(
             collective_id=0, has_side_effects=True, vmem_limit_bytes=64 * 2**20

time: 161 us -> 161 us (level)
  no operation moved by 1% of the time
where the time goes in v8:
time: 161 us; the launch traced here: 160 us
  Pallas kernels  159 us (99%)
    pallas_call x1, Pallas kernels, layer_kernel(): pl.pallas_call(layer_body, out_shape=[jax.ShapeDtypeStruct((packs, tok, w...  157 us

profile of v8, /device:TPU:12, one launch (start us, length us, event | category | flops | bytes accessed | tf_op | source)
XLA Modules:
  0.0 160.3 jit_solution(3797322350296970412)
XLA Ops:
  0.6 156.6 %layer.1 = (bf16[2,64,768]{2,1,0:T(8,128)(2,1)}, f32[144,768]{1,0:T(8,128)}, f32[48,768]{1,0:T(8,128)}, f32[48,3072]{1,0:T(8,128)}, f32[192,768]{1,0:T(8,128)}, ...) custom-call(s32[2,3]{1,0:T(2,128)} %bitcast.36, ...), custom_call_target="tpu_custom_call" | custom-call | tf_op jit(solution)/shard_map/layer/pallas_call | solution.py:1243
  157.3 2.8 %deliver.1 = (bf16[2,64,768]{2,1,0:T(8,128)(2,1)}, f32[144,768]{1,0:T(8,128)}, f32[48,768]{1,0:T(8,128)}, f32[48,3072]{1,0:T(8,128)}, f32[192,768]{1,0:T(8,128)}...) custom-call(bf16[2,64,768]{2,1,0:T(8,128)(2,1)} %get-tuple-element.30., ...), custom_call_target="tpu_custom_call" | custom-call | tf_op jit(solution)/shard_map/deliver/pallas_call | solution.py:1204

commit v9 on v8

--- a/solution.py
+++ b/solution.py
@@ -226,7 +226,7 @@
         total[at] = (total[at].astype(F32) + other[at].astype(F32)).astype(total.dtype)
         return carry
 
-    lax.fori_loop(0, count * (rows // step), body, 0)
+    lax.fori_loop(0, count * (rows // step), body, 0, unroll=min(count * (rows // step), 4))
 
 
 def norm_back_rows(value, gain, grad, total, gain_grad, step=64):
@@ -678,12 +678,13 @@
                         send(dense_core(0, k, x, y, u), ys[0].at[k, ny - 2 - j, x, pl.ds(u, 1)],
                              y_send.at[k, j, x, u], y_recv.at[k, ny - 2 - j, x, u], y=y)
             return
-        for x, _ in xs_in_order():
+        for x, away in xs_in_order():
             arrive(dense_core(1, k, x), core_recv.at[1, k, x])
             add_into(dense_core(1, k, x), dense_part(1, order_d[k], x, at.c))
-        for j, x in enumerate(at.other_x()):
-            send(dense_core(1, k, x), xs[1].at[k, nx - 2 - j], x_send.at[k, j, units[0]],
-                 x_recv.at[k, nx - 2 - j, units[0]], x=x)
+            if away:
+                j = lax.rem(x - at.x + nx, nx) - 1
+                send(dense_core(1, k, x), xs[1].at[k, nx - 2 - j], x_send.at[k, j, units[0]],
+                     x_recv.at[k, nx - 2 - j, units[0]], x=x)
 
     def second_dense(k, a):
         if a == 0:

time: 161 us -> 161 us (level)
  no operation moved by 1% of the time
where the time goes in v9:
time: 161 us; the launch traced here: 160 us
  Pallas kernels  159 us (99%)
    pallas_call x1, Pallas kernels, layer_kernel(): pl.pallas_call(layer_body, out_shape=[jax.ShapeDtypeStruct((packs, tok, w...  156 us

profile of v9, /device:TPU:12, one launch (start us, length us, event | category | flops | bytes accessed | tf_op | source)
XLA Modules:
  0.0 159.6 jit_solution(16216676398953149650)
XLA Ops:
  0.6 155.9 %layer.1 = (bf16[2,64,768]{2,1,0:T(8,128)(2,1)}, f32[144,768]{1,0:T(8,128)}, f32[48,768]{1,0:T(8,128)}, f32[48,3072]{1,0:T(8,128)}, f32[192,768]{1,0:T(8,128)}, ...) custom-call(s32[2,3]{1,0:T(2,128)} %bitcast.36, ...), custom_call_target="tpu_custom_call" | custom-call | tf_op jit(solution)/shard_map/layer/pallas_call | solution.py:1244
  156.6 2.8 %deliver.1 = (bf16[2,64,768]{2,1,0:T(8,128)(2,1)}, f32[144,768]{1,0:T(8,128)}, f32[48,768]{1,0:T(8,128)}, f32[48,3072]{1,0:T(8,128)}, f32[192,768]{1,0:T(8,128)}...) custom-call(bf16[2,64,768]{2,1,0:T(8,128)(2,1)} %get-tuple-element.30., ...), custom_call_target="tpu_custom_call" | custom-call | tf_op jit(solution)/shard_map/deliver/pallas_call | solution.py:1205
